TPU v7x, 256 devices: a whole 4x4x8 slice. The times are simulated.
256 devices in a mesh: ctx: 64 (over y, z, core), chan: 4 (over x).
Axes of the slice: x: 4, y: 4, z: 8, core: 2. Of those that a mesh axis runs over, the one named last changes fastest.
Arguments:
- query_feat: bfloat16 [8192, 2048], P('ctx', 'chan'), may hold values from -6 to 6
- key_feat: bfloat16 [8192, 2048], P('ctx', 'chan'), may hold values from -6 to 6
- value_feat: bfloat16 [8192, 2048], P('ctx', 'chan'), may hold values from -6 to 6
- decay_rate: float32 [2048, 16], P('chan'), may hold values from 3.6621095e-05 to 0.03
- residue: float32 [2048, 16], P('chan'), may hold values from -0.12 to 0.12
- conv_skip: float32 [2048], P('chan'), may hold values from 0.1 to 1.9
- out_weight: bfloat16 [2048, 4096], P('chan'), may hold values from -0.125 to 0.125
- stream: bfloat16 [8192, 4096], P('ctx', 'chan'), may hold values from -6 to 6
- attn_query: bfloat16 [8192, 4096], P('ctx', 'chan'), may hold values from -8 to 8
- attn_key: bfloat16 [8192, 4096], P('ctx', 'chan'), may hold values from -8 to 8
- attn_value: bfloat16 [8192, 4096], P('ctx', 'chan'), may hold values from -6 to 6
- doc_start: int32 [8192], P('ctx'), may hold values from 0 to 8191, as said below
- read_mask: int32 [64, 4], P('ctx'), may hold values from 0 to 1, as said below
Outputs:
- mixed: bfloat16 [8192, 4096], P('ctx', 'chan')
- attended: bfloat16 [8192, 4096], P('ctx', 'chan')
Inputs may be any that keep to these rules, and one draw needn't show every extreme that they name: doc_start[t] is the first position of the document that holds position t: never above t, never falling, the same for all positions of one document; documents are contiguous and hold 1 to 384 positions, and some document holds exactly 384. read_mask[b, k] is 1 exactly when b - k >= doc_start[b * 128] // 128; read_mask[b, 0] is always 1, and some row is all ones.
All inputs are finite; a program needn't handle non-finite values.
Results may differ from a plain program's by a relative error of at most 0.022.
Values may be sent and summed in bfloat16 or wider, within the bound.
No kernel may reach another device: no remote copies, remote signals or barrier semaphores. Data moves between devices by JAX's collectives and lax.ppermute only.
A program may use at most 64 MiB of HBM per device.

v0:
```python
import math

import jax
import jax.numpy as jnp
from jax import lax
from jax.sharding import PartitionSpec as P

HD = 128
DOC_BLOCKS = 3


def partner_2(shard, axis, bit):
    return lax.ppermute(shard, axis, [(i, i ^ 1 << bit) for i in range(lax.axis_size(axis))])


def passed_along(value, axis, steps):
    count = lax.axis_size(axis)
    initial, last = (max(0, -steps), min(count, count - steps))
    return lax.ppermute(value, axis, [(source, source + steps) for source in range(initial, last)])


def complex_mul(grid_value, cos_part, sin_part):
    real_part = grid_value[0] * cos_part - grid_value[1] * sin_part
    imag_part = grid_value[0] * sin_part + grid_value[1] * cos_part
    return jnp.stack([real_part, imag_part])


def table_product(table, operand):
    return jnp.einsum("dm,bmc->bdc", table, operand, precision=lax.Precision.HIGHEST)


def local_dft(grid_value, cos_table, sin_table, sign_value):
    real_part = table_product(cos_table, grid_value[0]) - sign_value * table_product(
        sin_table, grid_value[1]
    )
    imag_part = table_product(cos_table, grid_value[1]) + sign_value * table_product(
        sin_table, grid_value[0]
    )
    return jnp.stack([real_part, imag_part])


def pairs_forward(signal_grid, ctx_index, ctx_count):
    levels = ctx_count.bit_length() - 1
    for bit_level in reversed(range(levels)):
        partner = partner_2(signal_grid.astype(jnp.bfloat16), "ctx", bit_level).astype(
            signal_grid.dtype
        )
        upper_half = jnp.right_shift(ctx_index, bit_level) % 2 == 1
        offset = (ctx_index % (1 << bit_level)).astype(jnp.float32)
        twist_angle = -math.pi * offset / (1 << bit_level)
        rotated = complex_mul(partner - signal_grid, jnp.cos(twist_angle), jnp.sin(twist_angle))
        signal_grid = jnp.where(upper_half, rotated, signal_grid + partner)
    reversed_index = jnp.zeros((), jnp.int32)
    for bit_level in range(levels):
        reversed_index = reversed_index + jnp.right_shift(ctx_index, bit_level) % 2 * (
            1 << levels - 1 - bit_level
        )
    return (signal_grid, reversed_index)


def pairs_inverse(spectrum_grid, ctx_index, ctx_count):
    levels = ctx_count.bit_length() - 1
    for bit_level in range(levels):
        partner = partner_2(spectrum_grid.astype(jnp.bfloat16), "ctx", bit_level).astype(
            spectrum_grid.dtype
        )
        upper_half = jnp.right_shift(ctx_index, bit_level) % 2 == 1
        offset = (ctx_index % (1 << bit_level)).astype(jnp.float32)
        twist_angle = math.pi * offset / (1 << bit_level)
        twist_cos = jnp.cos(twist_angle)
        twist_sin = jnp.sin(twist_angle)
        lower_value = 0.5 * (spectrum_grid + complex_mul(partner, twist_cos, twist_sin))
        upper_value = 0.5 * (partner - complex_mul(spectrum_grid, twist_cos, twist_sin))
        spectrum_grid = jnp.where(upper_half, upper_value, lower_value)
    return spectrum_grid


def filter_spectrum(decay_rate, residue, freq_class, ctx_count, tok_rows, seq_len):
    digit_ids = jnp.arange(tok_rows, dtype=jnp.int32)
    branch_ids = jnp.arange(2, dtype=jnp.int32)
    freq_ids = 2 * (freq_class + ctx_count * digit_ids)[None, :] + branch_ids[:, None]
    half_angle = (math.pi * freq_ids.astype(jnp.float32) / (2 * seq_len))[:, :, None]
    full_angle = 2.0 * half_angle
    parity_sign = (1 - 2 * (freq_ids % 2)).astype(jnp.float32)[:, :, None]
    sin_half = jnp.sin(half_angle)
    cos_full = jnp.cos(full_angle)
    sin_full = jnp.sin(full_angle)
    spec_real = jnp.zeros((2, tok_rows, decay_rate.shape[0]), jnp.float32)
    spec_imag = jnp.zeros((2, tok_rows, decay_rate.shape[0]), jnp.float32)
    for order_index in range(decay_rate.shape[1]):
        rate_now = decay_rate[:, order_index][None, None, :]
        weight_now = residue[:, order_index][None, None, :]
        real_den = 2.0 * sin_half * sin_half - jnp.expm1(-rate_now) * cos_full
        imag_den = jnp.exp(-rate_now) * sin_full
        numerator = weight_now * (1.0 - parity_sign * jnp.exp(-rate_now * seq_len))
        scaled = numerator / (real_den * real_den + imag_den * imag_den)
        spec_real = spec_real + scaled * real_den
        spec_imag = spec_imag - scaled * imag_den
    return (spec_real, spec_imag)


def class_filter(
    grid_value,
    freq_class,
    decay_rate,
    residue,
    cos_table,
    sin_table,
    block_count,
    tok_rows,
    seq_len,
):
    digit_ids = jnp.arange(tok_rows, dtype=jnp.int32)
    twist_angle = 2.0 * math.pi * (digit_ids * freq_class % seq_len).astype(jnp.float32) / seq_len
    twist_cos = jnp.cos(twist_angle)[:, None]
    twist_sin = jnp.sin(twist_angle)[:, None]
    grid_value = complex_mul(grid_value, twist_cos, -twist_sin)
    spectrum = local_dft(grid_value, cos_table, sin_table, -1.0)
    spec_real, spec_imag = filter_spectrum(
        decay_rate, residue, freq_class, block_count, tok_rows, seq_len
    )
    spectrum = complex_mul(spectrum, spec_real, spec_imag)
    restored = local_dft(spectrum, cos_table, sin_table, 1.0) / tok_rows
    return complex_mul(restored, twist_cos, twist_sin)


def shards(
    query_feat,
    key_feat,
    value_feat,
    decay_rate,
    residue,
    conv_skip,
    out_weight,
    stream,
    attn_query,
    attn_key,
    attn_value,
    doc_start,
    read_mask,
):
    ctx_count = lax.axis_size("ctx")
    ctx_index = lax.axis_index("ctx")
    tok_rows = query_feat.shape[0]
    seq_len = tok_rows * ctx_count
    product = key_feat.astype(jnp.float32) * value_feat.astype(jnp.float32)
    positions = ctx_index * tok_rows + jnp.arange(tok_rows, dtype=jnp.int32)
    pos_angle = math.pi * positions.astype(jnp.float32) / seq_len
    pos_cos = jnp.cos(pos_angle)[:, None]
    pos_sin = jnp.sin(pos_angle)[:, None]
    zeros_grid = jnp.zeros_like(product)
    signal_grid = jnp.stack(
        [jnp.stack([product, product * pos_cos]), jnp.stack([zeros_grid, -product * pos_sin])]
    )
    signal_grid, freq_class = pairs_forward(signal_grid, ctx_index, ctx_count)
    digit_ids = jnp.arange(tok_rows, dtype=jnp.int32)
    table_angle = (
        2.0
        * math.pi
        * (digit_ids[:, None] * digit_ids[None, :] % tok_rows).astype(jnp.float32)
        / tok_rows
    )
    cos_table = jnp.cos(table_angle)
    sin_table = jnp.sin(table_angle)
    restored = class_filter(
        signal_grid,
        freq_class,
        decay_rate,
        residue,
        cos_table,
        sin_table,
        ctx_count,
        tok_rows,
        seq_len,
    )
    restored = pairs_inverse(restored, ctx_index, ctx_count)
    convolved = 0.5 * (restored[0, 0] + pos_cos * restored[0, 1] - pos_sin * restored[1, 1])
    hyena = (query_feat.astype(jnp.float32) * (convolved + conv_skip[None, :] * product)).astype(
        jnp.bfloat16
    )
    partial_terms = jnp.dot(hyena, out_weight, preferred_element_type=jnp.float32)
    summed = lax.psum_scatter(
        partial_terms.astype(jnp.bfloat16), "chan", scatter_dimension=1, tiled=True
    ).astype(jnp.float32)
    mixed = (stream.astype(jnp.float32) + summed).astype(jnp.bfloat16)
    heads_here = attn_query.shape[1] // HD
    key_parts = []
    value_parts = []
    for distance in range(DOC_BLOCKS, 0, -1):
        older_keys, older_values = passed_along((attn_key, attn_value), "ctx", distance)
        key_parts.append(older_keys)
        value_parts.append(older_values)
    key_window = jnp.concatenate(key_parts + [attn_key], axis=0)
    value_window = jnp.concatenate(value_parts + [attn_value], axis=0)
    window_rows = key_window.shape[0]
    queries = attn_query.reshape(tok_rows, heads_here, HD)
    keys_here = key_window.reshape(window_rows, heads_here, HD)
    values_here = value_window.reshape(window_rows, heads_here, HD)
    key_pos = (ctx_index - DOC_BLOCKS) * tok_rows + jnp.arange(window_rows, dtype=jnp.int32)
    block_live = jnp.repeat(read_mask[0][::-1], tok_rows) == 1
    allowed = (
        (key_pos[None, :] >= doc_start[:, None])
        & (key_pos[None, :] <= positions[:, None])
        & block_live[None, :]
    )
    scores = jnp.einsum(
        "qhd,khd->hqk", queries, keys_here, preferred_element_type=jnp.float32
    ) * HD ** (-0.5)
    scores = jnp.where(allowed[None], scores, -jnp.inf)
    top = jnp.max(scores, axis=-1, keepdims=True)
    weights = jnp.where(allowed[None], jnp.exp(scores - top), 0.0)
    total = jnp.sum(weights, axis=-1, keepdims=True)
    rounded = weights.astype(jnp.bfloat16)
    weighted = jnp.einsum("hqk,khd->qhd", rounded, values_here, preferred_element_type=jnp.float32)
    attended = (
        (weighted / jnp.transpose(total, (1, 0, 2)))
        .reshape(tok_rows, heads_here * HD)
        .astype(jnp.bfloat16)
    )
    return (mixed, attended)


def solution(mesh):
    in_specs = (
        P("ctx", "chan"),
        P("ctx", "chan"),
        P("ctx", "chan"),
        P("chan", None),
        P("chan", None),
        P("chan"),
        P("chan", None),
        P("ctx", "chan"),
        P("ctx", "chan"),
        P("ctx", "chan"),
        P("ctx", "chan"),
        P("ctx"),
        P("ctx", None),
    )
    out_specs = (P("ctx", "chan"), P("ctx", "chan"))
    return jax.shard_map(shards, mesh=mesh, in_specs=in_specs, out_specs=out_specs, check_vma=False)
```

profile of v0, /device:TPU:14, one launch (start us, length us, event | category | flops | bytes accessed | tf_op | source)
XLA Modules:
  0.0 282.7 jit_solution(14012144604615933620)
XLA Ops:
  9.6 2.4 collective-permute-start
  12.1 12.7 %collective-permute-done = bf16[2,2,128,512]{2,3,1,0:T(8,128)(2,1)S(1)} collective-permute-done((bf16[2,2,128,512]{2,3,1,0:T(8,128)(2,1)S(1)}, bf16[2,2,128,512]{2,3,1,0:T(8,128)(2,1)S(1)}, u32[]{:S(2)}, u32[]{:S(2)}) %collective-permute-start) | collective-permute-done | bytes 524320 | tf_op jit(solution)/shard_map/ppermute | solution.py:13
  26.6 12.4 %collective-permute-done.1 = bf16[2,2,128,512]{2,3,1,0:T(8,128)(2,1)S(1)} collective-permute-done((bf16[2,2,128,512]{2,3,1,0:T(8,128)(2,1)}, bf16[2,2,128,512]{2,3,1,0:T(8,128)(2,1)S(1)}, u32[]{:S(2)}, u32[]{:S(2)}) %collective-permute-start.1) | collective-permute-done | bytes 524320 | tf_op jit(solution)/shard_map/ppermute | solution.py:13
  40.2 7.2 %collective-permute-start.2 = (bf16[2,2,128,512]{2,3,1,0:T(8,128)(2,1)}, bf16[2,2,128,512]{2,3,1,0:T(8,128)(2,1)S(1)}, u32[]{:S(2)}, u32[]{:S(2)}) collective-permute-start(bf16[2,2,128,512]{2,3,1,0:T(8,128)(2,1)} %get-tuple-element.28), channel_id=1, source_target_pairs={{0,32},{4,36},{8,40},{12,44},{16,48},{20,52},{24,56},{28,60},{32,0... | collective-permute-start | bytes 1572872 | tf_op jit(solution)/shard_map/ppermute | solution.py:13
  48.0 12.1 %collective-permute-done.2 = bf16[2,2,128,512]{2,3,1,0:T(8,128)(2,1)S(1)} collective-permute-done((bf16[2,2,128,512]{2,3,1,0:T(8,128)(2,1)}, bf16[2,2,128,512]{2,3,1,0:T(8,128)(2,1)S(1)}, u32[]{:S(2)}, u32[]{:S(2)}) %collective-permute-start.2) | collective-permute-done | bytes 524320 | tf_op jit(solution)/shard_map/ppermute | solution.py:13
  60.4 11.0 %collective-permute-start.3 = (bf16[2,2,128,512]{2,3,1,0:T(8,128)(2,1)S(1)}, bf16[2,2,128,512]{2,3,1,0:T(8,128)(2,1)S(1)}, u32[]{:S(2)}, u32[]{:S(2)}) collective-permute-start(bf16[2,2,128,512]{2,3,1,0:T(8,128)(2,1)S(1)} %get-tuple-element.26), channel_id=1, source_target_pairs={{0,16},{4,20},{8,24},{12,28},{16,0},{20,4},{24,8},{28,12},{32,48},... | collective-permute-start | bytes 1572872 | tf_op jit(solution)/shard_map/ppermute | solution.py:13
  71.5 22.3 %collective-permute-done.3 = bf16[2,2,128,512]{2,3,1,0:T(8,128)(2,1)S(1)} collective-permute-done((bf16[2,2,128,512]{2,3,1,0:T(8,128)(2,1)S(1)}, bf16[2,2,128,512]{2,3,1,0:T(8,128)(2,1)S(1)}, u32[]{:S(2)}, u32[]{:S(2)}) %collective-permute-start.3) | collective-permute-done | bytes 524320 | tf_op jit(solution)/shard_map/ppermute | solution.py:13
  94.9 13.3 %collective-permute-done.4 = bf16[2,2,128,512]{2,3,1,0:T(8,128)(2,1)S(1)} collective-permute-done((bf16[2,2,128,512]{2,3,1,0:T(8,128)(2,1)S(1)}, bf16[2,2,128,512]{2,3,1,0:T(8,128)(2,1)S(1)}, u32[]{:S(2)}, u32[]{:S(2)}) %collective-permute-start.4) | collective-permute-done | bytes 524320 | tf_op jit(solution)/shard_map/ppermute | solution.py:13
  113.5 5.0 %multiply_subtract_fusion.13 = (f32[2,128,512]{1,2,0:T(8,128)S(1)}, f32[2,128,512]{1,2,0:T(8,128)S(1)}, f32[2,128,512]{1,2,0:T(8,128)S(1)}, f32[2,128,512]{1,2,0:T(8,128)S(1)}) fusion(f32[2,128,512]{1,2,0:T(8,128)S(1)} %fusion.8, f32[512]{0:T(512)S(1)} %bitcast.263, f32[512]{0:T(512)S(1)} %bitcast.262, f32[512]{0:T(512)S(1)} %bitcast.224, ...), kind=kOutput, calls=%fused_computation.188 | convolution fusion | flops 231833600 | bytes 4330496 | tf_op jit(solution)/shard_map/dm,bmc->bdc/dot_general | solution.py:29
  125.5 13.4 %collective-permute-done.7 = bf16[2,2,128,512]{2,3,1,0:T(8,128)(2,1)S(1)} collective-permute-done((bf16[2,2,128,512]{2,3,1,0:T(8,128)(2,1)S(1)}, bf16[2,2,128,512]{2,3,1,0:T(8,128)(2,1)S(1)}, u32[]{:S(2)}, u32[]{:S(2)}) %collective-permute-start.7) | collective-permute-done | bytes 524320 | tf_op jit(solution)/shard_map/ppermute | solution.py:13
  140.4 24.9 %collective-permute-done.8 = bf16[2,2,128,512]{2,3,1,0:T(8,128)(2,1)S(1)} collective-permute-done((bf16[2,2,128,512]{2,3,1,0:T(8,128)(2,1)}, bf16[2,2,128,512]{2,3,1,0:T(8,128)(2,1)S(1)}, u32[]{:S(2)}, u32[]{:S(2)}) %collective-permute-start.8) | collective-permute-done | bytes 524320 | tf_op jit(solution)/shard_map/ppermute | solution.py:13
  166.6 4.2 %collective-permute-start.9 = (bf16[2,2,128,512]{2,3,1,0:T(8,128)(2,1)}, bf16[2,2,128,512]{2,3,1,0:T(8,128)(2,1)S(1)}, u32[]{:S(2)}, u32[]{:S(2)}) collective-permute-start(bf16[2,2,128,512]{2,3,1,0:T(8,128)(2,1)} %get-tuple-element.10), channel_id=1, source_target_pairs={{0,32},{4,36},{8,40},{12,44},{16,48},{20,52},{24,56},{28,60},{32,0... | collective-permute-start | bytes 1572872 | tf_op jit(solution)/shard_map/ppermute | solution.py:13
  171.1 24.8 %collective-permute-done.9 = bf16[2,2,128,512]{2,3,1,0:T(8,128)(2,1)S(1)} collective-permute-done((bf16[2,2,128,512]{2,3,1,0:T(8,128)(2,1)}, bf16[2,2,128,512]{2,3,1,0:T(8,128)(2,1)S(1)}, u32[]{:S(2)}, u32[]{:S(2)}) %collective-permute-start.9) | collective-permute-done | bytes 524320 | tf_op jit(solution)/shard_map/ppermute | solution.py:13
  198.0 12.4 %collective-permute-done.10 = bf16[2,2,128,512]{2,3,1,0:T(8,128)(2,1)S(1)} collective-permute-done((bf16[2,2,128,512]{2,3,1,0:T(8,128)(2,1)}, bf16[2,2,128,512]{2,3,1,0:T(8,128)(2,1)S(1)}, u32[]{:S(2)}, u32[]{:S(2)}) %collective-permute-start.10) | collective-permute-done | bytes 524320 | tf_op jit(solution)/shard_map/ppermute | solution.py:13
  211.7 2.3 collective-permute-start.11
  214.4 11.0 %collective-permute-done.11 = bf16[2,2,128,512]{2,3,1,0:T(8,128)(2,1)S(1)} collective-permute-done((bf16[2,2,128,512]{2,3,1,0:T(8,128)(2,1)}, bf16[2,2,128,512]{2,3,1,0:T(8,128)(2,1)S(1)}, u32[]{:S(2)}, u32[]{:S(2)}) %collective-permute-start.11) | collective-permute-done | bytes 524320 | tf_op jit(solution)/shard_map/ppermute | solution.py:13
  227.8 2.0 convolution_convert_fusion
  230.0 1.9 collective-permute-start.15
  233.9 6.8 %collective-permute-start.12 = (bf16[128,1024]{1,0:T(8,128)(2,1)S(1)}, bf16[128,1024]{1,0:T(8,128)(2,1)S(1)}, u32[]{:S(2)}, u32[]{:S(2)}) collective-permute-start(bf16[128,1024]{1,0:T(8,128)(2,1)S(1)} %copy-done.4), channel_id=1, source_target_pairs={{0,12},{4,16},{8,20},{12,24},{16,28},{20,32},{24,36},{28,40},{32,4... | collective-permute-start | bytes 786440 | tf_op jit(solution)/shard_map/ppermute | solution.py:19
  240.7 2.2 collective-permute-start.13
  242.9 2.1 collective-permute-start.14
  245.2 14.3 %collective-permute-done.12 = bf16[128,1024]{1,0:T(8,128)(2,1)S(1)} collective-permute-done((bf16[128,1024]{1,0:T(8,128)(2,1)S(1)}, bf16[128,1024]{1,0:T(8,128)(2,1)S(1)}, u32[]{:S(2)}, u32[]{:S(2)}) %collective-permute-start.12) | collective-permute-done | bytes 262176 | tf_op jit(solution)/shard_map/ppermute | solution.py:19
  264.0 5.3 %collective-permute-done.17 = bf16[128,1024]{0,1:T(8,128)(2,1)S(1)} collective-permute-done((bf16[128,1024]{0,1:T(8,128)(2,1)S(1)}, bf16[128,1024]{0,1:T(8,128)(2,1)S(1)}, u32[]{:S(2)}, u32[]{:S(2)}) %collective-permute-start.17) | collective-permute-done | bytes 262176 | tf_op jit(solution)/shard_map/ppermute | solution.py:19
  271.0 2.3 fusion.9
  (126 shorter events, 38.1 us)
Async XLA Ops:
  7.2 262.3 %copy-start = (bf16[128,1024]{1,0:T(8,128)(2,1)S(1)}, bf16[128,1024]{1,0:T(8,128)(2,1)}, u32[]{:S(2)}) copy-start(bf16[128,1024]{1,0:T(8,128)(2,1)} %param.21) | copy-start | bytes 786436
  7.2 267.0 %reduce-scatter.2.cloned.1.call-start = ((), (), s32[]{:S(2)}) async-start(), calls=%async_computation.1 | async-start | bytes 1310720 | tf_op jit(solution)/shard_map/reduce_scatter | solution.py:182
  9.6 15.3 %collective-permute-start = (bf16[2,2,128,512]{2,3,1,0:T(8,128)(2,1)S(1)}, bf16[2,2,128,512]{2,3,1,0:T(8,128)(2,1)S(1)}, u32[]{:S(2)}, u32[]{:S(2)}) collective-permute-start(bf16[2,2,128,512]{2,3,1,0:T(8,128)(2,1)S(1)} %fusion.39), channel_id=1, source_target_pairs={{0,128},{4,132},{8,136},{12,140},{16,144},{20,148},{24,152},{28,15... | collective-permute-start | bytes 1572872 | tf_op jit(solution)/shard_map/ppermute | solution.py:13
  26.0 13.0 %collective-permute-start.1 = (bf16[2,2,128,512]{2,3,1,0:T(8,128)(2,1)}, bf16[2,2,128,512]{2,3,1,0:T(8,128)(2,1)S(1)}, u32[]{:S(2)}, u32[]{:S(2)}) collective-permute-start(bf16[2,2,128,512]{2,3,1,0:T(8,128)(2,1)} %get-tuple-element.30), channel_id=1, source_target_pairs={{0,64},{4,68},{8,72},{12,76},{16,80},{20,84},{24,88},{28,92},{32,9... | collective-permute-start | bytes 1572872 | tf_op jit(solution)/shard_map/ppermute | solution.py:13
  40.2 19.8 %collective-permute-start.2 = (bf16[2,2,128,512]{2,3,1,0:T(8,128)(2,1)}, bf16[2,2,128,512]{2,3,1,0:T(8,128)(2,1)S(1)}, u32[]{:S(2)}, u32[]{:S(2)}) collective-permute-start(bf16[2,2,128,512]{2,3,1,0:T(8,128)(2,1)} %get-tuple-element.28), channel_id=1, source_target_pairs={{0,32},{4,36},{8,40},{12,44},{16,48},{20,52},{24,56},{28,60},{32,0... | collective-permute-start | bytes 1572872 | tf_op jit(solution)/shard_map/ppermute | solution.py:13
  60.4 33.4 %collective-permute-start.3 = (bf16[2,2,128,512]{2,3,1,0:T(8,128)(2,1)S(1)}, bf16[2,2,128,512]{2,3,1,0:T(8,128)(2,1)S(1)}, u32[]{:S(2)}, u32[]{:S(2)}) collective-permute-start(bf16[2,2,128,512]{2,3,1,0:T(8,128)(2,1)S(1)} %get-tuple-element.26), channel_id=1, source_target_pairs={{0,16},{4,20},{8,24},{12,28},{16,0},{20,4},{24,8},{28,12},{32,48},... | collective-permute-start | bytes 1572872 | tf_op jit(solution)/shard_map/ppermute | solution.py:13
  94.2 13.9 %collective-permute-start.4 = (bf16[2,2,128,512]{2,3,1,0:T(8,128)(2,1)S(1)}, bf16[2,2,128,512]{2,3,1,0:T(8,128)(2,1)S(1)}, u32[]{:S(2)}, u32[]{:S(2)}) collective-permute-start(bf16[2,2,128,512]{2,3,1,0:T(8,128)(2,1)S(1)} %get-tuple-element.24), channel_id=1, source_target_pairs={{0,8},{4,12},{8,0},{12,4},{16,24},{20,28},{24,16},{28,20},{32,40},... | collective-permute-start | bytes 1572872 | tf_op jit(solution)/shard_map/ppermute | solution.py:13
  108.5 2.2 collective-permute-start.5
  122.2 2.2 collective-permute-start.6
  124.8 14.1 %collective-permute-start.7 = (bf16[2,2,128,512]{2,3,1,0:T(8,128)(2,1)S(1)}, bf16[2,2,128,512]{2,3,1,0:T(8,128)(2,1)S(1)}, u32[]{:S(2)}, u32[]{:S(2)}) collective-permute-start(bf16[2,2,128,512]{2,3,1,0:T(8,128)(2,1)S(1)} %get-tuple-element.14), channel_id=1, source_target_pairs={{0,8},{4,12},{8,0},{12,4},{16,24},{20,28},{24,16},{28,20},{32,40},... | collective-permute-start | bytes 1572872 | tf_op jit(solution)/shard_map/ppermute | solution.py:13
  140.2 25.2 %collective-permute-start.8 = (bf16[2,2,128,512]{2,3,1,0:T(8,128)(2,1)}, bf16[2,2,128,512]{2,3,1,0:T(8,128)(2,1)S(1)}, u32[]{:S(2)}, u32[]{:S(2)}) collective-permute-start(bf16[2,2,128,512]{2,3,1,0:T(8,128)(2,1)} %get-tuple-element.12), channel_id=1, source_target_pairs={{0,16},{4,20},{8,24},{12,28},{16,0},{20,4},{24,8},{28,12},{32,48},... | collective-permute-start | bytes 1572872 | tf_op jit(solution)/shard_map/ppermute | solution.py:13
  166.6 29.3 %collective-permute-start.9 = (bf16[2,2,128,512]{2,3,1,0:T(8,128)(2,1)}, bf16[2,2,128,512]{2,3,1,0:T(8,128)(2,1)S(1)}, u32[]{:S(2)}, u32[]{:S(2)}) collective-permute-start(bf16[2,2,128,512]{2,3,1,0:T(8,128)(2,1)} %get-tuple-element.10), channel_id=1, source_target_pairs={{0,32},{4,36},{8,40},{12,44},{16,48},{20,52},{24,56},{28,60},{32,0... | collective-permute-start | bytes 1572872 | tf_op jit(solution)/shard_map/ppermute | solution.py:13
  197.2 13.2 %collective-permute-start.10 = (bf16[2,2,128,512]{2,3,1,0:T(8,128)(2,1)}, bf16[2,2,128,512]{2,3,1,0:T(8,128)(2,1)S(1)}, u32[]{:S(2)}, u32[]{:S(2)}) collective-permute-start(bf16[2,2,128,512]{2,3,1,0:T(8,128)(2,1)} %get-tuple-element.8), channel_id=1, source_target_pairs={{0,64},{4,68},{8,72},{12,76},{16,80},{20,84},{24,88},{28,92},{32,9... | collective-permute-start | bytes 1572872 | tf_op jit(solution)/shard_map/ppermute | solution.py:13
  211.7 13.7 %collective-permute-start.11 = (bf16[2,2,128,512]{2,3,1,0:T(8,128)(2,1)}, bf16[2,2,128,512]{2,3,1,0:T(8,128)(2,1)S(1)}, u32[]{:S(2)}, u32[]{:S(2)}) collective-permute-start(bf16[2,2,128,512]{2,3,1,0:T(8,128)(2,1)} %get-tuple-element.6), channel_id=1, source_target_pairs={{0,128},{4,132},{8,136},{12,140},{16,144},{20,148},{24,152},{28,15... | collective-permute-start | bytes 1572872 | tf_op jit(solution)/shard_map/ppermute | solution.py:13
  227.8 6.1 %copy-start.4 = (bf16[128,1024]{1,0:T(8,128)(2,1)S(1)}, bf16[128,1024]{1,0:T(8,128)(2,1)}, u32[]{:S(2)}) copy-start(bf16[128,1024]{1,0:T(8,128)(2,1)} %param.23) | copy-start | bytes 786436
  227.8 17.2 %copy-start.11 = (s32[1,4]{1,0:T(1,128)S(1)}, s32[1,4]{1,0:T(1,128)}, u32[]{:S(2)}) copy-start(s32[1,4]{1,0:T(1,128)} %param.25) | copy-start | bytes 52
  227.8 33.6 %copy-start.10 = (s32[128]{0:T(128)S(1)}, s32[128]{0:T(128)}, u32[]{:S(2)}) copy-start(s32[128]{0:T(128)} %param.24) | copy-start | bytes 1540
  230.0 34.0 %collective-permute-start.15 = (bf16[128,1024]{0,1:T(8,128)(2,1)S(1)}, bf16[128,1024]{0,1:T(8,128)(2,1)S(1)}, u32[]{:S(2)}, u32[]{:S(2)}) collective-permute-start(bf16[128,1024]{0,1:T(8,128)(2,1)S(1)} %copy.26), channel_id=1, source_target_pairs={{0,12},{4,16},{8,20},{12,24},{16,28},{20,32},{24,36},{28,40},{32,4... | collective-permute-start | bytes 786440 | tf_op jit(solution)/shard_map/ppermute | solution.py:19
  231.9 32.0 %collective-permute-start.16 = (bf16[128,1024]{0,1:T(8,128)(2,1)S(1)}, bf16[128,1024]{0,1:T(8,128)(2,1)S(1)}, u32[]{:S(2)}, u32[]{:S(2)}) collective-permute-start(bf16[128,1024]{0,1:T(8,128)(2,1)S(1)} %copy.26), channel_id=1, source_target_pairs={{0,8},{4,12},{8,16},{12,20},{16,24},{20,28},{24,32},{28,36},{32,40... | collective-permute-start | bytes 786440 | tf_op jit(solution)/shard_map/ppermute | solution.py:19
  233.9 25.6 %collective-permute-start.12 = (bf16[128,1024]{1,0:T(8,128)(2,1)S(1)}, bf16[128,1024]{1,0:T(8,128)(2,1)S(1)}, u32[]{:S(2)}, u32[]{:S(2)}) collective-permute-start(bf16[128,1024]{1,0:T(8,128)(2,1)S(1)} %copy-done.4), channel_id=1, source_target_pairs={{0,12},{4,16},{8,20},{12,24},{16,28},{20,32},{24,36},{28,40},{32,4... | collective-permute-start | bytes 786440 | tf_op jit(solution)/shard_map/ppermute | solution.py:19
  240.7 20.9 %collective-permute-start.13 = (bf16[128,1024]{1,0:T(8,128)(2,1)S(1)}, bf16[128,1024]{1,0:T(8,128)(2,1)S(1)}, u32[]{:S(2)}, u32[]{:S(2)}) collective-permute-start(bf16[128,1024]{1,0:T(8,128)(2,1)S(1)} %copy-done.4), channel_id=1, source_target_pairs={{0,8},{4,12},{8,16},{12,20},{16,24},{20,28},{24,32},{28,36},{32,40... | collective-permute-start | bytes 786440 | tf_op jit(solution)/shard_map/ppermute | solution.py:19
  242.9 19.6 %collective-permute-start.14 = (bf16[128,1024]{1,0:T(8,128)(2,1)S(1)}, bf16[128,1024]{1,0:T(8,128)(2,1)S(1)}, u32[]{:S(2)}, u32[]{:S(2)}) collective-permute-start(bf16[128,1024]{1,0:T(8,128)(2,1)S(1)} %copy-done.4), channel_id=1, source_target_pairs={{0,4},{4,8},{8,12},{12,16},{16,20},{20,24},{24,28},{28,32},{32,36}... | collective-permute-start | bytes 786440 | tf_op jit(solution)/shard_map/ppermute | solution.py:19
  259.5 9.8 %collective-permute-start.17 = (bf16[128,1024]{0,1:T(8,128)(2,1)S(1)}, bf16[128,1024]{0,1:T(8,128)(2,1)S(1)}, u32[]{:S(2)}, u32[]{:S(2)}) collective-permute-start(bf16[128,1024]{0,1:T(8,128)(2,1)S(1)} %copy.26), channel_id=1, source_target_pairs={{0,4},{4,8},{8,12},{12,16},{16,20},{20,24},{24,28},{28,32},{32,36}... | collective-permute-start | bytes 786440 | tf_op jit(solution)/shard_map/ppermute | solution.py:19
  261.6 7.8 %copy-start.7 = (pred[128,512]{0,1:T(8,128)(4,1)}, pred[128,512]{0,1:T(8,128)(4,1)S(1)}, u32[]{:S(2)}) copy-start(pred[128,512]{0,1:T(8,128)(4,1)S(1)} %and_and_fusion) | copy-start | bytes 196612
  (7 other events, 14.7 us)
Sparse Core Ops, SparseCore 0:
  229.9 23.9 reduce-scatter.1
where the time goes:
time: 283 us
  waiting for transfers between devices  183 us (65%)
  starting transfers between devices  46 us (16%)
  matrix products  16.5 us (6%)
  between operations  16.4 us (6%)
  other arithmetic  13.4 us (5%)
  local copies, waits for them, and re-layouts  7.11 us (3%)
    ppermute x12, waiting for transfers between devices, partner_2(): lax.ppermute(shard, axis, [(i, i ^ 1 << bit) for i in range(lax.axis_size...  163 us
    ppermute x12, starting transfers between devices, partner_2(): lax.ppermute(shard, axis, [(i, i ^ 1 << bit) for i in range(lax.axis_size...  29.1 us
    ppermute x6, waiting for transfers between devices, passed_along(): lax.ppermute(value, axis, [(source, source + steps) for source in range(i...  20.5 us
    ppermute x6, starting transfers between devices, passed_along(): lax.ppermute(value, axis, [(source, source + steps) for source in range(i...  16.8 us
    dot_general x8, matrix products, table_product(): jnp.einsum('dm,bmc->bdc', table, operand, precision=lax.Precision.HIGHEST)  10.7 us
  transfers between devices with their start and end apart: 19, of which 15 were waited for; matrix products, arithmetic and copies ran while one was open for 3% of the time, Pallas kernels for 0%

commit v1 on v0

v1 whole, which is shorter than its diff:
```python
import math

import jax
import jax.numpy as jnp
from jax import lax
from jax.experimental import pallas as pl
from jax.experimental.pallas import tpu as pltpu
from jax.sharding import PartitionSpec as P

HD = 128
LANES = 128
DOC_BLOCKS = 3
VMEM = pltpu.VMEM


def whole(count):
    return [pl.BlockSpec(memory_space=VMEM) for _ in range(count)]


def shifted(value, axis, steps):
    count = lax.axis_size(axis)
    return lax.ppermute(value, axis, [(i, (i + steps) % count) for i in range(count)])


def core_swap(value):
    count = lax.axis_size("ctx")
    return lax.ppermute(value, "ctx", [(i, i ^ 1) for i in range(count)])


def room(mib):
    return pltpu.CompilerParams(vmem_limit_bytes=mib * 1024 * 1024)


def to_state_rows(source_ref, target_ref, groups):
    for g in range(groups):
        block = source_ref[:, g * LANES : (g + 1) * LANES]
        target_ref[pl.ds(g, block.shape[0], stride=groups), :] = block


def to_position_rows(product, target_ref, groups):
    rows = product.shape[0]
    for g in range(groups):
        block = product[:, g * LANES : (g + 1) * LANES]
        for half in range(2):
            target_ref[pl.ds(half * groups + g, rows, stride=2 * groups), :] = block


def states_kernel(
    key_ref, value_ref, decay_ref, keep_ref, send_ref, rates_ref, product_ref, state_ref
):
    groups = key_ref.shape[1] // LANES
    rows = key_ref.shape[0]
    to_state_rows(decay_ref, rates_ref, groups)
    product = key_ref[...].astype(jnp.float32) * value_ref[...].astype(jnp.float32)
    to_position_rows(product, product_ref, groups)
    count = rates_ref.shape[0] // 8
    steps = [jnp.exp(-rates_ref[8 * i : 8 * i + 8, :]) for i in range(count)]
    parts = 4
    span = rows // parts
    states = [[jnp.zeros((8, LANES), jnp.float32)] * count for _ in range(parts)]
    for t in range(span):
        for part in range(parts):
            row = 8 * (part * span + t)
            value = product_ref[row : row + 8, :]
            states[part] = [s * a + value for s, a in zip(states[part], steps)]
    for i in range(count):
        long_step = jnp.exp(-span * rates_ref[8 * i : 8 * i + 8, :])
        total = states[0][i]
        for part in range(1, parts):
            total = total * long_step + states[part][i]
        state_ref[8 * i : 8 * i + 8, :] = total
    core = lax.rem(lax.axis_index("ctx"), 2)
    half = state_ref.shape[0] // 2
    keep_ref[...] = state_ref[pl.ds(pl.multiple_of(core * half, half), half), :]
    send_ref[...] = state_ref[pl.ds(pl.multiple_of((1 - core) * half, half), half), :]


def pair_kernel(rows, keep_ref, got_ref, rates_ref, out_ref):
    core = lax.rem(lax.axis_index("ctx"), 2)
    half = keep_ref.shape[0]
    rates = rates_ref[pl.ds(pl.multiple_of(core * half, half), half), :]
    keep, got = keep_ref[...], got_ref[...]
    first = jnp.where(core == 0, keep, got)
    second = jnp.where(core == 0, got, keep)
    both = (first * jnp.exp(-rows * rates) + second).astype(out_ref.dtype)
    for i in range(out_ref.shape[0]):
        out_ref[i] = both


def carry_kernel(rows, all_ref, keep_ref, got_ref, rates_ref, mine_ref, other_ref):
    index = lax.axis_index("ctx")
    core = lax.rem(index, 2)
    chip = lax.div(index, 2)
    half = keep_ref.shape[0]
    rates = rates_ref[pl.ds(pl.multiple_of(core * half, half), half), :]
    step = jnp.exp(-2 * rows * rates)
    carry = jnp.zeros((half, LANES), jnp.float32)
    for i in range(all_ref.shape[0] - 1):
        carry = jnp.where(i < chip, carry * step + all_ref[i].astype(jnp.float32), carry)
    first = jnp.where(core == 0, keep_ref[...], got_ref[...])
    later = carry * jnp.exp(-rows * rates) + first
    mine_ref[...] = jnp.where(core == 0, carry, later)
    other_ref[...] = jnp.where(core == 0, later, carry)


def project_kernel(
    query_ref,
    key_ref,
    value_ref,
    rates_ref,
    residue_ref,
    skip_ref,
    mine_ref,
    other_ref,
    weight_hbm,
    own_ref,
    near_ref,
    far_ref,
    back_ref,
    product_ref,
    weights_ref,
    state_ref,
    conv_ref,
    weight_ref,
    sems,
):
    chan = lax.axis_index("chan")
    groups = key_ref.shape[1] // LANES
    rows = key_ref.shape[0]
    chans = weight_hbm.shape[1] // own_ref.shape[1]
    width = own_ref.shape[1]
    order = [2, 1, 3, 0]
    copies = []
    for slot, ahead in enumerate(order):
        column = pl.multiple_of(lax.rem(chan + ahead, chans) * width, width)
        copies.append(
            pltpu.make_async_copy(
                weight_hbm.at[:, pl.ds(column, width)], weight_ref.at[slot], sems.at[slot]
            )
        )
        copies[-1].start()
    to_state_rows(residue_ref, weights_ref, groups)
    product = key_ref[...].astype(jnp.float32) * value_ref[...].astype(jnp.float32)
    to_position_rows(product, product_ref, groups)
    core = lax.rem(lax.axis_index("ctx"), 2)
    half = mine_ref.shape[0]
    state_ref[pl.ds(pl.multiple_of(core * half, half), half), :] = mine_ref[...]
    state_ref[pl.ds(pl.multiple_of((1 - core) * half, half), half), :] = other_ref[...]
    count = rates_ref.shape[0] // 8
    steps = [jnp.exp(-rates_ref[8 * i : 8 * i + 8, :]) for i in range(count)]
    scale = [weights_ref[8 * i : 8 * i + 8, :] for i in range(count)]
    states = [state_ref[8 * i : 8 * i + 8, :] for i in range(count)]
    for t in range(rows):
        value = product_ref[8 * t : 8 * t + 8, :]
        states = [s * a + value for s, a in zip(states, steps)]
        terms = [s * w for s, w in zip(states, scale)]
        while len(terms) > 1:
            terms = [u + v for u, v in zip(terms[::2], terms[1::2])]
        conv_ref[8 * t : 8 * t + 8, :] = terms[0]
    blocks = []
    for g in range(groups):
        conv = (
            conv_ref[pl.ds(g, rows, stride=2 * groups), :]
            + conv_ref[pl.ds(groups + g, rows, stride=2 * groups), :]
        )
        lanes = slice(g * LANES, (g + 1) * LANES)
        skipped = skip_ref[:, lanes] * product[:, lanes]
        blocks.append(
            (query_ref[:, lanes].astype(jnp.float32) * (conv + skipped)).astype(jnp.bfloat16)
        )
    hyena = jnp.concatenate(blocks, axis=1)
    targets = [far_ref, near_ref, back_ref, own_ref]
    for slot, target in enumerate(targets):
        copies[slot].wait()
        target[...] = jnp.dot(
            hyena, weight_ref[slot], preferred_element_type=jnp.float32
        ).astype(target.dtype)


def attention_kernel(
    query_ref, key_ref, value_ref, one_ref, two_ref, three_ref, start_ref, read_ref, out_ref
):
    rows = query_ref.shape[0]
    base = lax.axis_index("ctx") * rows
    starts = jnp.broadcast_to(start_ref[...] - base, (rows, rows)).T
    query_pos = lax.broadcasted_iota(jnp.int32, (rows, rows), 0)
    key_pos = lax.broadcasted_iota(jnp.int32, (rows, rows), 1)
    allowed = []
    for back in range(DOC_BLOCKS, -1, -1):
        pos = key_pos - back * rows
        ok = (pos >= starts) & (read_ref[0, back] == 1)
        if back == 0:
            ok = ok & (pos <= query_pos)
        allowed.append(ok)
    mask = jnp.concatenate(allowed, axis=1)
    for head in range(query_ref.shape[1] // HD):
        cols = slice(head * HD, (head + 1) * HD)
        query = query_ref[:, cols]
        keys = [r[:rows, cols] for r in (three_ref, two_ref, one_ref)] + [key_ref[:, cols]]
        values = [r[rows:, cols] for r in (three_ref, two_ref, one_ref)] + [value_ref[:, cols]]
        keys = jnp.concatenate(keys, axis=0)
        values = jnp.concatenate(values, axis=0)
        scores = lax.dot_general(
            query, keys, (((1,), (1,)), ((), ())), preferred_element_type=jnp.float32
        )
        scores = jnp.where(mask, scores * HD ** (-0.5), -jnp.inf)
        top = jnp.max(scores, axis=1, keepdims=True)
        weights = jnp.exp(scores - top)
        total = jnp.sum(weights, axis=1, keepdims=True)
        summed = jnp.dot(weights.astype(jnp.bfloat16), values, preferred_element_type=jnp.float32)
        out_ref[:, cols] = (summed / total).astype(out_ref.dtype)


def shards(
    query_feat,
    key_feat,
    value_feat,
    decay_rate,
    residue,
    conv_skip,
    out_weight,
    stream,
    attn_query,
    attn_key,
    attn_value,
    doc_start,
    read_mask,
):
    ctx_count = lax.axis_size("ctx")
    rows, channels = query_feat.shape
    order = decay_rate.shape[1]
    state_rows = order * channels // LANES
    half = state_rows // 2
    chips = ctx_count // 2
    f32, bf16 = jnp.float32, jnp.bfloat16
    state_half = jax.ShapeDtypeStruct((half, LANES), f32)

    key_value = jnp.concatenate([attn_key, attn_value], axis=0)
    two_back = shifted(key_value, "ctx", 2)
    one_back = shifted(key_value, "ctx", 1)
    three_back = shifted(two_back, "ctx", 1)

    keep, send, rates = pl.pallas_call(
        states_kernel,
        out_shape=(state_half, state_half, jax.ShapeDtypeStruct((state_rows, LANES), f32)),
        in_specs=whole(3),
        out_specs=tuple(whole(3)),
        scratch_shapes=[VMEM((8 * rows, LANES), f32), VMEM((state_rows, LANES), f32)],
        compiler_params=room(4),
        name="filter_states",
    )(key_feat, value_feat, decay_rate.T)
    got = core_swap(send)
    spread = pl.pallas_call(
        lambda *refs: pair_kernel(rows, *refs),
        out_shape=jax.ShapeDtypeStruct((chips, half, LANES), bf16),
        in_specs=whole(3),
        out_specs=whole(1)[0],
        compiler_params=room(4),
        name="chip_states",
    )(keep, got, rates)
    groups = [list(range(core, ctx_count, 2)) for core in range(2)]
    spread = lax.all_to_all(spread, "ctx", 0, 0, axis_index_groups=groups)
    mine, other = pl.pallas_call(
        lambda *refs: carry_kernel(rows, *refs),
        out_shape=(state_half, state_half),
        in_specs=whole(4),
        out_specs=tuple(whole(2)),
        compiler_params=room(4),
        name="carried_states",
    )(spread, keep, got, rates)
    other = core_swap(other)

    width = out_weight.shape[1] // lax.axis_size("chan")
    piece = jax.ShapeDtypeStruct((rows, width), bf16)
    own, near, far, back = pl.pallas_call(
        project_kernel,
        out_shape=(jax.ShapeDtypeStruct((rows, width), f32), piece, piece, piece),
        in_specs=whole(8) + [pl.BlockSpec(memory_space=pl.ANY)],
        out_specs=tuple(whole(4)),
        scratch_shapes=[
            VMEM((8 * rows, LANES), f32),
            VMEM((state_rows, LANES), f32),
            VMEM((state_rows, LANES), f32),
            VMEM((8 * rows, LANES), f32),
            VMEM((4, channels, width), bf16),
            pltpu.SemaphoreType.DMA((4,)),
        ],
        compiler_params=room(12),
        name="project",
    )(
        query_feat,
        key_feat,
        value_feat,
        rates,
        residue.T,
        conv_skip.reshape(1, channels),
        mine,
        other,
        out_weight,
    )
    far = shifted(far, "chan", 2)
    near = shifted(near, "chan", 1)
    back = shifted(back, "chan", 3)

    attended = pl.pallas_call(
        attention_kernel,
        out_shape=jax.ShapeDtypeStruct(attn_query.shape, bf16),
        in_specs=whole(7) + [pl.BlockSpec(memory_space=pltpu.SMEM)],
        out_specs=whole(1)[0],
        compiler_params=room(12),
        name="attention",
    )(
        attn_query,
        attn_key,
        attn_value,
        one_back,
        two_back,
        three_back,
        doc_start.reshape(1, rows),
        read_mask,
    )
    summed = own + far.astype(f32) + near.astype(f32) + back.astype(f32)
    mixed = (stream.astype(f32) + summed).astype(bf16)
    return (mixed, attended)


def solution(mesh):
    in_specs = (
        P("ctx", "chan"),
        P("ctx", "chan"),
        P("ctx", "chan"),
        P("chan", None),
        P("chan", None),
        P("chan"),
        P("chan", None),
        P("ctx", "chan"),
        P("ctx", "chan"),
        P("ctx", "chan"),
        P("ctx", "chan"),
        P("ctx"),
        P("ctx", None),
    )
    out_specs = (P("ctx", "chan"), P("ctx", "chan"))
    return jax.shard_map(shards, mesh=mesh, in_specs=in_specs, out_specs=out_specs, check_vma=False)
```

time: 283 us -> 68.3 us (0.24)
  the two profiles are of different devices: /device:TPU:14 before, /device:TPU:2 now
where the time goes in v1:
time: 68.3 us; the launch traced here: 67.8 us
  waiting for transfers between devices  27.9 us (41%)
  starting transfers between devices  19.9 us (29%)
  local copies, waits for them, and re-layouts  10.9 us (16%)
  Pallas kernels  7.35 us (11%)
  other arithmetic  0.91 us (1%)
  between operations  0.76 us (1%)
    ppermute x6, waiting for transfers between devices, shifted(): lax.ppermute(value, axis, [(i, (i + steps) % count) for i in range(count)])  15.7 us
    all_to_all x1, starting transfers between devices, shards(): spread = lax.all_to_all(spread, 'ctx', 0, 0, axis_index_groups=groups)  11.5 us
    all_to_all x1, waiting for transfers between devices, shards(): spread = lax.all_to_all(spread, 'ctx', 0, 0, axis_index_groups=groups)  10.9 us
    unnamed x31, local copies, waits for them, and re-layouts  9.9 us
    ppermute x6, starting transfers between devices, shifted(): lax.ppermute(value, axis, [(i, (i + steps) % count) for i in range(count)])  8.24 us
    pallas_call x1, Pallas kernels, shards(): pl.pallas_call(attention_kernel, out_shape=jax.ShapeDtypeStruct(attn_quer...  3.54 us
    pallas_call x1, Pallas kernels, shards(): pl.pallas_call(project_kernel, out_shape=(jax.ShapeDtypeStruct((rows, wid...  2.6 us
  transfers between devices with their start and end apart: 9, of which 8 were waited for; matrix products, arithmetic and copies ran while one was open for 4% of the time, Pallas kernels for 4%

profile of v1, /device:TPU:2, one launch (start us, length us, event | category | flops | bytes accessed | tf_op | source)
XLA Modules:
  0.0 67.8 jit_solution(16622859206678919151)
XLA Ops:
  0.6 0.9 %copy-done.3 = bf16[128,512]{1,0:T(8,128)(2,1)S(1)} copy-done((bf16[128,512]{1,0:T(8,128)(2,1)S(1)}, bf16[128,512]{1,0:T(8,128)(2,1)}, u32[]{:S(2)}) %copy-start.3) | copy-done | bytes 131096
  1.5 0.9 %copy-done.5 = bf16[128,512]{1,0:T(8,128)(2,1)S(1)} copy-done((bf16[128,512]{1,0:T(8,128)(2,1)S(1)}, bf16[128,512]{1,0:T(8,128)(2,1)}, u32[]{:S(2)}) %copy-start.5) | copy-done | bytes 131096
  2.4 0.8 %copy-done.10 = f32[512,16]{0,1:T(8,128)S(1)} copy-done((f32[512,16]{0,1:T(8,128)S(1)}, f32[512,16]{0,1:T(8,128)}, u32[]{:S(2)}) %copy-start.10) | copy-done | bytes 32792
  3.7 1.0 %constant_dynamic-update-slice_fusion.1 = bf16[256,1024]{1,0:T(8,128)(2,1)S(1)} fusion(bf16[128,1024]{1,0:T(8,128)(2,1)} %key_ref.5), kind=kLoop, calls=%fused_computation.2 | loop fusion | bytes 524288
  5.6 11.5 %all-to-all-start = ((bf16[32,32,128]{2,1,0:T(8,128)(2,1)}), bf16[32,32,128]{2,1,0:T(8,128)(2,1)S(1)}, u32[]{:S(2)}, u32[]{:S(2)}) async-start(bf16[32,32,128]{2,1,0:T(8,128)(2,1)} %chip_states.1), calls=%async_computation | async-start | bytes 524288 | tf_op jit(solution)/shard_map/all_to_all | solution.py:262
  17.1 1.0 %constant_dynamic-update-slice_fusion = bf16[256,1024]{1,0:T(8,128)(2,1)S(1)} fusion(bf16[256,1024]{1,0:T(8,128)(2,1)S(1)} %constant_dynamic-update-slice_fusion.1, bf16[128,1024]{1,0:T(8,128)(2,1)} %value_ref.5), kind=kLoop, calls=%fused_computation.1 | loop fusion | bytes 524288 | tf_op jit(solution)/shard_map/concatenate | solution.py:238
  18.1 1.9 %collective-permute-start.6 = (bf16[256,1024]{1,0:T(8,128)(2,1)S(1)}, bf16[256,1024]{1,0:T(8,128)(2,1)S(1)}, u32[]{:S(2)}, u32[]{:S(2)}) collective-permute-start(bf16[256,1024]{1,0:T(8,128)(2,1)S(1)} %constant_dynamic-update-slice_fusion), channel_id=1, source_target_pairs={{0,8},{4,12},{8,16},{12,20},{16,24},{20,28},{24,32},{28,36},{32,40... | collective-permute-start | bytes 1572872 | tf_op jit(solution)/shard_map/ppermute | solution.py:22
  19.9 10.9 %all-to-all-done.refs_0_ = bf16[32,32,128]{2,1,0:T(8,128)(2,1)S(1)} async-done(((bf16[32,32,128]{2,1,0:T(8,128)(2,1)}), bf16[32,32,128]{2,1,0:T(8,128)(2,1)S(1)}, u32[]{:S(2)}, u32[]{:S(2)}) %all-to-all-start) | async-done | bytes 262176 | tf_op jit(solution)/shard_map/all_to_all | solution.py:262
  31.1 1.2 %collective-permute-done.1.other_ref = f32[32,128]{1,0:T(8,128)S(1)} collective-permute-done((f32[32,128]{1,0:T(8,128)S(1)}, f32[32,128]{1,0:T(8,128)S(1)}, u32[]{:S(2)}, u32[]{:S(2)}) %collective-permute-start.1) | collective-permute-done | bytes 16416 | tf_op jit(solution)/shard_map/ppermute | solution.py:27
  32.3 2.2 %copy-done = bf16[512,4096]{1,0:T(8,128)(2,1)S(1)} copy-done((bf16[512,4096]{1,0:T(8,128)(2,1)S(1)}, bf16[512,4096]{1,0:T(8,128)(2,1)}, u32[]{:S(2)}) %copy-start) | copy-done | bytes 4194328
  34.4 0.9 %copy-done.4 = bf16[128,512]{1,0:T(8,128)(2,1)S(1)} copy-done((bf16[128,512]{1,0:T(8,128)(2,1)S(1)}, bf16[128,512]{1,0:T(8,128)(2,1)}, u32[]{:S(2)}) %copy-start.4) | copy-done | bytes 131096
  35.4 0.9 %copy-done.6 = bf16[128,512]{1,0:T(8,128)(2,1)S(1)} copy-done((bf16[128,512]{1,0:T(8,128)(2,1)S(1)}, bf16[128,512]{1,0:T(8,128)(2,1)}, u32[]{:S(2)}) %copy-start.6) | copy-done | bytes 131096
  36.3 0.9 %copy-done.8 = bf16[128,512]{1,0:T(8,128)(2,1)S(1)} copy-done((bf16[128,512]{1,0:T(8,128)(2,1)S(1)}, bf16[128,512]{1,0:T(8,128)(2,1)}, u32[]{:S(2)}) %copy-start.8) | copy-done | bytes 131096
  38.6 2.6 %project.1 = (f32[128,1024]{1,0:T(8,128)S(1)}, bf16[128,1024]{1,0:T(8,128)(2,1)S(1)}, bf16[128,1024]{1,0:T(8,128)(2,1)S(1)}, bf16[128,1024]{1,0:T(8,128)(2,1)S(1)}) custom-call(bf16[128,512]{1,0:T(8,128)(2,1)S(1)} %copy-done.8, bf16[128,512]{1,0:T(8,128)(2,1)S(1)} %copy-done.4, bf16[128,512]{1,0:T(8,128)(2,1)S(1)} %copy-done.6, ...), custom_call_target="tpu_custom_call" | custom-call | tf_op jit(solution)/shard_map/project/pallas_call | solution.py:275
  41.8 1.5 %collective-permute-start.3 = (bf16[128,1024]{1,0:T(8,128)(2,1)S(1)}, bf16[128,1024]{1,0:T(8,128)(2,1)S(1)}, u32[]{:S(2)}, u32[]{:S(2)}) collective-permute-start(bf16[128,1024]{1,0:T(8,128)(2,1)S(1)} %get-tuple-element.18), channel_id=1, source_target_pairs={{0,1},{1,2},{2,3},{3,0},{4,5},{5,6},{6,7},{7,4},{8,9},{9,10},{10,1... | collective-permute-start | bytes 786440 | tf_op jit(solution)/shard_map/ppermute | solution.py:22
  43.3 3.3 %collective-permute-start.2 = (bf16[128,1024]{1,0:T(8,128)(2,1)S(1)}, bf16[128,1024]{1,0:T(8,128)(2,1)S(1)}, u32[]{:S(2)}, u32[]{:S(2)}) collective-permute-start(bf16[128,1024]{1,0:T(8,128)(2,1)S(1)} %get-tuple-element.17), channel_id=1, source_target_pairs={{0,2},{1,3},{2,0},{3,1},{4,6},{5,7},{6,4},{7,5},{8,10},{9,11},{10,... | collective-permute-start | bytes 786440 | tf_op jit(solution)/shard_map/ppermute | solution.py:22
  46.7 0.9 %collective-permute-start.7 = (bf16[256,1024]{1,0:T(8,128)(2,1)S(1)}, bf16[256,1024]{1,0:T(8,128)(2,1)S(1)}, u32[]{:S(2)}, u32[]{:S(2)}) collective-permute-start(bf16[256,1024]{1,0:T(8,128)(2,1)S(1)} %collective-permute-done.6.two_ref), channel_id=1, source_target_pairs={{0,4},{4,8},{8,12},{12,16},{16,20},{20,24},{24,28},{28,32},{32,36}... | collective-permute-start | bytes 1572872 | tf_op jit(solution)/shard_map/ppermute | solution.py:22
  47.6 2.1 %collective-permute-done.4 = bf16[128,1024]{1,0:T(8,128)(2,1)S(1)} collective-permute-done((bf16[128,1024]{1,0:T(8,128)(2,1)S(1)}, bf16[128,1024]{1,0:T(8,128)(2,1)S(1)}, u32[]{:S(2)}, u32[]{:S(2)}) %collective-permute-start.4) | collective-permute-done | bytes 262176 | tf_op jit(solution)/shard_map/ppermute | solution.py:22
  49.7 2.0 %collective-permute-done.3 = bf16[128,1024]{1,0:T(8,128)(2,1)S(1)} collective-permute-done((bf16[128,1024]{1,0:T(8,128)(2,1)S(1)}, bf16[128,1024]{1,0:T(8,128)(2,1)S(1)}, u32[]{:S(2)}, u32[]{:S(2)}) %collective-permute-start.3) | collective-permute-done | bytes 262176 | tf_op jit(solution)/shard_map/ppermute | solution.py:22
  51.7 4.5 %collective-permute-done.2 = bf16[128,1024]{1,0:T(8,128)(2,1)S(1)} collective-permute-done((bf16[128,1024]{1,0:T(8,128)(2,1)S(1)}, bf16[128,1024]{1,0:T(8,128)(2,1)S(1)}, u32[]{:S(2)}, u32[]{:S(2)}) %collective-permute-start.2) | collective-permute-done | bytes 262176 | tf_op jit(solution)/shard_map/ppermute | solution.py:22
  56.2 0.9 %add_convert_fusion = bf16[128,1024]{1,0:T(8,128)(2,1)} fusion(bf16[128,1024]{1,0:T(8,128)(2,1)S(1)} %collective-permute-done.4, bf16[128,1024]{1,0:T(8,128)(2,1)S(1)} %collective-permute-done.3, f32[128,1024]{1,0:T(8,128)S(1)} %get-tuple-element.16, bf16[128,1024]{1,0:T(8,128)(2,1)S(1)} %collective-permute-done.2, bf16[128,1024]{1,0:T(8,128)(2,1)S(1)} %copy-done.14), kind=kLoop, calls=%fused_computation | loop fusion | flops 1179648 | bytes 1835008 | tf_op jit(solution)/shard_map/convert_element_type | solution.py:323
  57.1 1.5 %collective-permute-done.5.one_ref = bf16[256,1024]{1,0:T(8,128)(2,1)S(1)} collective-permute-done((bf16[256,1024]{1,0:T(8,128)(2,1)S(1)}, bf16[256,1024]{1,0:T(8,128)(2,1)S(1)}, u32[]{:S(2)}, u32[]{:S(2)}) %collective-permute-start.5) | collective-permute-done | bytes 524320 | tf_op jit(solution)/shard_map/ppermute | solution.py:22
  58.6 5.6 %collective-permute-done.7.three_ref = bf16[256,1024]{1,0:T(8,128)(2,1)S(1)} collective-permute-done((bf16[256,1024]{1,0:T(8,128)(2,1)S(1)}, bf16[256,1024]{1,0:T(8,128)(2,1)S(1)}, u32[]{:S(2)}, u32[]{:S(2)}) %collective-permute-start.7) | collective-permute-done | bytes 524320 | tf_op jit(solution)/shard_map/ppermute | solution.py:22
  64.2 3.5 %attention.1 = bf16[128,1024]{1,0:T(8,128)(2,1)} custom-call(bf16[128,1024]{1,0:T(8,128)(2,1)S(1)} %copy-done.7, bf16[128,1024]{1,0:T(8,128)(2,1)S(1)} %copy-done.1, bf16[128,1024]{1,0:T(8,128)(2,1)S(1)} %copy-done.2, bf16[256,1024]{1,0:T(8,128)(2,1)S(1)} %collective-permute-done.5.one_ref, bf16[256,1024]{1,0:T(8,128)(2,1)S(1)} %collective-permute-done.6.two_ref, ...), custom_call_target="tpu_custom_call" | custom-call | tf_op jit(solution)/shard_map/attention/pallas_call | solution.py:305
  (32 shorter events, 3.6 us)
Async XLA Ops:
  0.6 0.9 %copy-start.3 = (bf16[128,512]{1,0:T(8,128)(2,1)S(1)}, bf16[128,512]{1,0:T(8,128)(2,1)}, u32[]{:S(2)}) copy-start(bf16[128,512]{1,0:T(8,128)(2,1)} %key_ref.4) | copy-start | bytes 393220
  1.5 0.9 %copy-start.5 = (bf16[128,512]{1,0:T(8,128)(2,1)S(1)}, bf16[128,512]{1,0:T(8,128)(2,1)}, u32[]{:S(2)}) copy-start(bf16[128,512]{1,0:T(8,128)(2,1)} %value_ref.4) | copy-start | bytes 393220
  2.4 0.8 %copy-start.10 = (f32[512,16]{0,1:T(8,128)S(1)}, f32[512,16]{0,1:T(8,128)}, u32[]{:S(2)}) copy-start(f32[512,16]{0,1:T(8,128)} %param.16) | copy-start | bytes 98308
  3.2 53.0 %copy-start.14 = (bf16[128,1024]{1,0:T(8,128)(2,1)S(1)}, bf16[128,1024]{1,0:T(8,128)(2,1)}, u32[]{:S(2)}) copy-start(bf16[128,1024]{1,0:T(8,128)(2,1)} %param.20) | copy-start | bytes 786436
  3.6 1.3 %collective-permute-start = (f32[32,128]{1,0:T(8,128)S(1)}, f32[32,128]{1,0:T(8,128)S(1)}, u32[]{:S(2)}, u32[]{:S(2)}) collective-permute-start(f32[32,128]{1,0:T(8,128)S(1)} %get-tuple-element.13), channel_id=1, source_target_pairs={{0,4},{4,0},{8,12},{12,8},{16,20},{20,16},{24,28},{28,24},{32,36},... | collective-permute-start | bytes 49160 | tf_op jit(solution)/shard_map/ppermute | solution.py:27
  4.7 59.5 %copy-start.1 = (bf16[128,1024]{1,0:T(8,128)(2,1)S(1)}, bf16[128,1024]{1,0:T(8,128)(2,1)}, u32[]{:S(2)}) copy-start(bf16[128,1024]{1,0:T(8,128)(2,1)} %key_ref.5) | copy-start | bytes 786436
  4.7 59.5 %copy-start.2 = (bf16[128,1024]{1,0:T(8,128)(2,1)S(1)}, bf16[128,1024]{1,0:T(8,128)(2,1)}, u32[]{:S(2)}) copy-start(bf16[128,1024]{1,0:T(8,128)(2,1)} %value_ref.5) | copy-start | bytes 786436
  4.7 59.5 %copy-start.7 = (bf16[128,1024]{1,0:T(8,128)(2,1)S(1)}, bf16[128,1024]{1,0:T(8,128)(2,1)}, u32[]{:S(2)}) copy-start(bf16[128,1024]{1,0:T(8,128)(2,1)} %query_ref.3) | copy-start | bytes 786436
  4.7 59.5 %copy-start.12 = (s32[128]{0:T(128)S(1)}, s32[128]{0:T(128)}, u32[]{:S(2)}) copy-start(s32[128]{0:T(128)} %param.24) | copy-start | bytes 1540
  4.7 59.5 %copy-start.13 = (s32[1,4]{1,0:T(1,128)S(1)}, s32[1,4]{1,0:T(1,128)}, u32[]{:S(2)}) copy-start(s32[1,4]{1,0:T(1,128)} %read_ref.1) | copy-start | bytes 52
  5.6 25.3 %all-to-all-start = ((bf16[32,32,128]{2,1,0:T(8,128)(2,1)}), bf16[32,32,128]{2,1,0:T(8,128)(2,1)S(1)}, u32[]{:S(2)}, u32[]{:S(2)}) async-start(bf16[32,32,128]{2,1,0:T(8,128)(2,1)} %chip_states.1), calls=%async_computation | async-start | bytes 524288 | tf_op jit(solution)/shard_map/all_to_all | solution.py:262
  18.1 28.6 %collective-permute-start.6 = (bf16[256,1024]{1,0:T(8,128)(2,1)S(1)}, bf16[256,1024]{1,0:T(8,128)(2,1)S(1)}, u32[]{:S(2)}, u32[]{:S(2)}) collective-permute-start(bf16[256,1024]{1,0:T(8,128)(2,1)S(1)} %constant_dynamic-update-slice_fusion), channel_id=1, source_target_pairs={{0,8},{4,12},{8,16},{12,20},{16,24},{20,28},{24,32},{28,36},{32,40... | collective-permute-start | bytes 1572872 | tf_op jit(solution)/shard_map/ppermute | solution.py:22
  31.0 1.3 %collective-permute-start.1 = (f32[32,128]{1,0:T(8,128)S(1)}, f32[32,128]{1,0:T(8,128)S(1)}, u32[]{:S(2)}, u32[]{:S(2)}) collective-permute-start(f32[32,128]{1,0:T(8,128)S(1)} %get-tuple-element.15), channel_id=1, source_target_pairs={{0,4},{4,0},{8,12},{12,8},{16,20},{20,16},{24,28},{28,24},{32,36},... | collective-permute-start | bytes 49160 | tf_op jit(solution)/shard_map/ppermute | solution.py:27
  32.3 2.2 %copy-start = (bf16[512,4096]{1,0:T(8,128)(2,1)S(1)}, bf16[512,4096]{1,0:T(8,128)(2,1)}, u32[]{:S(2)}) copy-start(bf16[512,4096]{1,0:T(8,128)(2,1)} %weight_hbm.1) | copy-start | bytes 12582916
  34.4 0.9 %copy-start.4 = (bf16[128,512]{1,0:T(8,128)(2,1)S(1)}, bf16[128,512]{1,0:T(8,128)(2,1)}, u32[]{:S(2)}) copy-start(bf16[128,512]{1,0:T(8,128)(2,1)} %key_ref.4) | copy-start | bytes 393220
  35.3 0.9 %copy-start.6 = (bf16[128,512]{1,0:T(8,128)(2,1)S(1)}, bf16[128,512]{1,0:T(8,128)(2,1)}, u32[]{:S(2)}) copy-start(bf16[128,512]{1,0:T(8,128)(2,1)} %value_ref.4) | copy-start | bytes 393220
  36.3 0.9 %copy-start.8 = (bf16[128,512]{1,0:T(8,128)(2,1)S(1)}, bf16[128,512]{1,0:T(8,128)(2,1)}, u32[]{:S(2)}) copy-start(bf16[128,512]{1,0:T(8,128)(2,1)} %query_ref.2) | copy-start | bytes 393220
  37.2 0.8 %copy-start.9 = (f32[512,16]{0,1:T(8,128)S(1)}, f32[512,16]{0,1:T(8,128)}, u32[]{:S(2)}) copy-start(f32[512,16]{0,1:T(8,128)} %param.17) | copy-start | bytes 98308
  37.9 0.7 %copy-start.11 = (f32[512]{0:T(512)S(1)}, f32[512]{0:T(512)}, u32[]{:S(2)}) copy-start(f32[512]{0:T(512)} %param.18) | copy-start | bytes 6148
  41.2 8.5 %collective-permute-start.4 = (bf16[128,1024]{1,0:T(8,128)(2,1)S(1)}, bf16[128,1024]{1,0:T(8,128)(2,1)S(1)}, u32[]{:S(2)}, u32[]{:S(2)}) collective-permute-start(bf16[128,1024]{1,0:T(8,128)(2,1)S(1)} %get-tuple-element.19), channel_id=1, source_target_pairs={{0,3},{1,0},{2,1},{3,2},{4,7},{5,4},{6,5},{7,6},{8,11},{9,8},{10,9... | collective-permute-start | bytes 786440 | tf_op jit(solution)/shard_map/ppermute | solution.py:22
  41.8 9.9 %collective-permute-start.3 = (bf16[128,1024]{1,0:T(8,128)(2,1)S(1)}, bf16[128,1024]{1,0:T(8,128)(2,1)S(1)}, u32[]{:S(2)}, u32[]{:S(2)}) collective-permute-start(bf16[128,1024]{1,0:T(8,128)(2,1)S(1)} %get-tuple-element.18), channel_id=1, source_target_pairs={{0,1},{1,2},{2,3},{3,0},{4,5},{5,6},{6,7},{7,4},{8,9},{9,10},{10,1... | collective-permute-start | bytes 786440 | tf_op jit(solution)/shard_map/ppermute | solution.py:22
  43.3 12.9 %collective-permute-start.2 = (bf16[128,1024]{1,0:T(8,128)(2,1)S(1)}, bf16[128,1024]{1,0:T(8,128)(2,1)S(1)}, u32[]{:S(2)}, u32[]{:S(2)}) collective-permute-start(bf16[128,1024]{1,0:T(8,128)(2,1)S(1)} %get-tuple-element.17), channel_id=1, source_target_pairs={{0,2},{1,3},{2,0},{3,1},{4,6},{5,7},{6,4},{7,5},{8,10},{9,11},{10,... | collective-permute-start | bytes 786440 | tf_op jit(solution)/shard_map/ppermute | solution.py:22
  46.6 11.9 %collective-permute-start.5 = (bf16[256,1024]{1,0:T(8,128)(2,1)S(1)}, bf16[256,1024]{1,0:T(8,128)(2,1)S(1)}, u32[]{:S(2)}, u32[]{:S(2)}) collective-permute-start(bf16[256,1024]{1,0:T(8,128)(2,1)S(1)} %constant_dynamic-update-slice_fusion), channel_id=1, source_target_pairs={{0,4},{4,8},{8,12},{12,16},{16,20},{20,24},{24,28},{28,32},{32,36}... | collective-permute-start | bytes 1572872 | tf_op jit(solution)/shard_map/ppermute | solution.py:22
  46.7 17.5 %collective-permute-start.7 = (bf16[256,1024]{1,0:T(8,128)(2,1)S(1)}, bf16[256,1024]{1,0:T(8,128)(2,1)S(1)}, u32[]{:S(2)}, u32[]{:S(2)}) collective-permute-start(bf16[256,1024]{1,0:T(8,128)(2,1)S(1)} %collective-permute-done.6.two_ref), channel_id=1, source_target_pairs={{0,4},{4,8},{8,12},{12,16},{16,20},{20,24},{24,28},{28,32},{32,36}... | collective-permute-start | bytes 1572872 | tf_op jit(solution)/shard_map/ppermute | solution.py:22

commit v2 on v1

v2 whole, which is shorter than its diff:
```python
import math

import jax
import jax.numpy as jnp
from jax import lax
from jax.experimental import pallas as pl
from jax.experimental.pallas import tpu as pltpu
from jax.sharding import PartitionSpec as P

HD = 128
LANES = 128
DOC_BLOCKS = 3
VMEM = pltpu.VMEM


def whole(count):
    return [pl.BlockSpec(memory_space=VMEM) for _ in range(count)]


def in_hbm(count):
    return [pl.BlockSpec(memory_space=pltpu.HBM) for _ in range(count)]


def fixed(*values):
    return [pltpu.with_memory_space_constraint(value, pltpu.HBM) for value in values]


def shifted(value, axis, steps):
    count = lax.axis_size(axis)
    return lax.ppermute(value, axis, [(i, (i + steps) % count) for i in range(count)])


def core_swap(value):
    count = lax.axis_size("ctx")
    return lax.ppermute(value, "ctx", [(i, i ^ 1) for i in range(count)])


def room(mib):
    return pltpu.CompilerParams(vmem_limit_bytes=mib * 1024 * 1024)


def to_state_rows(source_ref, target_ref, groups):
    for g in range(groups):
        block = source_ref[:, g * LANES : (g + 1) * LANES]
        target_ref[pl.ds(g, block.shape[0], stride=groups), :] = block


def to_position_rows(product, target_ref, groups):
    rows = product.shape[0]
    for g in range(groups):
        block = product[:, g * LANES : (g + 1) * LANES]
        for half in range(2):
            target_ref[pl.ds(half * groups + g, rows, stride=2 * groups), :] = block


def load(pairs, sems):
    copies = [
        pltpu.make_async_copy(source, target, sems.at[i])
        for i, (source, target) in enumerate(pairs)
    ]
    for copy in copies:
        copy.start()
    return copies


def half_rows(ref, part):
    half = ref.shape[0] // 2
    return ref[pl.ds(pl.multiple_of(part * half, half), half), :]


def states_kernel(
    key_hbm,
    value_hbm,
    decay_hbm,
    attn_key_hbm,
    attn_value_hbm,
    keep_ref,
    send_ref,
    rates_ref,
    block_ref,
    key_ref,
    value_ref,
    decay_ref,
    product_ref,
    all_rates_ref,
    state_ref,
    sems,
):
    copies = load(
        [
            (decay_hbm, decay_ref),
            (key_hbm, key_ref),
            (value_hbm, value_ref),
            (attn_key_hbm, block_ref.at[: attn_key_hbm.shape[0]]),
            (attn_value_hbm, block_ref.at[attn_key_hbm.shape[0] :]),
        ],
        sems,
    )
    groups = key_ref.shape[1] // LANES
    rows = key_ref.shape[0]
    copies[0].wait()
    to_state_rows(decay_ref, all_rates_ref, groups)
    count = all_rates_ref.shape[0] // 8
    steps = [jnp.exp(-all_rates_ref[8 * i : 8 * i + 8, :]) for i in range(count)]
    copies[1].wait()
    copies[2].wait()
    product = key_ref[...].astype(jnp.float32) * value_ref[...].astype(jnp.float32)
    to_position_rows(product, product_ref, groups)
    parts = 4
    span = rows // parts
    states = [[jnp.zeros((8, LANES), jnp.float32)] * count for _ in range(parts)]
    for t in range(span):
        for part in range(parts):
            row = 8 * (part * span + t)
            value = product_ref[row : row + 8, :]
            states[part] = [s * a + value for s, a in zip(states[part], steps)]
    for i in range(count):
        long_step = jnp.exp(-span * all_rates_ref[8 * i : 8 * i + 8, :])
        total = states[0][i]
        for part in range(1, parts):
            total = total * long_step + states[part][i]
        state_ref[8 * i : 8 * i + 8, :] = total
    core = lax.rem(lax.axis_index("ctx"), 2)
    keep_ref[...] = half_rows(state_ref, core)
    send_ref[...] = half_rows(state_ref, 1 - core)
    rates_ref[...] = half_rows(all_rates_ref, core)
    copies[3].wait()
    copies[4].wait()


def carry_kernel(rows, all_ref, keep_ref, got_ref, rates_ref, *refs):
    mine_ref, other_ref = refs[-2:]
    index = lax.axis_index("ctx")
    core = lax.rem(index, 2)
    chip = lax.div(index, 2)
    half = keep_ref.shape[0]
    rates = rates_ref[...]
    step = jnp.exp(-2 * rows * rates)
    carry = jnp.zeros((half, LANES), jnp.float32)
    for i in range(all_ref.shape[0] - 1):
        carry = jnp.where(i < chip, carry * step + all_ref[i].astype(jnp.float32), carry)
    first = jnp.where(core == 0, keep_ref[...], got_ref[...])
    later = carry * jnp.exp(-rows * rates) + first
    mine_ref[...] = jnp.where(core == 0, carry, later)
    other_ref[...] = jnp.where(core == 0, later, carry)


def local_kernel(
    after_ref,
    key_hbm,
    value_hbm,
    decay_hbm,
    residue_hbm,
    query_hbm,
    skip_hbm,
    weight_hbm,
    query_ref,
    base_ref,
    steps_ref,
    scale_ref,
    far_ref,
    near_ref,
    key_ref,
    value_ref,
    decay_ref,
    residue_ref,
    skip_ref,
    product_ref,
    conv_ref,
    sems,
):
    copies = load(
        [
            (decay_hbm, decay_ref),
            (residue_hbm, residue_ref),
            (key_hbm, key_ref),
            (value_hbm, value_ref),
            (query_hbm, query_ref),
            (skip_hbm, skip_ref),
            *weight_pairs(weight_hbm, 2, far_ref),
            *weight_pairs(weight_hbm, 1, near_ref),
        ],
        sems,
    )
    for copy in copies[:-8]:
        copy.wait()
    groups = key_ref.shape[1] // LANES
    rows = key_ref.shape[0]
    to_state_rows(decay_ref, steps_ref, groups)
    to_state_rows(residue_ref, scale_ref, groups)
    steps_ref[...] = jnp.exp(-steps_ref[...])
    product = key_ref[...].astype(jnp.float32) * value_ref[...].astype(jnp.float32)
    to_position_rows(product, product_ref, groups)
    count = steps_ref.shape[0] // 8
    steps = [steps_ref[8 * i : 8 * i + 8, :] for i in range(count)]
    scale = [scale_ref[8 * i : 8 * i + 8, :] for i in range(count)]
    states = [jnp.zeros((8, LANES), jnp.float32)] * count
    for t in range(rows):
        value = product_ref[8 * t : 8 * t + 8, :]
        states = [s * a + value for s, a in zip(states, steps)]
        conv_ref[8 * t : 8 * t + 8, :] = tree_sum([s * w for s, w in zip(states, scale)])
    for g in range(groups):
        lanes = slice(g * LANES, (g + 1) * LANES)
        base_ref[:, lanes] = (
            from_position_rows(conv_ref, g, groups) + skip_ref[:, lanes] * product[:, lanes]
        )
    for copy in copies[-8:]:
        copy.wait()


def tree_sum(terms):
    while len(terms) > 1:
        terms = [u + v for u, v in zip(terms[::2], terms[1::2])]
    return terms[0]


def from_position_rows(source_ref, g, groups):
    rows = source_ref.shape[0] // (2 * groups)
    return (
        source_ref[pl.ds(g, rows, stride=2 * groups), :]
        + source_ref[pl.ds(groups + g, rows, stride=2 * groups), :]
    )


def gate_kernel(
    query_ref,
    base_ref,
    steps_ref,
    scale_ref,
    mine_ref,
    other_ref,
    far_weight_ref,
    near_weight_ref,
    weight_hbm,
    hyena_ref,
    far_ref,
    near_ref,
    back_ref,
    state_ref,
    conv_ref,
    back_weight_ref,
    sems,
):
    copies = load(weight_pairs(weight_hbm, 3, back_weight_ref), sems)
    rows = query_ref.shape[0]
    groups = query_ref.shape[1] // LANES
    core = lax.rem(lax.axis_index("ctx"), 2)
    half = mine_ref.shape[0]
    state_ref[pl.ds(pl.multiple_of(core * half, half), half), :] = mine_ref[...]
    state_ref[pl.ds(pl.multiple_of((1 - core) * half, half), half), :] = other_ref[...]
    count = steps_ref.shape[0] // 8
    steps = [steps_ref[8 * i : 8 * i + 8, :] for i in range(count)]
    states = [
        state_ref[8 * i : 8 * i + 8, :] * scale_ref[8 * i : 8 * i + 8, :] for i in range(count)
    ]
    for t in range(rows):
        states = [s * a for s, a in zip(states, steps)]
        conv_ref[8 * t : 8 * t + 8, :] = tree_sum(states)
    for g in range(groups):
        lanes = slice(g * LANES, (g + 1) * LANES)
        conv = from_position_rows(conv_ref, g, groups) + base_ref[:, lanes]
        hyena_ref[:, lanes] = (query_ref[:, lanes].astype(jnp.float32) * conv).astype(
            hyena_ref.dtype
        )
    pairs = ((far_weight_ref, far_ref), (near_weight_ref, near_ref), (back_weight_ref, back_ref))
    for weight_ref, target in pairs:
        if target is back_ref:
            for copy in copies:
                copy.wait()
        target[...] = jnp.dot(
            hyena_ref[...], weight_ref[...], preferred_element_type=jnp.float32
        ).astype(target.dtype)


def weight_pairs(weight_hbm, ahead, target_ref):
    source = weight_columns(weight_hbm, ahead, target_ref.shape[1])
    quarter = target_ref.shape[0] // 4
    rows = [slice(i * quarter, (i + 1) * quarter) for i in range(4)]
    return [(source.at[part, :], target_ref.at[part, :]) for part in rows]


def weight_columns(weight_hbm, ahead, width):
    chan, chans = lax.axis_index("chan"), weight_hbm.shape[1] // width
    column = pl.multiple_of(lax.rem(chan + ahead, chans) * width, width)
    return weight_hbm.at[:, pl.ds(column, width)]


def own_kernel(hyena_ref, weight_hbm, stream_hbm, own_ref, weight_ref, stream_ref, sems):
    copies = load(
        [*weight_pairs(weight_hbm, 0, weight_ref), (stream_hbm, stream_ref)],
        sems,
    )
    for copy in copies:
        copy.wait()
    own_ref[...] = stream_ref[...].astype(jnp.float32) + jnp.dot(
        hyena_ref[...], weight_ref[...], preferred_element_type=jnp.float32
    )


def finish_kernel(own_ref, far_ref, near_ref, back_ref, after_ref, out_ref):
    total = own_ref[...]
    for ref in (far_ref, near_ref, back_ref):
        total = total + ref[...].astype(jnp.float32)
    out_ref[...] = total.astype(out_ref.dtype)


def attention_kernel(
    query_hbm,
    block_hbm,
    one_hbm,
    two_hbm,
    three_hbm,
    start_ref,
    read_ref,
    out_ref,
    query_ref,
    block_ref,
    one_ref,
    two_ref,
    three_ref,
    sems,
):
    copies = load(
        [
            (query_hbm, query_ref),
            (block_hbm, block_ref),
            (one_hbm, one_ref),
            (two_hbm, two_ref),
            (three_hbm, three_ref),
        ],
        sems,
    )
    rows = query_ref.shape[0]
    base = lax.axis_index("ctx") * rows
    starts = jnp.broadcast_to(start_ref[...] - base, (rows, rows)).T
    query_pos = lax.broadcasted_iota(jnp.int32, (rows, rows), 0)
    key_pos = lax.broadcasted_iota(jnp.int32, (rows, rows), 1)
    allowed = []
    for back in range(DOC_BLOCKS, -1, -1):
        pos = key_pos - back * rows
        ok = (pos >= starts) & (read_ref[0, back] == 1)
        if back == 0:
            ok = ok & (pos <= query_pos)
        allowed.append(ok)
    mask = jnp.concatenate(allowed, axis=1)
    for copy in copies:
        copy.wait()
    for head in range(query_ref.shape[1] // HD):
        cols = slice(head * HD, (head + 1) * HD)
        query = query_ref[:, cols]
        blocks = (three_ref, two_ref, one_ref, block_ref)
        keys = jnp.concatenate([ref[:rows, cols] for ref in blocks], axis=0)
        values = jnp.concatenate([ref[rows:, cols] for ref in blocks], axis=0)
        scores = lax.dot_general(
            query, keys, (((1,), (1,)), ((), ())), preferred_element_type=jnp.float32
        )
        scores = jnp.where(mask, scores * HD ** (-0.5), -jnp.inf)
        top = jnp.max(scores, axis=1, keepdims=True)
        weights = jnp.exp(scores - top)
        total = jnp.sum(weights, axis=1, keepdims=True)
        summed = jnp.dot(weights.astype(jnp.bfloat16), values, preferred_element_type=jnp.float32)
        out_ref[:, cols] = (summed / total).astype(out_ref.dtype)


def shards(
    query_feat,
    key_feat,
    value_feat,
    decay_rate,
    residue,
    conv_skip,
    out_weight,
    stream,
    attn_query,
    attn_key,
    attn_value,
    doc_start,
    read_mask,
):
    rows, channels = query_feat.shape
    order = decay_rate.shape[1]
    state_rows = order * channels // LANES
    f32, bf16 = jnp.float32, jnp.bfloat16
    ctx_count = lax.axis_size("ctx")
    core = lax.axis_index("ctx") % 2
    half = state_rows // 2
    state = jax.ShapeDtypeStruct((state_rows, LANES), f32)
    state_half = jax.ShapeDtypeStruct((half, LANES), f32)

    keep, send, rates, block = pl.pallas_call(
        states_kernel,
        out_shape=(
            state_half,
            state_half,
            state_half,
            jax.ShapeDtypeStruct((2 * rows, attn_key.shape[1]), bf16),
        ),
        in_specs=in_hbm(5),
        out_specs=tuple(whole(4)),
        scratch_shapes=[
            VMEM((rows, channels), bf16),
            VMEM((rows, channels), bf16),
            VMEM((order, channels), f32),
            VMEM((8 * rows, LANES), f32),
            VMEM((state_rows, LANES), f32),
            VMEM((state_rows, LANES), f32),
            pltpu.SemaphoreType.DMA((5,)),
        ],
        compiler_params=room(4),
        name="filter_states",
    )(*fixed(key_feat, value_feat, decay_rate.T, attn_key, attn_value))
    block_2 = shifted(block, "ctx", 2)
    block_3 = shifted(block_2, "ctx", 1)
    block_1 = core_swap(jnp.where(core == 0, block, block_2))
    got = core_swap(send)
    first = jnp.where(core == 0, keep, got)
    second = jnp.where(core == 0, got, keep)
    both = (first * jnp.exp(-rows * rates) + second).astype(bf16)
    groups = [list(range(c, ctx_count, 2)) for c in range(2)]
    spread = lax.all_to_all(
        jnp.broadcast_to(both, (ctx_count // 2, half, LANES)),
        "ctx",
        0,
        0,
        axis_index_groups=groups,
    )

    width = out_weight.shape[1] // lax.axis_size("chan")
    columns = jax.ShapeDtypeStruct((channels, width), bf16)
    query, base, steps, scale, *weights = pl.pallas_call(
        local_kernel,
        out_shape=(
            jax.ShapeDtypeStruct((rows, channels), bf16),
            jax.ShapeDtypeStruct((rows, channels), f32),
            state,
            state,
            columns,
            columns,
        ),
        in_specs=whole(1) + in_hbm(7),
        out_specs=tuple(whole(6)),
        scratch_shapes=[
            VMEM((rows, channels), bf16),
            VMEM((rows, channels), bf16),
            VMEM((order, channels), f32),
            VMEM((order, channels), f32),
            VMEM((1, channels), f32),
            VMEM((8 * rows, LANES), f32),
            VMEM((8 * rows, LANES), f32),
            pltpu.SemaphoreType.DMA((14,)),
        ],
        compiler_params=room(6),
        cost_estimate=pl.CostEstimate(flops=0, bytes_accessed=8 * 1024 * 1024, transcendentals=0),
        name="local_part",
    )(
        got,
        *fixed(
            key_feat,
            value_feat,
            decay_rate.T,
            residue.T,
            query_feat,
            conv_skip.reshape(1, channels),
            out_weight,
        ),
    )
    mine, other = pl.pallas_call(
        lambda *refs: carry_kernel(rows, *refs),
        out_shape=(state_half, state_half),
        in_specs=whole(4) + [pl.BlockSpec(memory_space=pl.ANY)],
        out_specs=tuple(whole(2)),
        compiler_params=room(4),
        name="carried_states",
    )(spread, keep, got, rates, steps)
    other = core_swap(other)

    piece = jax.ShapeDtypeStruct((rows, width), bf16)
    hyena, far, near, back = pl.pallas_call(
        gate_kernel,
        out_shape=(jax.ShapeDtypeStruct((rows, channels), bf16), piece, piece, piece),
        in_specs=whole(8) + in_hbm(1),
        out_specs=tuple(whole(4)),
        scratch_shapes=[
            VMEM((state_rows, LANES), f32),
            VMEM((8 * rows, LANES), f32),
            VMEM((channels, width), bf16),
            pltpu.SemaphoreType.DMA((4,)),
        ],
        compiler_params=room(4),
        name="gate",
    )(query, base, steps, scale, mine, other, *weights, *fixed(out_weight))
    own = pl.pallas_call(
        own_kernel,
        out_shape=jax.ShapeDtypeStruct((rows, width), f32),
        in_specs=whole(1) + in_hbm(2),
        out_specs=whole(1)[0],
        scratch_shapes=[
            VMEM((channels, width), bf16),
            VMEM((rows, width), bf16),
            pltpu.SemaphoreType.DMA((5,)),
        ],
        compiler_params=room(8),
        name="own",
    )(hyena, *fixed(out_weight, stream))
    far = shifted(far, "chan", 2)
    near = shifted(near, "chan", 1)
    back = shifted(back, "chan", 3)

    attended = pl.pallas_call(
        attention_kernel,
        out_shape=jax.ShapeDtypeStruct(attn_query.shape, bf16),
        in_specs=in_hbm(5) + whole(1) + [pl.BlockSpec(memory_space=pltpu.SMEM)],
        out_specs=whole(1)[0],
        scratch_shapes=[VMEM(attn_query.shape, bf16)]
        + [VMEM((2 * rows, attn_query.shape[1]), bf16)] * 4
        + [pltpu.SemaphoreType.DMA((5,))],
        compiler_params=room(8),
        name="attention",
    )(
        *fixed(attn_query, block, block_1, block_2, block_3),
        doc_start.reshape(1, rows),
        read_mask,
    )
    mixed = pl.pallas_call(
        finish_kernel,
        out_shape=jax.ShapeDtypeStruct(stream.shape, bf16),
        in_specs=whole(4) + [pl.BlockSpec(memory_space=pl.ANY)],
        out_specs=whole(1)[0],
        compiler_params=room(4),
        name="finish",
    )(own, far, near, back, *fixed(attended))
    return (mixed, attended)


def solution(mesh):
    in_specs = (
        P("ctx", "chan"),
        P("ctx", "chan"),
        P("ctx", "chan"),
        P("chan", None),
        P("chan", None),
        P("chan"),
        P("chan", None),
        P("ctx", "chan"),
        P("ctx", "chan"),
        P("ctx", "chan"),
        P("ctx", "chan"),
        P("ctx"),
        P("ctx", None),
    )
    out_specs = (P("ctx", "chan"), P("ctx", "chan"))
    return jax.shard_map(shards, mesh=mesh, in_specs=in_specs, out_specs=out_specs, check_vma=False)
```

time: 68.3 us -> 50.7 us (0.74)
  the two profiles are of different devices: /device:TPU:2 before, /device:TPU:1 now
where the time goes in v2:
time: 50.7 us; the launch traced here: 50.4 us
  starting transfers between devices  23 us (45%)
  Pallas kernels  13.2 us (26%)
  waiting for transfers between devices  10.7 us (21%)
  other arithmetic  1.93 us (4%)
  local copies, waits for them, and re-layouts  0.76 us (1%)
  between operations  0.76 us (1%)
    all_to_all x1, starting transfers between devices, shards(): lax.all_to_all(jnp.broadcast_to(both, (ctx_count // 2, half, LANES)), 'ct...  10.3 us
    ppermute x5, waiting for transfers between devices, shifted(): lax.ppermute(value, axis, [(i, (i + steps) % count) for i in range(count)])  8.38 us
    ppermute x5, starting transfers between devices, shifted(): lax.ppermute(value, axis, [(i, (i + steps) % count) for i in range(count)])  8.05 us
    pallas_call x1, Pallas kernels, shards(): pl.pallas_call(attention_kernel, out_shape=jax.ShapeDtypeStruct(attn_quer...  5.14 us
    ppermute x3, starting transfers between devices, core_swap(): return lax.ppermute(value, 'ctx', [(i, i ^ 1) for i in range(count)])  4.69 us
    pallas_call x1, Pallas kernels, shards(): pl.pallas_call(gate_kernel, out_shape=(jax.ShapeDtypeStruct((rows, channe...  2.16 us
    pallas_call x1, Pallas kernels, shards(): pl.pallas_call(local_kernel, out_shape=(jax.ShapeDtypeStruct((rows, chann...  1.96 us
    select_n x1, other arithmetic, shards(): block_1 = core_swap(jnp.where(core == 0, block, block_2))  1.92 us
  transfers between devices with their start and end apart: 9, of which 5 were waited for; matrix products, arithmetic and copies ran while one was open for 5% of the time, Pallas kernels for 22%

profile of v2, /device:TPU:1, one launch (start us, length us, event | category | flops | bytes accessed | tf_op | source)
XLA Modules:
  0.0 50.4 jit_solution(10268328229536072276)
XLA Ops:
  0.6 1.4 %filter_states.1 = (f32[32,128]{1,0:T(8,128)S(1)}, f32[32,128]{1,0:T(8,128)S(1)}, f32[32,128]{1,0:T(8,128)S(1)}, bf16[256,1024]{1,0:T(8,128)(2,1)S(1)}) custom-call(bf16[128,512]{1,0:T(8,128)(2,1)} %key_hbm.3, bf16[128,512]{1,0:T(8,128)(2,1)} %value_hbm.3, f32[16,512]{1,0:T(8,128)} %bitcast.5, bf16[128,1024]{1,0:T(8,128)(2,1)} %attn_key_hbm.1, ...), custom_call_target="tpu_custom_call" | custom-call | tf_op jit(solution)/shard_map/filter_states/pallas_call | solution.py:390
  2.1 2.5 %collective-permute-start.5 = (bf16[256,1024]{1,0:T(8,128)(2,1)S(1)}, bf16[256,1024]{1,0:T(8,128)(2,1)}, u32[]{:S(2)}, u32[]{:S(2)}) collective-permute-start(bf16[256,1024]{1,0:T(8,128)(2,1)S(1)} %get-tuple-element.33.block_hbm), channel_id=1, source_target_pairs={{0,8},{4,12},{8,16},{12,20},{16,24},{20,28},{24,32},{28,36},{32,40... | collective-permute-start | bytes 1572872 | tf_op jit(solution)/shard_map/ppermute | solution.py:30
  4.6 1.0 %collective-permute-start = (f32[32,128]{1,0:T(8,128)S(1)}, f32[32,128]{1,0:T(8,128)S(1)}, u32[]{:S(2)}, u32[]{:S(2)}) collective-permute-start(f32[32,128]{1,0:T(8,128)S(1)} %get-tuple-element.18), channel_id=1, source_target_pairs={{0,4},{4,0},{8,12},{12,8},{16,20},{20,16},{24,28},{28,24},{32,36},... | collective-permute-start | bytes 49160 | tf_op jit(solution)/shard_map/ppermute | solution.py:35
  5.6 0.8 %collective-permute-done.after_ref.refs_2_ = f32[32,128]{1,0:T(8,128)S(1)} collective-permute-done((f32[32,128]{1,0:T(8,128)S(1)}, f32[32,128]{1,0:T(8,128)S(1)}, u32[]{:S(2)}, u32[]{:S(2)}) %collective-permute-start) | collective-permute-done | bytes 16416 | tf_op jit(solution)/shard_map/ppermute | solution.py:35
  6.4 0.7 %broadcast_in_dim.3 = bf16[32,32,128]{2,1,0:T(8,128)(2,1)} broadcast(bf16[32,128]{1,0:T(8,128)(2,1)S(1)} %add_convert_fusion), dimensions={1,2} | broadcast | bytes 270336 | tf_op jit(solution)/shard_map/broadcast_in_dim | solution.py:421
  7.2 10.3 %all-to-all-start = ((bf16[32,32,128]{2,1,0:T(8,128)(2,1)}), bf16[32,32,128]{2,1,0:T(8,128)(2,1)S(1)}, u32[]{:S(2)}, u32[]{:S(2)}) async-start(bf16[32,32,128]{2,1,0:T(8,128)(2,1)} %broadcast_in_dim.3), calls=%async_computation | async-start | bytes 524288 | tf_op jit(solution)/shard_map/all_to_all | solution.py:420
  17.5 5.3 %collective-permute-done.5.two_hbm = bf16[256,1024]{1,0:T(8,128)(2,1)} collective-permute-done((bf16[256,1024]{1,0:T(8,128)(2,1)S(1)}, bf16[256,1024]{1,0:T(8,128)(2,1)}, u32[]{:S(2)}, u32[]{:S(2)}) %collective-permute-start.5) | collective-permute-done | bytes 524320 | tf_op jit(solution)/shard_map/ppermute | solution.py:30
  22.8 1.9 %broadcast_select_fusion = bf16[256,1024]{1,0:T(8,128)(2,1)} fusion(bf16[256,1024]{1,0:T(8,128)(2,1)S(1)} %get-tuple-element.33.block_hbm, bf16[256,1024]{1,0:T(8,128)(2,1)} %collective-permute-done.5.two_hbm, pred[]{:T(512)S(6)} %eq.4), kind=kLoop, calls=%fused_computation | loop fusion | flops 262144 | bytes 1572865 | tf_op jit(solution)/shard_map/jit(_where)/select_n | solution.py:414
  24.7 0.6 %collective-permute-start.6 = (bf16[256,1024]{1,0:T(8,128)(2,1)}, bf16[256,1024]{1,0:T(8,128)(2,1)}, u32[]{:S(2)}, u32[]{:S(2)}) collective-permute-start(bf16[256,1024]{1,0:T(8,128)(2,1)} %broadcast_select_fusion), channel_id=1, source_target_pairs={{0,4},{4,0},{8,12},{12,8},{16,20},{20,16},{24,28},{28,24},{32,36},... | collective-permute-start | bytes 1572872 | tf_op jit(solution)/shard_map/ppermute | solution.py:35
  25.2 2.0 %local_part.1 = (bf16[128,512]{1,0:T(8,128)(2,1)S(1)}, f32[128,512]{1,0:T(8,128)S(1)}, f32[64,128]{1,0:T(8,128)S(1)}, f32[64,128]{1,0:T(8,128)S(1)}, bf16[512,10...) custom-call(f32[32,128]{1,0:T(8,128)S(1)} %collective-permute-done.after_ref.refs_2_, bf16[128,512]{1,0:T(8,128)(2,1)} %key_hbm.3, ...), custom_call_target="tpu_custom_call" | custom-call | bytes 8388608 | tf_op jit(solution)/shard_map/local_part/pallas_call | solution.py:430
  27.2 0.6 %all-to-all-done.refs_0_ = bf16[32,32,128]{2,1,0:T(8,128)(2,1)S(1)} async-done(((bf16[32,32,128]{2,1,0:T(8,128)(2,1)}), bf16[32,32,128]{2,1,0:T(8,128)(2,1)S(1)}, u32[]{:S(2)}, u32[]{:S(2)}) %all-to-all-start) | async-done | bytes 262176 | tf_op jit(solution)/shard_map/all_to_all | solution.py:420
  27.8 0.1 carried_states.1
  27.9 3.2 %collective-permute-start.1 = (f32[32,128]{1,0:T(8,128)S(1)}, f32[32,128]{1,0:T(8,128)S(1)}, u32[]{:S(2)}, u32[]{:S(2)}) collective-permute-start(f32[32,128]{1,0:T(8,128)S(1)} %get-tuple-element.26), channel_id=1, source_target_pairs={{0,4},{4,0},{8,12},{12,8},{16,20},{20,16},{24,28},{28,24},{32,36},... | collective-permute-start | bytes 49160 | tf_op jit(solution)/shard_map/ppermute | solution.py:35
  31.1 0.8 %collective-permute-done.1.other_ref = f32[32,128]{1,0:T(8,128)S(1)} collective-permute-done((f32[32,128]{1,0:T(8,128)S(1)}, f32[32,128]{1,0:T(8,128)S(1)}, u32[]{:S(2)}, u32[]{:S(2)}) %collective-permute-start.1) | collective-permute-done | bytes 16416 | tf_op jit(solution)/shard_map/ppermute | solution.py:35
  31.9 2.2 %gate.1 = (bf16[128,512]{1,0:T(8,128)(2,1)S(1)}, bf16[128,1024]{1,0:T(8,128)(2,1)S(1)}, bf16[128,1024]{1,0:T(8,128)(2,1)S(1)}, bf16[128,1024]{1,0:T(8,128)(2,1)S(1)}) custom-call(bf16[128,512]{1,0:T(8,128)(2,1)S(1)} %get-tuple-element.19.query_ref, f32[128,512]{1,0:T(8,128)S(1)} %get-tuple-element.20.base_ref, ...), custom_call_target="tpu_custom_call" | custom-call | tf_op jit(solution)/shard_map/gate/pallas_call | solution.py:478
  34.1 0.0 copy-start.1
  34.1 0.0 copy-start.2
  34.1 2.8 %collective-permute-start.2 = (bf16[128,1024]{1,0:T(8,128)(2,1)S(1)}, bf16[128,1024]{1,0:T(8,128)(2,1)S(1)}, u32[]{:S(2)}, u32[]{:S(2)}) collective-permute-start(bf16[128,1024]{1,0:T(8,128)(2,1)S(1)} %get-tuple-element.30), channel_id=1, source_target_pairs={{0,2},{1,3},{2,0},{3,1},{4,6},{5,7},{6,4},{7,5},{8,10},{9,11},{10,... | collective-permute-start | bytes 786440 | tf_op jit(solution)/shard_map/ppermute | solution.py:30
  37.0 0.3 collective-permute-start.3
  37.3 2.4 %collective-permute-start.4 = (bf16[128,1024]{1,0:T(8,128)(2,1)S(1)}, bf16[128,1024]{1,0:T(8,128)(2,1)S(1)}, u32[]{:S(2)}, u32[]{:S(2)}) collective-permute-start(bf16[128,1024]{1,0:T(8,128)(2,1)S(1)} %get-tuple-element.32), channel_id=1, source_target_pairs={{0,3},{1,0},{2,1},{3,2},{4,7},{5,4},{6,5},{7,6},{8,11},{9,8},{10,9... | collective-permute-start | bytes 786440 | tf_op jit(solution)/shard_map/ppermute | solution.py:30
  39.6 1.6 %own.1.own_ref = f32[128,1024]{1,0:T(8,128)S(1)} custom-call(bf16[128,512]{1,0:T(8,128)(2,1)S(1)} %get-tuple-element.29.hyena_ref, bf16[512,4096]{1,0:T(8,128)(2,1)} %weight_hbm.5, bf16[128,1024]{1,0:T(8,128)(2,1)} %stream_hbm.1), custom_call_target="tpu_custom_call" | custom-call | tf_op jit(solution)/shard_map/own/pallas_call | solution.py:492
  41.3 5.1 %attention.1.after_ref = bf16[128,1024]{1,0:T(8,128)(2,1)} custom-call(bf16[128,1024]{1,0:T(8,128)(2,1)} %query_hbm.3, bf16[256,1024]{1,0:T(8,128)(2,1)} %copy-done, bf16[256,1024]{1,0:T(8,128)(2,1)} %collective-permute-done.6.one_hbm, bf16[256,1024]{1,0:T(8,128)(2,1)} %collective-permute-done.5.two_hbm, bf16[256,1024]{1,0:T(8,128)(2,1)} %collective-permute-done.7.three_hbm, ...), custom_call_target="tpu_custom_call" | custom-call | tf_op jit(solution)/shard_map/attention/pallas_call | solution.py:509
  46.5 3.1 %collective-permute-done.3.near_ref = bf16[128,1024]{1,0:T(8,128)(2,1)S(1)} collective-permute-done((bf16[128,1024]{1,0:T(8,128)(2,1)S(1)}, bf16[128,1024]{1,0:T(8,128)(2,1)S(1)}, u32[]{:S(2)}, u32[]{:S(2)}) %collective-permute-start.3) | collective-permute-done | bytes 262176 | tf_op jit(solution)/shard_map/ppermute | solution.py:30
  49.6 0.8 %finish.1 = bf16[128,1024]{1,0:T(8,128)(2,1)} custom-call(f32[128,1024]{1,0:T(8,128)S(1)} %own.1.own_ref, bf16[128,1024]{1,0:T(8,128)(2,1)S(1)} %collective-permute-done.2.far_ref, bf16[128,1024]{1,0:T(8,128)(2,1)S(1)} %collective-permute-done.3.near_ref, bf16[128,1024]{1,0:T(8,128)(2,1)S(1)} %collective-permute-done.4.back_ref, ...), custom_call_target="tpu_custom_call" | custom-call | tf_op jit(solution)/shard_map/finish/pallas_call | solution.py:524
  (10 shorter events, 0.0 us)
Async XLA Ops:
  2.1 32.1 %copy-start = (bf16[256,1024]{1,0:T(8,128)(2,1)}, bf16[256,1024]{1,0:T(8,128)(2,1)S(1)}, u32[]{:S(2)}) copy-start(bf16[256,1024]{1,0:T(8,128)(2,1)S(1)} %get-tuple-element.33.block_hbm) | copy-start | bytes 1572868
  2.1 20.7 %collective-permute-start.5 = (bf16[256,1024]{1,0:T(8,128)(2,1)S(1)}, bf16[256,1024]{1,0:T(8,128)(2,1)}, u32[]{:S(2)}, u32[]{:S(2)}) collective-permute-start(bf16[256,1024]{1,0:T(8,128)(2,1)S(1)} %get-tuple-element.33.block_hbm), channel_id=1, source_target_pairs={{0,8},{4,12},{8,16},{12,20},{16,24},{20,28},{24,32},{28,36},{32,40... | collective-permute-start | bytes 1572872 | tf_op jit(solution)/shard_map/ppermute | solution.py:30
  4.6 1.8 %collective-permute-start = (f32[32,128]{1,0:T(8,128)S(1)}, f32[32,128]{1,0:T(8,128)S(1)}, u32[]{:S(2)}, u32[]{:S(2)}) collective-permute-start(f32[32,128]{1,0:T(8,128)S(1)} %get-tuple-element.18), channel_id=1, source_target_pairs={{0,4},{4,0},{8,12},{12,8},{16,20},{20,16},{24,28},{28,24},{32,36},... | collective-permute-start | bytes 49160 | tf_op jit(solution)/shard_map/ppermute | solution.py:35
  7.2 20.7 %all-to-all-start = ((bf16[32,32,128]{2,1,0:T(8,128)(2,1)}), bf16[32,32,128]{2,1,0:T(8,128)(2,1)S(1)}, u32[]{:S(2)}, u32[]{:S(2)}) async-start(bf16[32,32,128]{2,1,0:T(8,128)(2,1)} %broadcast_in_dim.3), calls=%async_computation | async-start | bytes 524288 | tf_op jit(solution)/shard_map/all_to_all | solution.py:420
  24.7 16.6 %collective-permute-start.6 = (bf16[256,1024]{1,0:T(8,128)(2,1)}, bf16[256,1024]{1,0:T(8,128)(2,1)}, u32[]{:S(2)}, u32[]{:S(2)}) collective-permute-start(bf16[256,1024]{1,0:T(8,128)(2,1)} %broadcast_select_fusion), channel_id=1, source_target_pairs={{0,4},{4,0},{8,12},{12,8},{16,20},{20,16},{24,28},{28,24},{32,36},... | collective-permute-start | bytes 1572872 | tf_op jit(solution)/shard_map/ppermute | solution.py:35
  25.2 16.1 %collective-permute-start.7 = (bf16[256,1024]{1,0:T(8,128)(2,1)}, bf16[256,1024]{1,0:T(8,128)(2,1)}, u32[]{:S(2)}, u32[]{:S(2)}) collective-permute-start(bf16[256,1024]{1,0:T(8,128)(2,1)} %collective-permute-done.5.two_hbm), channel_id=1, source_target_pairs={{0,4},{4,8},{8,12},{12,16},{16,20},{20,24},{24,28},{28,32},{32,36}... | collective-permute-start | bytes 1572872 | tf_op jit(solution)/shard_map/ppermute | solution.py:30
  27.9 4.0 %collective-permute-start.1 = (f32[32,128]{1,0:T(8,128)S(1)}, f32[32,128]{1,0:T(8,128)S(1)}, u32[]{:S(2)}, u32[]{:S(2)}) collective-permute-start(f32[32,128]{1,0:T(8,128)S(1)} %get-tuple-element.26), channel_id=1, source_target_pairs={{0,4},{4,0},{8,12},{12,8},{16,20},{20,16},{24,28},{28,24},{32,36},... | collective-permute-start | bytes 49160 | tf_op jit(solution)/shard_map/ppermute | solution.py:35
  34.1 7.2 %copy-start.1 = (s32[128]{0:T(128)S(1)}, s32[128]{0:T(128)}, u32[]{:S(2)}) copy-start(s32[128]{0:T(128)} %param.24) | copy-start | bytes 1540
  34.1 7.2 %copy-start.2 = (s32[1,4]{1,0:T(1,128)S(1)}, s32[1,4]{1,0:T(1,128)}, u32[]{:S(2)}) copy-start(s32[1,4]{1,0:T(1,128)} %read_ref.1) | copy-start | bytes 52
  34.1 12.3 %collective-permute-start.2 = (bf16[128,1024]{1,0:T(8,128)(2,1)S(1)}, bf16[128,1024]{1,0:T(8,128)(2,1)S(1)}, u32[]{:S(2)}, u32[]{:S(2)}) collective-permute-start(bf16[128,1024]{1,0:T(8,128)(2,1)S(1)} %get-tuple-element.30), channel_id=1, source_target_pairs={{0,2},{1,3},{2,0},{3,1},{4,6},{5,7},{6,4},{7,5},{8,10},{9,11},{10,... | collective-permute-start | bytes 786440 | tf_op jit(solution)/shard_map/ppermute | solution.py:30
  37.0 12.6 %collective-permute-start.3 = (bf16[128,1024]{1,0:T(8,128)(2,1)S(1)}, bf16[128,1024]{1,0:T(8,128)(2,1)S(1)}, u32[]{:S(2)}, u32[]{:S(2)}) collective-permute-start(bf16[128,1024]{1,0:T(8,128)(2,1)S(1)} %get-tuple-element.31), channel_id=1, source_target_pairs={{0,1},{1,2},{2,3},{3,0},{4,5},{5,6},{6,7},{7,4},{8,9},{9,10},{10,1... | collective-permute-start | bytes 786440 | tf_op jit(solution)/shard_map/ppermute | solution.py:30
  37.3 12.3 %collective-permute-start.4 = (bf16[128,1024]{1,0:T(8,128)(2,1)S(1)}, bf16[128,1024]{1,0:T(8,128)(2,1)S(1)}, u32[]{:S(2)}, u32[]{:S(2)}) collective-permute-start(bf16[128,1024]{1,0:T(8,128)(2,1)S(1)} %get-tuple-element.32), channel_id=1, source_target_pairs={{0,3},{1,0},{2,1},{3,2},{4,7},{5,4},{6,5},{7,6},{8,11},{9,8},{10,9... | collective-permute-start | bytes 786440 | tf_op jit(solution)/shard_map/ppermute | solution.py:30

commit v3 on v2

--- a/solution.py
+++ b/solution.py
@@ -74,10 +74,12 @@
     decay_hbm,
     attn_key_hbm,
     attn_value_hbm,
+    weight_hbm,
     keep_ref,
     send_ref,
     rates_ref,
     block_ref,
+    far_ref,
     key_ref,
     value_ref,
     decay_ref,
@@ -86,11 +88,15 @@
     state_ref,
     sems,
 ):
+    core = lax.rem(lax.axis_index("ctx"), 2)
+    far_source = weight_columns(weight_hbm, 2, far_ref.shape[1])
+    far_rows = pl.ds(pl.multiple_of(core * far_ref.shape[0], far_ref.shape[0]), far_ref.shape[0])
     copies = load(
         [
             (decay_hbm, decay_ref),
             (key_hbm, key_ref),
             (value_hbm, value_ref),
+            (far_source.at[far_rows, :], far_ref),
             (attn_key_hbm, block_ref.at[: attn_key_hbm.shape[0]]),
             (attn_value_hbm, block_ref.at[attn_key_hbm.shape[0] :]),
         ],
@@ -120,12 +126,11 @@
         for part in range(1, parts):
             total = total * long_step + states[part][i]
         state_ref[8 * i : 8 * i + 8, :] = total
-    core = lax.rem(lax.axis_index("ctx"), 2)
     keep_ref[...] = half_rows(state_ref, core)
     send_ref[...] = half_rows(state_ref, 1 - core)
     rates_ref[...] = half_rows(all_rates_ref, core)
-    copies[3].wait()
-    copies[4].wait()
+    for copy in copies[3:]:
+        copy.wait()
 
 
 def carry_kernel(rows, all_ref, keep_ref, got_ref, rates_ref, *refs):
@@ -158,8 +163,8 @@
     base_ref,
     steps_ref,
     scale_ref,
-    far_ref,
     near_ref,
+    back_ref,
     key_ref,
     value_ref,
     decay_ref,
@@ -177,8 +182,8 @@
             (value_hbm, value_ref),
             (query_hbm, query_ref),
             (skip_hbm, skip_ref),
-            *weight_pairs(weight_hbm, 2, far_ref),
             *weight_pairs(weight_hbm, 1, near_ref),
+            *weight_pairs(weight_hbm, 3, back_ref),
         ],
         sems,
     )
@@ -229,19 +234,10 @@
     scale_ref,
     mine_ref,
     other_ref,
-    far_weight_ref,
-    near_weight_ref,
-    weight_hbm,
     hyena_ref,
-    far_ref,
-    near_ref,
-    back_ref,
     state_ref,
     conv_ref,
-    back_weight_ref,
-    sems,
 ):
-    copies = load(weight_pairs(weight_hbm, 3, back_weight_ref), sems)
     rows = query_ref.shape[0]
     groups = query_ref.shape[1] // LANES
     core = lax.rem(lax.axis_index("ctx"), 2)
@@ -262,11 +258,10 @@
         hyena_ref[:, lanes] = (query_ref[:, lanes].astype(jnp.float32) * conv).astype(
             hyena_ref.dtype
         )
-    pairs = ((far_weight_ref, far_ref), (near_weight_ref, near_ref), (back_weight_ref, back_ref))
-    for weight_ref, target in pairs:
-        if target is back_ref:
-            for copy in copies:
-                copy.wait()
+
+
+def near_kernel(hyena_ref, near_weight_ref, back_weight_ref, near_ref, back_ref):
+    for weight_ref, target in ((near_weight_ref, near_ref), (back_weight_ref, back_ref)):
         target[...] = jnp.dot(
             hyena_ref[...], weight_ref[...], preferred_element_type=jnp.float32
         ).astype(target.dtype)
@@ -285,22 +280,14 @@
     return weight_hbm.at[:, pl.ds(column, width)]
 
 
-def own_kernel(hyena_ref, weight_hbm, stream_hbm, own_ref, weight_ref, stream_ref, sems):
-    copies = load(
-        [*weight_pairs(weight_hbm, 0, weight_ref), (stream_hbm, stream_ref)],
-        sems,
-    )
-    for copy in copies:
-        copy.wait()
-    own_ref[...] = stream_ref[...].astype(jnp.float32) + jnp.dot(
-        hyena_ref[...], weight_ref[...], preferred_element_type=jnp.float32
-    )
-
-
-def finish_kernel(own_ref, far_ref, near_ref, back_ref, after_ref, out_ref):
-    total = own_ref[...]
-    for ref in (far_ref, near_ref, back_ref):
-        total = total + ref[...].astype(jnp.float32)
+def far_kernel(own_ref, far_ref, weight_ref, out_ref):
+    out_ref[...] = own_ref[...] + jnp.dot(
+        far_ref[...], weight_ref[...], preferred_element_type=jnp.float32
+    )
+
+
+def finish_kernel(own_ref, near_ref, back_ref, after_ref, out_ref):
+    total = own_ref[...] + near_ref[...].astype(jnp.float32) + back_ref[...].astype(jnp.float32)
     out_ref[...] = total.astype(out_ref.dtype)
 
 
@@ -310,26 +297,41 @@
     one_hbm,
     two_hbm,
     three_hbm,
+    weight_hbm,
+    stream_hbm,
+    half_hbm,
+    other_hbm,
+    hyena_ref,
     start_ref,
     read_ref,
     out_ref,
+    own_ref,
+    far_ref,
     query_ref,
     block_ref,
     one_ref,
     two_ref,
     three_ref,
+    weight_ref,
+    stream_ref,
     sems,
+    own_sems,
 ):
-    copies = load(
-        [
-            (query_hbm, query_ref),
-            (block_hbm, block_ref),
-            (one_hbm, one_ref),
-            (two_hbm, two_ref),
-            (three_hbm, three_ref),
-        ],
-        sems,
-    )
+    core = lax.rem(lax.axis_index("ctx"), 2)
+    sources = (query_hbm, block_hbm, one_hbm, two_hbm, three_hbm)
+    targets = (query_ref, block_ref, one_ref, two_ref, three_ref)
+    chunk = query_ref.shape[1] // 4
+    waits = []
+    for i in range(4):
+        cols = slice(i * chunk, (i + 1) * chunk)
+        pairs = [(source.at[:, cols], target.at[:, cols]) for source, target in zip(sources, targets)]
+        waits.append(load(pairs, sems.at[i]))
+    half = half_hbm.shape[0]
+    pairs = [*weight_pairs(weight_hbm, 0, weight_ref), (stream_hbm, stream_ref)]
+    for part, source in ((core, half_hbm), (1 - core, other_hbm)):
+        part_rows = pl.ds(pl.multiple_of(part * half, half), half)
+        pairs.append((source, far_ref.at[part_rows, :]))
+    own_copies = load(pairs, own_sems)
     rows = query_ref.shape[0]
     base = lax.axis_index("ctx") * rows
     starts = jnp.broadcast_to(start_ref[...] - base, (rows, rows)).T
@@ -343,23 +345,29 @@
             ok = ok & (pos <= query_pos)
         allowed.append(ok)
     mask = jnp.concatenate(allowed, axis=1)
-    for copy in copies:
-        copy.wait()
+    scale = math.log2(math.e) * HD ** (-0.5)
+    blocks = (three_ref, two_ref, one_ref, block_ref)
     for head in range(query_ref.shape[1] // HD):
+        if head * HD % chunk == 0:
+            for copy in waits[head * HD // chunk]:
+                copy.wait()
         cols = slice(head * HD, (head + 1) * HD)
-        query = query_ref[:, cols]
-        blocks = (three_ref, two_ref, one_ref, block_ref)
         keys = jnp.concatenate([ref[:rows, cols] for ref in blocks], axis=0)
         values = jnp.concatenate([ref[rows:, cols] for ref in blocks], axis=0)
         scores = lax.dot_general(
-            query, keys, (((1,), (1,)), ((), ())), preferred_element_type=jnp.float32
+            query_ref[:, cols], keys, (((1,), (1,)), ((), ())), preferred_element_type=jnp.float32
         )
-        scores = jnp.where(mask, scores * HD ** (-0.5), -jnp.inf)
+        scores = jnp.where(mask, scores * scale, -jnp.inf)
         top = jnp.max(scores, axis=1, keepdims=True)
-        weights = jnp.exp(scores - top)
+        weights = jnp.exp2(scores - top)
         total = jnp.sum(weights, axis=1, keepdims=True)
         summed = jnp.dot(weights.astype(jnp.bfloat16), values, preferred_element_type=jnp.float32)
         out_ref[:, cols] = (summed / total).astype(out_ref.dtype)
+    for copy in own_copies:
+        copy.wait()
+    own_ref[...] = stream_ref[...].astype(jnp.float32) + jnp.dot(
+        hyena_ref[...], weight_ref[...], preferred_element_type=jnp.float32
+    )
 
 
 def shards(
@@ -382,21 +390,23 @@
     state_rows = order * channels // LANES
     f32, bf16 = jnp.float32, jnp.bfloat16
     ctx_count = lax.axis_size("ctx")
+    width = out_weight.shape[1] // lax.axis_size("chan")
     core = lax.axis_index("ctx") % 2
     half = state_rows // 2
     state = jax.ShapeDtypeStruct((state_rows, LANES), f32)
     state_half = jax.ShapeDtypeStruct((half, LANES), f32)
 
-    keep, send, rates, block = pl.pallas_call(
+    keep, send, rates, block, far_half = pl.pallas_call(
         states_kernel,
         out_shape=(
             state_half,
             state_half,
             state_half,
             jax.ShapeDtypeStruct((2 * rows, attn_key.shape[1]), bf16),
+            jax.ShapeDtypeStruct((channels // 2, width), bf16),
         ),
-        in_specs=in_hbm(5),
-        out_specs=tuple(whole(4)),
+        in_specs=in_hbm(6),
+        out_specs=tuple(whole(5)),
         scratch_shapes=[
             VMEM((rows, channels), bf16),
             VMEM((rows, channels), bf16),
@@ -404,14 +414,16 @@
             VMEM((8 * rows, LANES), f32),
             VMEM((state_rows, LANES), f32),
             VMEM((state_rows, LANES), f32),
-            pltpu.SemaphoreType.DMA((5,)),
+            pltpu.SemaphoreType.DMA((6,)),
         ],
         compiler_params=room(4),
         name="filter_states",
-    )(*fixed(key_feat, value_feat, decay_rate.T, attn_key, attn_value))
+    )(*fixed(key_feat, value_feat, decay_rate.T, attn_key, attn_value, out_weight))
     block_2 = shifted(block, "ctx", 2)
     block_3 = shifted(block_2, "ctx", 1)
     block_1 = core_swap(jnp.where(core == 0, block, block_2))
+    far_half = shifted(far_half, "chan", 2)
+    far_other = core_swap(far_half)
     got = core_swap(send)
     first = jnp.where(core == 0, keep, got)
     second = jnp.where(core == 0, got, keep)
@@ -425,7 +437,6 @@
         axis_index_groups=groups,
     )
 
-    width = out_weight.shape[1] // lax.axis_size("chan")
     columns = jax.ShapeDtypeStruct((channels, width), bf16)
     query, base, steps, scale, *weights = pl.pallas_call(
         local_kernel,
@@ -475,60 +486,70 @@
     other = core_swap(other)
 
     piece = jax.ShapeDtypeStruct((rows, width), bf16)
-    hyena, far, near, back = pl.pallas_call(
+    hyena = pl.pallas_call(
         gate_kernel,
-        out_shape=(jax.ShapeDtypeStruct((rows, channels), bf16), piece, piece, piece),
-        in_specs=whole(8) + in_hbm(1),
-        out_specs=tuple(whole(4)),
-        scratch_shapes=[
-            VMEM((state_rows, LANES), f32),
-            VMEM((8 * rows, LANES), f32),
-            VMEM((channels, width), bf16),
-            pltpu.SemaphoreType.DMA((4,)),
-        ],
+        out_shape=jax.ShapeDtypeStruct((rows, channels), bf16),
+        in_specs=whole(6),
+        out_specs=whole(1)[0],
+        scratch_shapes=[VMEM((state_rows, LANES), f32), VMEM((8 * rows, LANES), f32)],
         compiler_params=room(4),
         name="gate",
-    )(query, base, steps, scale, mine, other, *weights, *fixed(out_weight))
-    own = pl.pallas_call(
-        own_kernel,
-        out_shape=jax.ShapeDtypeStruct((rows, width), f32),
-        in_specs=whole(1) + in_hbm(2),
-        out_specs=whole(1)[0],
-        scratch_shapes=[
+    )(query, base, steps, scale, mine, other)
+    near, back = pl.pallas_call(
+        near_kernel,
+        out_shape=(piece, piece),
+        in_specs=whole(3),
+        out_specs=tuple(whole(2)),
+        compiler_params=room(4),
+        name="near",
+    )(hyena, *weights)
+    far = shifted(hyena, "chan", 2)
+    near = shifted(near, "chan", 1)
+    back = shifted(back, "chan", 3)
+
+    attended, own, far_weight = pl.pallas_call(
+        attention_kernel,
+        out_shape=(
+            jax.ShapeDtypeStruct(attn_query.shape, bf16),
+            jax.ShapeDtypeStruct((rows, width), f32),
+            columns,
+        ),
+        in_specs=in_hbm(9) + whole(2) + [pl.BlockSpec(memory_space=pltpu.SMEM)],
+        out_specs=tuple(whole(3)),
+        scratch_shapes=[VMEM(attn_query.shape, bf16)]
+        + [VMEM((2 * rows, attn_query.shape[1]), bf16)] * 4
+        + [
             VMEM((channels, width), bf16),
             VMEM((rows, width), bf16),
-            pltpu.SemaphoreType.DMA((5,)),
+            pltpu.SemaphoreType.DMA((4, 5)),
+            pltpu.SemaphoreType.DMA((7,)),
         ],
-        compiler_params=room(8),
-        name="own",
-    )(hyena, *fixed(out_weight, stream))
-    far = shifted(far, "chan", 2)
-    near = shifted(near, "chan", 1)
-    back = shifted(back, "chan", 3)
-
-    attended = pl.pallas_call(
-        attention_kernel,
-        out_shape=jax.ShapeDtypeStruct(attn_query.shape, bf16),
-        in_specs=in_hbm(5) + whole(1) + [pl.BlockSpec(memory_space=pltpu.SMEM)],
-        out_specs=whole(1)[0],
-        scratch_shapes=[VMEM(attn_query.shape, bf16)]
-        + [VMEM((2 * rows, attn_query.shape[1]), bf16)] * 4
-        + [pltpu.SemaphoreType.DMA((5,))],
         compiler_params=room(8),
         name="attention",
     )(
         *fixed(attn_query, block, block_1, block_2, block_3),
+        *fixed(out_weight, stream, far_half, far_other),
+        hyena,
         doc_start.reshape(1, rows),
         read_mask,
     )
+    own = pl.pallas_call(
+        far_kernel,
+        out_shape=jax.ShapeDtypeStruct((rows, width), f32),
+        in_specs=whole(3),
+        out_specs=whole(1)[0],
+        compiler_params=room(4),
+        cost_estimate=pl.CostEstimate(flops=0, bytes_accessed=64 << 20, transcendentals=0),
+        name="far_product",
+    )(own, far, far_weight)
     mixed = pl.pallas_call(
         finish_kernel,
         out_shape=jax.ShapeDtypeStruct(stream.shape, bf16),
-        in_specs=whole(4) + [pl.BlockSpec(memory_space=pl.ANY)],
+        in_specs=whole(3) + [pl.BlockSpec(memory_space=pl.ANY)],
         out_specs=whole(1)[0],
         compiler_params=room(4),
         name="finish",
-    )(own, far, near, back, *fixed(attended))
+    )(own, near, back, *fixed(attended))
     return (mixed, attended)
 
 

time: 50.7 us -> 47.4 us (0.935)
  Pallas kernels: 13.2 us -> 10.9 us
  waiting for transfers between devices: 10.7 us -> 9.3 us
    pallas_call x3 -> x4, Pallas kernels: 8.94 us -> 6.59 us  [the longest x1 5.44 us: shards(): pl.pallas_call(attention_kernel, out_shape=(jax.ShapeDtypeStruct(attn_que...]
    ppermute x5 -> x6, waiting for transfers between devices: 8.38 us -> 6.47 us  [shifted(): lax.ppermute(value, axis, [(i, (i + steps) % count) for i in range(count)])]
    all_to_all x1, waiting for transfers between devices: 0.61 us -> 1.99 us  [shards(): lax.all_to_all(jnp.broadcast_to(both, (ctx_count // 2, half, LANES)), 'ct...]
    ppermute x3 -> x4, waiting for transfers between devices: 1.68 us -> 0.85 us  [core_swap(): return lax.ppermute(value, 'ctx', [(i, i ^ 1) for i in range(count)])]
    ppermute x3 -> x4, starting transfers between devices: 4.69 us -> 5.18 us  [core_swap(): return lax.ppermute(value, 'ctx', [(i, i ^ 1) for i in range(count)])]
    ppermute x5 -> x6, starting transfers between devices: 8.05 us -> 8.05 us  [shifted(): lax.ppermute(value, axis, [(i, (i + steps) % count) for i in range(count)])]
  transfers between devices with their start and end apart: 9 -> 11, of which waited for: 5 -> 5; matrix products, arithmetic and copies ran while one was open for 5% -> 6% of each run, Pallas kernels for 22% -> 18%
where the time goes in v3:
time: 47.4 us; the launch traced here: 47.1 us
  starting transfers between devices  23.5 us (50%)
  Pallas kernels  10.9 us (23%)
  waiting for transfers between devices  9.3 us (20%)
  other arithmetic  1.9 us (4%)
  local copies, waits for them, and re-layouts  0.75 us (2%)
  between operations  0.74 us (2%)
    all_to_all x1, starting transfers between devices, shards(): lax.all_to_all(jnp.broadcast_to(both, (ctx_count // 2, half, LANES)), 'ct...  10.3 us
    ppermute x6, starting transfers between devices, shifted(): lax.ppermute(value, axis, [(i, (i + steps) % count) for i in range(count)])  8.05 us
    ppermute x6, waiting for transfers between devices, shifted(): lax.ppermute(value, axis, [(i, (i + steps) % count) for i in range(count)])  6.47 us
    pallas_call x1, Pallas kernels, shards(): pl.pallas_call(attention_kernel, out_shape=(jax.ShapeDtypeStruct(attn_que...  5.44 us
    ppermute x4, starting transfers between devices, core_swap(): return lax.ppermute(value, 'ctx', [(i, i ^ 1) for i in range(count)])  5.18 us
    all_to_all x1, waiting for transfers between devices, shards(): lax.all_to_all(jnp.broadcast_to(both, (ctx_count // 2, half, LANES)), 'ct...  1.99 us
    pallas_call x1, Pallas kernels, shards(): pl.pallas_call(local_kernel, out_shape=(jax.ShapeDtypeStruct((rows, chann...  1.96 us
    select_n x1, other arithmetic, shards(): block_1 = core_swap(jnp.where(core == 0, block, block_2))  1.89 us
  transfers between devices with their start and end apart: 11, of which 5 were waited for; matrix products, arithmetic and copies ran while one was open for 6% of the time, Pallas kernels for 18%

profile of v3, /device:TPU:1, one launch (start us, length us, event | category | flops | bytes accessed | tf_op | source)
XLA Modules:
  0.0 47.1 jit_solution(11978101645161213772)
XLA Ops:
  0.6 1.4 %filter_states.1 = (f32[32,128]{1,0:T(8,128)S(1)}, f32[32,128]{1,0:T(8,128)S(1)}, f32[32,128]{1,0:T(8,128)S(1)}, bf16[256,1024]{1,0:T(8,128)(2,1)S(1)}, bf16[256,1024]{1,0:T(8,128)(2,1)S(1)}) custom-call(bf16[128,512]{1,0:T(8,128)(2,1)} %key_hbm.3, bf16[128,512]{1,0:T(8,128)(2,1)} %value_hbm.3, f32[16,512]{1,0:T(8,128)} %bitcast.5, ...), custom_call_target="tpu_custom_call" | custom-call | tf_op jit(solution)/shard_map/filter_states/pallas_call | solution.py:399
  2.1 2.5 %collective-permute-start = (bf16[256,1024]{1,0:T(8,128)(2,1)S(1)}, bf16[256,1024]{1,0:T(8,128)(2,1)}, u32[]{:S(2)}, u32[]{:S(2)}) collective-permute-start(bf16[256,1024]{1,0:T(8,128)(2,1)S(1)} %get-tuple-element.20.block_hbm), channel_id=1, source_target_pairs={{0,8},{4,12},{8,16},{12,20},{16,24},{20,28},{24,32},{28,36},{32,40... | collective-permute-start | bytes 1572872 | tf_op jit(solution)/shard_map/ppermute | solution.py:30
  4.6 1.0 %collective-permute-start.5 = (f32[32,128]{1,0:T(8,128)S(1)}, f32[32,128]{1,0:T(8,128)S(1)}, u32[]{:S(2)}, u32[]{:S(2)}) collective-permute-start(f32[32,128]{1,0:T(8,128)S(1)} %get-tuple-element.22), channel_id=1, source_target_pairs={{0,4},{4,0},{8,12},{12,8},{16,20},{20,16},{24,28},{28,24},{32,36},... | collective-permute-start | bytes 49160 | tf_op jit(solution)/shard_map/ppermute | solution.py:35
  5.6 2.7 %collective-permute-start.3 = (bf16[256,1024]{1,0:T(8,128)(2,1)S(1)}, bf16[256,1024]{1,0:T(8,128)(2,1)}, u32[]{:S(2)}, u32[]{:S(2)}) collective-permute-start(bf16[256,1024]{1,0:T(8,128)(2,1)S(1)} %get-tuple-element.21), channel_id=1, source_target_pairs={{0,2},{1,3},{2,0},{3,1},{4,6},{5,7},{6,4},{7,5},{8,10},{9,11},{10,... | collective-permute-start | bytes 1572872 | tf_op jit(solution)/shard_map/ppermute | solution.py:30
  8.3 0.7 %broadcast_in_dim.3 = bf16[32,32,128]{2,1,0:T(8,128)(2,1)} broadcast(bf16[32,128]{1,0:T(8,128)(2,1)S(1)} %add_convert_fusion), dimensions={1,2} | broadcast | bytes 270336 | tf_op jit(solution)/shard_map/broadcast_in_dim | solution.py:433
  9.1 10.3 %all-to-all-start = ((bf16[32,32,128]{2,1,0:T(8,128)(2,1)}), bf16[32,32,128]{2,1,0:T(8,128)(2,1)S(1)}, u32[]{:S(2)}, u32[]{:S(2)}) async-start(bf16[32,32,128]{2,1,0:T(8,128)(2,1)} %broadcast_in_dim.3), calls=%async_computation | async-start | bytes 524288 | tf_op jit(solution)/shard_map/all_to_all | solution.py:432
  19.4 3.4 %collective-permute-done.two_hbm = bf16[256,1024]{1,0:T(8,128)(2,1)} collective-permute-done((bf16[256,1024]{1,0:T(8,128)(2,1)S(1)}, bf16[256,1024]{1,0:T(8,128)(2,1)}, u32[]{:S(2)}, u32[]{:S(2)}) %collective-permute-start) | collective-permute-done | bytes 524320 | tf_op jit(solution)/shard_map/ppermute | solution.py:30
  22.8 1.9 %broadcast_select_fusion = bf16[256,1024]{1,0:T(8,128)(2,1)} fusion(bf16[256,1024]{1,0:T(8,128)(2,1)S(1)} %get-tuple-element.20.block_hbm, bf16[256,1024]{1,0:T(8,128)(2,1)} %collective-permute-done.two_hbm, pred[]{:T(512)S(6)} %eq.4), kind=kLoop, calls=%fused_computation | loop fusion | flops 262144 | bytes 1572865 | tf_op jit(solution)/shard_map/jit(_where)/select_n | solution.py:424
  24.7 0.2 collective-permute-start.1
  24.9 0.5 %collective-permute-start.4 = (bf16[256,1024]{1,0:T(8,128)(2,1)}, bf16[256,1024]{1,0:T(8,128)(2,1)}, u32[]{:S(2)}, u32[]{:S(2)}) collective-permute-start(bf16[256,1024]{1,0:T(8,128)(2,1)} %collective-permute-done.3.half_hbm), channel_id=1, source_target_pairs={{0,4},{4,0},{8,12},{12,8},{16,20},{20,16},{24,28},{28,24},{32,36},... | collective-permute-start | bytes 1572872 | tf_op jit(solution)/shard_map/ppermute | solution.py:35
  25.4 2.0 %local_part.1 = (bf16[128,512]{1,0:T(8,128)(2,1)S(1)}, f32[128,512]{1,0:T(8,128)S(1)}, f32[64,128]{1,0:T(8,128)S(1)}, f32[64,128]{1,0:T(8,128)S(1)}, bf16[512,10...) custom-call(f32[32,128]{1,0:T(8,128)S(1)} %collective-permute-done.5.after_ref.refs_2_, bf16[128,512]{1,0:T(8,128)(2,1)} %key_hbm.3, ...), custom_call_target="tpu_custom_call" | custom-call | bytes 8388608 | tf_op jit(solution)/shard_map/local_part/pallas_call | solution.py:441
  27.3 2.0 %all-to-all-done.refs_0_ = bf16[32,32,128]{2,1,0:T(8,128)(2,1)S(1)} async-done(((bf16[32,32,128]{2,1,0:T(8,128)(2,1)}), bf16[32,32,128]{2,1,0:T(8,128)(2,1)S(1)}, u32[]{:S(2)}, u32[]{:S(2)}) %all-to-all-start) | async-done | bytes 262176 | tf_op jit(solution)/shard_map/all_to_all | solution.py:432
  29.3 0.1 carried_states.1
  29.4 3.5 %collective-permute-start.6 = (f32[32,128]{1,0:T(8,128)S(1)}, f32[32,128]{1,0:T(8,128)S(1)}, u32[]{:S(2)}, u32[]{:S(2)}) collective-permute-start(f32[32,128]{1,0:T(8,128)S(1)} %get-tuple-element.30), channel_id=1, source_target_pairs={{0,4},{4,0},{8,12},{12,8},{16,20},{20,16},{24,28},{28,24},{32,36},... | collective-permute-start | bytes 49160 | tf_op jit(solution)/shard_map/ppermute | solution.py:35
  33.0 0.8 %collective-permute-done.6.other_ref = f32[32,128]{1,0:T(8,128)S(1)} collective-permute-done((f32[32,128]{1,0:T(8,128)S(1)}, f32[32,128]{1,0:T(8,128)S(1)}, u32[]{:S(2)}, u32[]{:S(2)}) %collective-permute-start.6) | collective-permute-done | bytes 16416 | tf_op jit(solution)/shard_map/ppermute | solution.py:35
  33.8 0.4 gate.1.hyena_ref
  34.2 0.5 near.1
  34.7 0.4 collective-permute-start.8
  35.0 2.4 %collective-permute-start.9 = (bf16[128,1024]{1,0:T(8,128)(2,1)S(1)}, bf16[128,1024]{1,0:T(8,128)(2,1)S(1)}, u32[]{:S(2)}, u32[]{:S(2)}) collective-permute-start(bf16[128,1024]{1,0:T(8,128)(2,1)S(1)} %get-tuple-element.36), channel_id=1, source_target_pairs={{0,3},{1,0},{2,1},{3,2},{4,7},{5,4},{6,5},{7,6},{8,11},{9,8},{10,9... | collective-permute-start | bytes 786440 | tf_op jit(solution)/shard_map/ppermute | solution.py:30
  37.5 5.4 %attention.1 = (bf16[128,1024]{1,0:T(8,128)(2,1)}, f32[128,1024]{1,0:T(8,128)S(1)}, bf16[512,1024]{1,0:T(8,128)(2,1)S(1)}) custom-call(bf16[128,1024]{1,0:T(8,128)(2,1)} %query_hbm.3, bf16[256,1024]{1,0:T(8,128)(2,1)} %copy-done, bf16[256,1024]{1,0:T(8,128)(2,1)} %collective-permute-done.1.one_hbm, bf16[256,1024]{1,0:T(8,128)(2,1)} %collective-permute-done.two_hbm, ...), custom_call_target="tpu_custom_call" | custom-call | tf_op jit(solution)/shard_map/attention/pallas_call | solution.py:510
  42.9 2.5 %collective-permute-done.7.far_ref = bf16[128,512]{1,0:T(8,128)(2,1)S(1)} collective-permute-done((bf16[128,512]{1,0:T(8,128)(2,1)S(1)}, bf16[128,512]{1,0:T(8,128)(2,1)S(1)}, u32[]{:S(2)}, u32[]{:S(2)}) %collective-permute-start.7) | collective-permute-done | bytes 131104 | tf_op jit(solution)/shard_map/ppermute | solution.py:30
  45.4 0.3 far_product.1.own_ref
  45.7 0.6 %collective-permute-done.8.near_ref = bf16[128,1024]{1,0:T(8,128)(2,1)S(1)} collective-permute-done((bf16[128,1024]{1,0:T(8,128)(2,1)S(1)}, bf16[128,1024]{1,0:T(8,128)(2,1)S(1)}, u32[]{:S(2)}, u32[]{:S(2)}) %collective-permute-start.8) | collective-permute-done | bytes 262176 | tf_op jit(solution)/shard_map/ppermute | solution.py:30
  46.3 0.8 %finish.1 = bf16[128,1024]{1,0:T(8,128)(2,1)} custom-call(f32[128,1024]{1,0:T(8,128)S(1)} %far_product.1.own_ref, bf16[128,1024]{1,0:T(8,128)(2,1)S(1)} %collective-permute-done.8.near_ref, bf16[128,1024]{1,0:T(8,128)(2,1)S(1)} %collective-permute-done.9.back_ref, bf16[128,1024]{1,0:T(8,128)(2,1)} %get-tuple-element.19.after_ref), custom_call_target="tpu_custom_call" | custom-call | tf_op jit(solution)/shard_map/finish/pallas_call | solution.py:545
  (15 shorter events, 0.0 us)
Async XLA Ops:
  2.1 32.6 %copy-start = (bf16[256,1024]{1,0:T(8,128)(2,1)}, bf16[256,1024]{1,0:T(8,128)(2,1)S(1)}, u32[]{:S(2)}) copy-start(bf16[256,1024]{1,0:T(8,128)(2,1)S(1)} %get-tuple-element.20.block_hbm) | copy-start | bytes 1572868
  2.1 20.7 %collective-permute-start = (bf16[256,1024]{1,0:T(8,128)(2,1)S(1)}, bf16[256,1024]{1,0:T(8,128)(2,1)}, u32[]{:S(2)}, u32[]{:S(2)}) collective-permute-start(bf16[256,1024]{1,0:T(8,128)(2,1)S(1)} %get-tuple-element.20.block_hbm), channel_id=1, source_target_pairs={{0,8},{4,12},{8,16},{12,20},{16,24},{20,28},{24,32},{28,36},{32,40... | collective-permute-start | bytes 1572872 | tf_op jit(solution)/shard_map/ppermute | solution.py:30
  4.6 3.7 %collective-permute-start.5 = (f32[32,128]{1,0:T(8,128)S(1)}, f32[32,128]{1,0:T(8,128)S(1)}, u32[]{:S(2)}, u32[]{:S(2)}) collective-permute-start(f32[32,128]{1,0:T(8,128)S(1)} %get-tuple-element.22), channel_id=1, source_target_pairs={{0,4},{4,0},{8,12},{12,8},{16,20},{20,16},{24,28},{28,24},{32,36},... | collective-permute-start | bytes 49160 | tf_op jit(solution)/shard_map/ppermute | solution.py:35
  5.6 19.3 %collective-permute-start.3 = (bf16[256,1024]{1,0:T(8,128)(2,1)S(1)}, bf16[256,1024]{1,0:T(8,128)(2,1)}, u32[]{:S(2)}, u32[]{:S(2)}) collective-permute-start(bf16[256,1024]{1,0:T(8,128)(2,1)S(1)} %get-tuple-element.21), channel_id=1, source_target_pairs={{0,2},{1,3},{2,0},{3,1},{4,6},{5,7},{6,4},{7,5},{8,10},{9,11},{10,... | collective-permute-start | bytes 1572872 | tf_op jit(solution)/shard_map/ppermute | solution.py:30
  9.1 20.3 %all-to-all-start = ((bf16[32,32,128]{2,1,0:T(8,128)(2,1)}), bf16[32,32,128]{2,1,0:T(8,128)(2,1)S(1)}, u32[]{:S(2)}, u32[]{:S(2)}) async-start(bf16[32,32,128]{2,1,0:T(8,128)(2,1)} %broadcast_in_dim.3), calls=%async_computation | async-start | bytes 524288 | tf_op jit(solution)/shard_map/all_to_all | solution.py:432
  24.7 12.8 %copy-start.1 = (s32[128]{0:T(128)S(1)}, s32[128]{0:T(128)}, u32[]{:S(2)}) copy-start(s32[128]{0:T(128)} %param.24) | copy-start | bytes 1540
  24.7 12.8 %copy-start.2 = (s32[1,4]{1,0:T(1,128)S(1)}, s32[1,4]{1,0:T(1,128)}, u32[]{:S(2)}) copy-start(s32[1,4]{1,0:T(1,128)} %read_ref.1) | copy-start | bytes 52
  24.7 12.8 %collective-permute-start.1 = (bf16[256,1024]{1,0:T(8,128)(2,1)}, bf16[256,1024]{1,0:T(8,128)(2,1)}, u32[]{:S(2)}, u32[]{:S(2)}) collective-permute-start(bf16[256,1024]{1,0:T(8,128)(2,1)} %broadcast_select_fusion), channel_id=1, source_target_pairs={{0,4},{4,0},{8,12},{12,8},{16,20},{20,16},{24,28},{28,24},{32,36},... | collective-permute-start | bytes 1572872 | tf_op jit(solution)/shard_map/ppermute | solution.py:35
  24.9 12.6 %collective-permute-start.2 = (bf16[256,1024]{1,0:T(8,128)(2,1)}, bf16[256,1024]{1,0:T(8,128)(2,1)}, u32[]{:S(2)}, u32[]{:S(2)}) collective-permute-start(bf16[256,1024]{1,0:T(8,128)(2,1)} %collective-permute-done.two_hbm), channel_id=1, source_target_pairs={{0,4},{4,8},{8,12},{12,16},{16,20},{20,24},{24,28},{28,32},{32,36}... | collective-permute-start | bytes 1572872 | tf_op jit(solution)/shard_map/ppermute | solution.py:30
  24.9 12.6 %collective-permute-start.4 = (bf16[256,1024]{1,0:T(8,128)(2,1)}, bf16[256,1024]{1,0:T(8,128)(2,1)}, u32[]{:S(2)}, u32[]{:S(2)}) collective-permute-start(bf16[256,1024]{1,0:T(8,128)(2,1)} %collective-permute-done.3.half_hbm), channel_id=1, source_target_pairs={{0,4},{4,0},{8,12},{12,8},{16,20},{20,16},{24,28},{28,24},{32,36},... | collective-permute-start | bytes 1572872 | tf_op jit(solution)/shard_map/ppermute | solution.py:35
  29.4 4.3 %collective-permute-start.6 = (f32[32,128]{1,0:T(8,128)S(1)}, f32[32,128]{1,0:T(8,128)S(1)}, u32[]{:S(2)}, u32[]{:S(2)}) collective-permute-start(f32[32,128]{1,0:T(8,128)S(1)} %get-tuple-element.30), channel_id=1, source_target_pairs={{0,4},{4,0},{8,12},{12,8},{16,20},{20,16},{24,28},{28,24},{32,36},... | collective-permute-start | bytes 49160 | tf_op jit(solution)/shard_map/ppermute | solution.py:35
  34.7 11.6 %collective-permute-start.8 = (bf16[128,1024]{1,0:T(8,128)(2,1)S(1)}, bf16[128,1024]{1,0:T(8,128)(2,1)S(1)}, u32[]{:S(2)}, u32[]{:S(2)}) collective-permute-start(bf16[128,1024]{1,0:T(8,128)(2,1)S(1)} %get-tuple-element.35), channel_id=1, source_target_pairs={{0,1},{1,2},{2,3},{3,0},{4,5},{5,6},{6,7},{7,4},{8,9},{9,10},{10,1... | collective-permute-start | bytes 786440 | tf_op jit(solution)/shard_map/ppermute | solution.py:30
  35.0 11.3 %collective-permute-start.9 = (bf16[128,1024]{1,0:T(8,128)(2,1)S(1)}, bf16[128,1024]{1,0:T(8,128)(2,1)S(1)}, u32[]{:S(2)}, u32[]{:S(2)}) collective-permute-start(bf16[128,1024]{1,0:T(8,128)(2,1)S(1)} %get-tuple-element.36), channel_id=1, source_target_pairs={{0,3},{1,0},{2,1},{3,2},{4,7},{5,4},{6,5},{7,6},{8,11},{9,8},{10,9... | collective-permute-start | bytes 786440 | tf_op jit(solution)/shard_map/ppermute | solution.py:30
  37.4 8.0 %collective-permute-start.7 = (bf16[128,512]{1,0:T(8,128)(2,1)S(1)}, bf16[128,512]{1,0:T(8,128)(2,1)S(1)}, u32[]{:S(2)}, u32[]{:S(2)}) collective-permute-start(bf16[128,512]{1,0:T(8,128)(2,1)S(1)} %gate.1.hyena_ref), channel_id=1, source_target_pairs={{0,2},{1,3},{2,0},{3,1},{4,6},{5,7},{6,4},{7,5},{8,10},{9,11},{10,... | collective-permute-start | bytes 393224 | tf_op jit(solution)/shard_map/ppermute | solution.py:30

commit v4 on v3

--- a/solution.py
+++ b/solution.py
@@ -63,8 +63,7 @@
     return copies
 
 
-def half_rows(ref, part):
-    half = ref.shape[0] // 2
+def half_rows(ref, part, half):
     return ref[pl.ds(pl.multiple_of(part * half, half), half), :]
 
 
@@ -106,7 +105,7 @@
     rows = key_ref.shape[0]
     copies[0].wait()
     to_state_rows(decay_ref, all_rates_ref, groups)
-    count = all_rates_ref.shape[0] // 8
+    count = state_ref.shape[0] // 8
     steps = [jnp.exp(-all_rates_ref[8 * i : 8 * i + 8, :]) for i in range(count)]
     copies[1].wait()
     copies[2].wait()
@@ -126,9 +125,10 @@
         for part in range(1, parts):
             total = total * long_step + states[part][i]
         state_ref[8 * i : 8 * i + 8, :] = total
-    keep_ref[...] = half_rows(state_ref, core)
-    send_ref[...] = half_rows(state_ref, 1 - core)
-    rates_ref[...] = half_rows(all_rates_ref, core)
+    half = keep_ref.shape[0]
+    keep_ref[...] = half_rows(state_ref, core, half)
+    send_ref[...] = half_rows(state_ref, 1 - core, half)
+    rates_ref[...] = half_rows(all_rates_ref, core, half)
     for copy in copies[3:]:
         copy.wait()
 
@@ -170,6 +170,8 @@
     decay_ref,
     residue_ref,
     skip_ref,
+    first_ref,
+    second_ref,
     product_ref,
     conv_ref,
     sems,
@@ -191,9 +193,11 @@
         copy.wait()
     groups = key_ref.shape[1] // LANES
     rows = key_ref.shape[0]
-    to_state_rows(decay_ref, steps_ref, groups)
-    to_state_rows(residue_ref, scale_ref, groups)
-    steps_ref[...] = jnp.exp(-steps_ref[...])
+    state_rows = steps_ref.shape[0]
+    to_state_rows(decay_ref, first_ref, groups)
+    to_state_rows(residue_ref, second_ref, groups)
+    steps_ref[...] = jnp.exp(-first_ref[:state_rows, :])
+    scale_ref[...] = second_ref[:state_rows, :]
     product = key_ref[...].astype(jnp.float32) * value_ref[...].astype(jnp.float32)
     to_position_rows(product, product_ref, groups)
     count = steps_ref.shape[0] // 8
@@ -220,7 +224,7 @@
 
 
 def from_position_rows(source_ref, g, groups):
-    rows = source_ref.shape[0] // (2 * groups)
+    rows = source_ref.shape[0] // (2 * groups) - 1
     return (
         source_ref[pl.ds(g, rows, stride=2 * groups), :]
         + source_ref[pl.ds(groups + g, rows, stride=2 * groups), :]
@@ -411,8 +415,8 @@
             VMEM((rows, channels), bf16),
             VMEM((rows, channels), bf16),
             VMEM((order, channels), f32),
-            VMEM((8 * rows, LANES), f32),
-            VMEM((state_rows, LANES), f32),
+            VMEM((8 * rows + 8, LANES), f32),
+            VMEM((state_rows + 8, LANES), f32),
             VMEM((state_rows, LANES), f32),
             pltpu.SemaphoreType.DMA((6,)),
         ],
@@ -456,8 +460,10 @@
             VMEM((order, channels), f32),
             VMEM((order, channels), f32),
             VMEM((1, channels), f32),
-            VMEM((8 * rows, LANES), f32),
-            VMEM((8 * rows, LANES), f32),
+            VMEM((state_rows + 8, LANES), f32),
+            VMEM((state_rows + 8, LANES), f32),
+            VMEM((8 * rows + 8, LANES), f32),
+            VMEM((8 * rows + 8, LANES), f32),
             pltpu.SemaphoreType.DMA((14,)),
         ],
         compiler_params=room(6),
@@ -491,7 +497,7 @@
         out_shape=jax.ShapeDtypeStruct((rows, channels), bf16),
         in_specs=whole(6),
         out_specs=whole(1)[0],
-        scratch_shapes=[VMEM((state_rows, LANES), f32), VMEM((8 * rows, LANES), f32)],
+        scratch_shapes=[VMEM((state_rows, LANES), f32), VMEM((8 * rows + 8, LANES), f32)],
         compiler_params=room(4),
         name="gate",
     )(query, base, steps, scale, mine, other)

time: 47.4 us -> 47.4 us (level)
  no operation moved by 1% of the time
where the time goes in v4:
time: 47.4 us; the launch traced here: 47.1 us
  starting transfers between devices  23.5 us (50%)
  Pallas kernels  10.9 us (23%)
  waiting for transfers between devices  9.3 us (20%)
  other arithmetic  1.9 us (4%)
  local copies, waits for them, and re-layouts  0.75 us (2%)
  between operations  0.74 us (2%)
    all_to_all x1, starting transfers between devices, shards(): lax.all_to_all(jnp.broadcast_to(both, (ctx_count // 2, half, LANES)), 'ct...  10.3 us
    ppermute x6, starting transfers between devices, shifted(): lax.ppermute(value, axis, [(i, (i + steps) % count) for i in range(count)])  8.05 us
    ppermute x6, waiting for transfers between devices, shifted(): lax.ppermute(value, axis, [(i, (i + steps) % count) for i in range(count)])  6.46 us
    pallas_call x1, Pallas kernels, shards(): pl.pallas_call(attention_kernel, out_shape=(jax.ShapeDtypeStruct(attn_que...  5.43 us
    ppermute x4, starting transfers between devices, core_swap(): return lax.ppermute(value, 'ctx', [(i, i ^ 1) for i in range(count)])  5.18 us
    all_to_all x1, waiting for transfers between devices, shards(): lax.all_to_all(jnp.broadcast_to(both, (ctx_count // 2, half, LANES)), 'ct...  1.99 us
    pallas_call x1, Pallas kernels, shards(): pl.pallas_call(local_kernel, out_shape=(jax.ShapeDtypeStruct((rows, chann...  1.96 us
    select_n x1, other arithmetic, shards(): block_1 = core_swap(jnp.where(core == 0, block, block_2))  1.89 us
  transfers between devices with their start and end apart: 11, of which 5 were waited for; matrix products, arithmetic and copies ran while one was open for 6% of the time, Pallas kernels for 18%

profile of v4, /device:TPU:1, one launch (start us, length us, event | category | flops | bytes accessed | tf_op | source)
XLA Modules:
  0.0 47.1 jit_solution(18443252366547324786)
XLA Ops:
  0.6 1.4 %filter_states.1 = (f32[32,128]{1,0:T(8,128)S(1)}, f32[32,128]{1,0:T(8,128)S(1)}, f32[32,128]{1,0:T(8,128)S(1)}, bf16[256,1024]{1,0:T(8,128)(2,1)S(1)}, bf16[256,1024]{1,0:T(8,128)(2,1)S(1)}) custom-call(bf16[128,512]{1,0:T(8,128)(2,1)} %key_hbm.3, bf16[128,512]{1,0:T(8,128)(2,1)} %value_hbm.3, f32[16,512]{1,0:T(8,128)} %bitcast.5, ...), custom_call_target="tpu_custom_call" | custom-call | tf_op jit(solution)/shard_map/filter_states/pallas_call | solution.py:403
  2.1 2.5 %collective-permute-start = (bf16[256,1024]{1,0:T(8,128)(2,1)S(1)}, bf16[256,1024]{1,0:T(8,128)(2,1)}, u32[]{:S(2)}, u32[]{:S(2)}) collective-permute-start(bf16[256,1024]{1,0:T(8,128)(2,1)S(1)} %get-tuple-element.20.block_hbm), channel_id=1, source_target_pairs={{0,8},{4,12},{8,16},{12,20},{16,24},{20,28},{24,32},{28,36},{32,40... | collective-permute-start | bytes 1572872 | tf_op jit(solution)/shard_map/ppermute | solution.py:30
  4.6 1.0 %collective-permute-start.5 = (f32[32,128]{1,0:T(8,128)S(1)}, f32[32,128]{1,0:T(8,128)S(1)}, u32[]{:S(2)}, u32[]{:S(2)}) collective-permute-start(f32[32,128]{1,0:T(8,128)S(1)} %get-tuple-element.22), channel_id=1, source_target_pairs={{0,4},{4,0},{8,12},{12,8},{16,20},{20,16},{24,28},{28,24},{32,36},... | collective-permute-start | bytes 49160 | tf_op jit(solution)/shard_map/ppermute | solution.py:35
  5.6 2.7 %collective-permute-start.3 = (bf16[256,1024]{1,0:T(8,128)(2,1)S(1)}, bf16[256,1024]{1,0:T(8,128)(2,1)}, u32[]{:S(2)}, u32[]{:S(2)}) collective-permute-start(bf16[256,1024]{1,0:T(8,128)(2,1)S(1)} %get-tuple-element.21), channel_id=1, source_target_pairs={{0,2},{1,3},{2,0},{3,1},{4,6},{5,7},{6,4},{7,5},{8,10},{9,11},{10,... | collective-permute-start | bytes 1572872 | tf_op jit(solution)/shard_map/ppermute | solution.py:30
  8.3 0.7 %broadcast_in_dim.3 = bf16[32,32,128]{2,1,0:T(8,128)(2,1)} broadcast(bf16[32,128]{1,0:T(8,128)(2,1)S(1)} %add_convert_fusion), dimensions={1,2} | broadcast | bytes 270336 | tf_op jit(solution)/shard_map/broadcast_in_dim | solution.py:437
  9.1 10.3 %all-to-all-start = ((bf16[32,32,128]{2,1,0:T(8,128)(2,1)}), bf16[32,32,128]{2,1,0:T(8,128)(2,1)S(1)}, u32[]{:S(2)}, u32[]{:S(2)}) async-start(bf16[32,32,128]{2,1,0:T(8,128)(2,1)} %broadcast_in_dim.3), calls=%async_computation | async-start | bytes 524288 | tf_op jit(solution)/shard_map/all_to_all | solution.py:436
  19.4 3.4 %collective-permute-done.two_hbm = bf16[256,1024]{1,0:T(8,128)(2,1)} collective-permute-done((bf16[256,1024]{1,0:T(8,128)(2,1)S(1)}, bf16[256,1024]{1,0:T(8,128)(2,1)}, u32[]{:S(2)}, u32[]{:S(2)}) %collective-permute-start) | collective-permute-done | bytes 524320 | tf_op jit(solution)/shard_map/ppermute | solution.py:30
  22.8 1.9 %broadcast_select_fusion = bf16[256,1024]{1,0:T(8,128)(2,1)} fusion(bf16[256,1024]{1,0:T(8,128)(2,1)S(1)} %get-tuple-element.20.block_hbm, bf16[256,1024]{1,0:T(8,128)(2,1)} %collective-permute-done.two_hbm, pred[]{:T(512)S(6)} %eq.4), kind=kLoop, calls=%fused_computation | loop fusion | flops 262144 | bytes 1572865 | tf_op jit(solution)/shard_map/jit(_where)/select_n | solution.py:428
  24.7 0.2 collective-permute-start.1
  24.9 0.5 %collective-permute-start.4 = (bf16[256,1024]{1,0:T(8,128)(2,1)}, bf16[256,1024]{1,0:T(8,128)(2,1)}, u32[]{:S(2)}, u32[]{:S(2)}) collective-permute-start(bf16[256,1024]{1,0:T(8,128)(2,1)} %collective-permute-done.3.half_hbm), channel_id=1, source_target_pairs={{0,4},{4,0},{8,12},{12,8},{16,20},{20,16},{24,28},{28,24},{32,36},... | collective-permute-start | bytes 1572872 | tf_op jit(solution)/shard_map/ppermute | solution.py:35
  25.4 2.0 %local_part.1 = (bf16[128,512]{1,0:T(8,128)(2,1)S(1)}, f32[128,512]{1,0:T(8,128)S(1)}, f32[64,128]{1,0:T(8,128)S(1)}, f32[64,128]{1,0:T(8,128)S(1)}, bf16[512,10...) custom-call(f32[32,128]{1,0:T(8,128)S(1)} %collective-permute-done.5.after_ref.refs_2_, bf16[128,512]{1,0:T(8,128)(2,1)} %key_hbm.3, ...), custom_call_target="tpu_custom_call" | custom-call | bytes 8388608 | tf_op jit(solution)/shard_map/local_part/pallas_call | solution.py:445
  27.3 2.0 %all-to-all-done.refs_0_ = bf16[32,32,128]{2,1,0:T(8,128)(2,1)S(1)} async-done(((bf16[32,32,128]{2,1,0:T(8,128)(2,1)}), bf16[32,32,128]{2,1,0:T(8,128)(2,1)S(1)}, u32[]{:S(2)}, u32[]{:S(2)}) %all-to-all-start) | async-done | bytes 262176 | tf_op jit(solution)/shard_map/all_to_all | solution.py:436
  29.3 0.1 carried_states.1
  29.4 3.5 %collective-permute-start.6 = (f32[32,128]{1,0:T(8,128)S(1)}, f32[32,128]{1,0:T(8,128)S(1)}, u32[]{:S(2)}, u32[]{:S(2)}) collective-permute-start(f32[32,128]{1,0:T(8,128)S(1)} %get-tuple-element.30), channel_id=1, source_target_pairs={{0,4},{4,0},{8,12},{12,8},{16,20},{20,16},{24,28},{28,24},{32,36},... | collective-permute-start | bytes 49160 | tf_op jit(solution)/shard_map/ppermute | solution.py:35
  33.0 0.8 %collective-permute-done.6.other_ref = f32[32,128]{1,0:T(8,128)S(1)} collective-permute-done((f32[32,128]{1,0:T(8,128)S(1)}, f32[32,128]{1,0:T(8,128)S(1)}, u32[]{:S(2)}, u32[]{:S(2)}) %collective-permute-start.6) | collective-permute-done | bytes 16416 | tf_op jit(solution)/shard_map/ppermute | solution.py:35
  33.8 0.4 gate.1.hyena_ref
  34.2 0.5 near.1
  34.7 0.4 collective-permute-start.8
  35.0 2.4 %collective-permute-start.9 = (bf16[128,1024]{1,0:T(8,128)(2,1)S(1)}, bf16[128,1024]{1,0:T(8,128)(2,1)S(1)}, u32[]{:S(2)}, u32[]{:S(2)}) collective-permute-start(bf16[128,1024]{1,0:T(8,128)(2,1)S(1)} %get-tuple-element.36), channel_id=1, source_target_pairs={{0,3},{1,0},{2,1},{3,2},{4,7},{5,4},{6,5},{7,6},{8,11},{9,8},{10,9... | collective-permute-start | bytes 786440 | tf_op jit(solution)/shard_map/ppermute | solution.py:30
  37.5 5.4 %attention.1 = (bf16[128,1024]{1,0:T(8,128)(2,1)}, f32[128,1024]{1,0:T(8,128)S(1)}, bf16[512,1024]{1,0:T(8,128)(2,1)S(1)}) custom-call(bf16[128,1024]{1,0:T(8,128)(2,1)} %query_hbm.3, bf16[256,1024]{1,0:T(8,128)(2,1)} %copy-done, bf16[256,1024]{1,0:T(8,128)(2,1)} %collective-permute-done.1.one_hbm, bf16[256,1024]{1,0:T(8,128)(2,1)} %collective-permute-done.two_hbm, ...), custom_call_target="tpu_custom_call" | custom-call | tf_op jit(solution)/shard_map/attention/pallas_call | solution.py:516
  42.9 2.5 %collective-permute-done.7.far_ref = bf16[128,512]{1,0:T(8,128)(2,1)S(1)} collective-permute-done((bf16[128,512]{1,0:T(8,128)(2,1)S(1)}, bf16[128,512]{1,0:T(8,128)(2,1)S(1)}, u32[]{:S(2)}, u32[]{:S(2)}) %collective-permute-start.7) | collective-permute-done | bytes 131104 | tf_op jit(solution)/shard_map/ppermute | solution.py:30
  45.4 0.3 far_product.1.own_ref
  45.7 0.6 %collective-permute-done.8.near_ref = bf16[128,1024]{1,0:T(8,128)(2,1)S(1)} collective-permute-done((bf16[128,1024]{1,0:T(8,128)(2,1)S(1)}, bf16[128,1024]{1,0:T(8,128)(2,1)S(1)}, u32[]{:S(2)}, u32[]{:S(2)}) %collective-permute-start.8) | collective-permute-done | bytes 262176 | tf_op jit(solution)/shard_map/ppermute | solution.py:30
  46.3 0.8 %finish.1 = bf16[128,1024]{1,0:T(8,128)(2,1)} custom-call(f32[128,1024]{1,0:T(8,128)S(1)} %far_product.1.own_ref, bf16[128,1024]{1,0:T(8,128)(2,1)S(1)} %collective-permute-done.8.near_ref, bf16[128,1024]{1,0:T(8,128)(2,1)S(1)} %collective-permute-done.9.back_ref, bf16[128,1024]{1,0:T(8,128)(2,1)} %get-tuple-element.19.after_ref), custom_call_target="tpu_custom_call" | custom-call | tf_op jit(solution)/shard_map/finish/pallas_call | solution.py:551
  (15 shorter events, 0.0 us)
Async XLA Ops:
  2.1 32.6 %copy-start = (bf16[256,1024]{1,0:T(8,128)(2,1)}, bf16[256,1024]{1,0:T(8,128)(2,1)S(1)}, u32[]{:S(2)}) copy-start(bf16[256,1024]{1,0:T(8,128)(2,1)S(1)} %get-tuple-element.20.block_hbm) | copy-start | bytes 1572868
  2.1 20.7 %collective-permute-start = (bf16[256,1024]{1,0:T(8,128)(2,1)S(1)}, bf16[256,1024]{1,0:T(8,128)(2,1)}, u32[]{:S(2)}, u32[]{:S(2)}) collective-permute-start(bf16[256,1024]{1,0:T(8,128)(2,1)S(1)} %get-tuple-element.20.block_hbm), channel_id=1, source_target_pairs={{0,8},{4,12},{8,16},{12,20},{16,24},{20,28},{24,32},{28,36},{32,40... | collective-permute-start | bytes 1572872 | tf_op jit(solution)/shard_map/ppermute | solution.py:30
  4.6 3.7 %collective-permute-start.5 = (f32[32,128]{1,0:T(8,128)S(1)}, f32[32,128]{1,0:T(8,128)S(1)}, u32[]{:S(2)}, u32[]{:S(2)}) collective-permute-start(f32[32,128]{1,0:T(8,128)S(1)} %get-tuple-element.22), channel_id=1, source_target_pairs={{0,4},{4,0},{8,12},{12,8},{16,20},{20,16},{24,28},{28,24},{32,36},... | collective-permute-start | bytes 49160 | tf_op jit(solution)/shard_map/ppermute | solution.py:35
  5.6 19.3 %collective-permute-start.3 = (bf16[256,1024]{1,0:T(8,128)(2,1)S(1)}, bf16[256,1024]{1,0:T(8,128)(2,1)}, u32[]{:S(2)}, u32[]{:S(2)}) collective-permute-start(bf16[256,1024]{1,0:T(8,128)(2,1)S(1)} %get-tuple-element.21), channel_id=1, source_target_pairs={{0,2},{1,3},{2,0},{3,1},{4,6},{5,7},{6,4},{7,5},{8,10},{9,11},{10,... | collective-permute-start | bytes 1572872 | tf_op jit(solution)/shard_map/ppermute | solution.py:30
  9.1 20.3 %all-to-all-start = ((bf16[32,32,128]{2,1,0:T(8,128)(2,1)}), bf16[32,32,128]{2,1,0:T(8,128)(2,1)S(1)}, u32[]{:S(2)}, u32[]{:S(2)}) async-start(bf16[32,32,128]{2,1,0:T(8,128)(2,1)} %broadcast_in_dim.3), calls=%async_computation | async-start | bytes 524288 | tf_op jit(solution)/shard_map/all_to_all | solution.py:436
  24.7 12.8 %copy-start.1 = (s32[128]{0:T(128)S(1)}, s32[128]{0:T(128)}, u32[]{:S(2)}) copy-start(s32[128]{0:T(128)} %param.24) | copy-start | bytes 1540
  24.7 12.8 %copy-start.2 = (s32[1,4]{1,0:T(1,128)S(1)}, s32[1,4]{1,0:T(1,128)}, u32[]{:S(2)}) copy-start(s32[1,4]{1,0:T(1,128)} %read_ref.1) | copy-start | bytes 52
  24.7 12.8 %collective-permute-start.1 = (bf16[256,1024]{1,0:T(8,128)(2,1)}, bf16[256,1024]{1,0:T(8,128)(2,1)}, u32[]{:S(2)}, u32[]{:S(2)}) collective-permute-start(bf16[256,1024]{1,0:T(8,128)(2,1)} %broadcast_select_fusion), channel_id=1, source_target_pairs={{0,4},{4,0},{8,12},{12,8},{16,20},{20,16},{24,28},{28,24},{32,36},... | collective-permute-start | bytes 1572872 | tf_op jit(solution)/shard_map/ppermute | solution.py:35
  24.9 12.6 %collective-permute-start.2 = (bf16[256,1024]{1,0:T(8,128)(2,1)}, bf16[256,1024]{1,0:T(8,128)(2,1)}, u32[]{:S(2)}, u32[]{:S(2)}) collective-permute-start(bf16[256,1024]{1,0:T(8,128)(2,1)} %collective-permute-done.two_hbm), channel_id=1, source_target_pairs={{0,4},{4,8},{8,12},{12,16},{16,20},{20,24},{24,28},{28,32},{32,36}... | collective-permute-start | bytes 1572872 | tf_op jit(solution)/shard_map/ppermute | solution.py:30
  24.9 12.6 %collective-permute-start.4 = (bf16[256,1024]{1,0:T(8,128)(2,1)}, bf16[256,1024]{1,0:T(8,128)(2,1)}, u32[]{:S(2)}, u32[]{:S(2)}) collective-permute-start(bf16[256,1024]{1,0:T(8,128)(2,1)} %collective-permute-done.3.half_hbm), channel_id=1, source_target_pairs={{0,4},{4,0},{8,12},{12,8},{16,20},{20,16},{24,28},{28,24},{32,36},... | collective-permute-start | bytes 1572872 | tf_op jit(solution)/shard_map/ppermute | solution.py:35
  29.4 4.3 %collective-permute-start.6 = (f32[32,128]{1,0:T(8,128)S(1)}, f32[32,128]{1,0:T(8,128)S(1)}, u32[]{:S(2)}, u32[]{:S(2)}) collective-permute-start(f32[32,128]{1,0:T(8,128)S(1)} %get-tuple-element.30), channel_id=1, source_target_pairs={{0,4},{4,0},{8,12},{12,8},{16,20},{20,16},{24,28},{28,24},{32,36},... | collective-permute-start | bytes 49160 | tf_op jit(solution)/shard_map/ppermute | solution.py:35
  34.7 11.6 %collective-permute-start.8 = (bf16[128,1024]{1,0:T(8,128)(2,1)S(1)}, bf16[128,1024]{1,0:T(8,128)(2,1)S(1)}, u32[]{:S(2)}, u32[]{:S(2)}) collective-permute-start(bf16[128,1024]{1,0:T(8,128)(2,1)S(1)} %get-tuple-element.35), channel_id=1, source_target_pairs={{0,1},{1,2},{2,3},{3,0},{4,5},{5,6},{6,7},{7,4},{8,9},{9,10},{10,1... | collective-permute-start | bytes 786440 | tf_op jit(solution)/shard_map/ppermute | solution.py:30
  35.0 11.3 %collective-permute-start.9 = (bf16[128,1024]{1,0:T(8,128)(2,1)S(1)}, bf16[128,1024]{1,0:T(8,128)(2,1)S(1)}, u32[]{:S(2)}, u32[]{:S(2)}) collective-permute-start(bf16[128,1024]{1,0:T(8,128)(2,1)S(1)} %get-tuple-element.36), channel_id=1, source_target_pairs={{0,3},{1,0},{2,1},{3,2},{4,7},{5,4},{6,5},{7,6},{8,11},{9,8},{10,9... | collective-permute-start | bytes 786440 | tf_op jit(solution)/shard_map/ppermute | solution.py:30
  37.4 8.0 %collective-permute-start.7 = (bf16[128,512]{1,0:T(8,128)(2,1)S(1)}, bf16[128,512]{1,0:T(8,128)(2,1)S(1)}, u32[]{:S(2)}, u32[]{:S(2)}) collective-permute-start(bf16[128,512]{1,0:T(8,128)(2,1)S(1)} %gate.1.hyena_ref), channel_id=1, source_target_pairs={{0,2},{1,3},{2,0},{3,1},{4,6},{5,7},{6,4},{7,5},{8,10},{9,11},{10,... | collective-permute-start | bytes 393224 | tf_op jit(solution)/shard_map/ppermute | solution.py:30

commit v5 on v4

--- a/solution.py
+++ b/solution.py
@@ -238,7 +238,11 @@
     scale_ref,
     mine_ref,
     other_ref,
+    near_weight_ref,
+    back_weight_ref,
     hyena_ref,
+    near_ref,
+    back_ref,
     state_ref,
     conv_ref,
 ):
@@ -262,9 +266,6 @@
         hyena_ref[:, lanes] = (query_ref[:, lanes].astype(jnp.float32) * conv).astype(
             hyena_ref.dtype
         )
-
-
-def near_kernel(hyena_ref, near_weight_ref, back_weight_ref, near_ref, back_ref):
     for weight_ref, target in ((near_weight_ref, near_ref), (back_weight_ref, back_ref)):
         target[...] = jnp.dot(
             hyena_ref[...], weight_ref[...], preferred_element_type=jnp.float32
@@ -284,15 +285,25 @@
     return weight_hbm.at[:, pl.ds(column, width)]
 
 
-def far_kernel(own_ref, far_ref, weight_ref, out_ref):
-    out_ref[...] = own_ref[...] + jnp.dot(
-        far_ref[...], weight_ref[...], preferred_element_type=jnp.float32
-    )
-
-
-def finish_kernel(own_ref, near_ref, back_ref, after_ref, out_ref):
-    total = own_ref[...] + near_ref[...].astype(jnp.float32) + back_ref[...].astype(jnp.float32)
-    out_ref[...] = total.astype(out_ref.dtype)
+def finish_kernel(
+    own_ref, near_ref, back_ref, far_ref, weight_ref, after_ref, out_hbm, out_ref, sems
+):
+    pieces = sems.shape[0]
+    width = out_ref.shape[1] // pieces
+    copies = []
+    for i in range(pieces):
+        lanes = slice(i * width, (i + 1) * width)
+        total = own_ref[:, lanes] + near_ref[:, lanes].astype(jnp.float32)
+        total = total + back_ref[:, lanes].astype(jnp.float32)
+        total = total + jnp.dot(
+            far_ref[...], weight_ref[:, lanes], preferred_element_type=jnp.float32
+        )
+        out_ref[:, lanes] = total.astype(out_ref.dtype)
+        copy = pltpu.make_async_copy(out_ref.at[:, lanes], out_hbm.at[:, lanes], sems.at[i])
+        copy.start()
+        copies.append(copy)
+    for copy in copies:
+        copy.wait()
 
 
 def attention_kernel(
@@ -492,23 +503,15 @@
     other = core_swap(other)
 
     piece = jax.ShapeDtypeStruct((rows, width), bf16)
-    hyena = pl.pallas_call(
+    hyena, near, back = pl.pallas_call(
         gate_kernel,
-        out_shape=jax.ShapeDtypeStruct((rows, channels), bf16),
-        in_specs=whole(6),
-        out_specs=whole(1)[0],
+        out_shape=(jax.ShapeDtypeStruct((rows, channels), bf16), piece, piece),
+        in_specs=whole(8),
+        out_specs=tuple(whole(3)),
         scratch_shapes=[VMEM((state_rows, LANES), f32), VMEM((8 * rows + 8, LANES), f32)],
         compiler_params=room(4),
         name="gate",
-    )(query, base, steps, scale, mine, other)
-    near, back = pl.pallas_call(
-        near_kernel,
-        out_shape=(piece, piece),
-        in_specs=whole(3),
-        out_specs=tuple(whole(2)),
-        compiler_params=room(4),
-        name="near",
-    )(hyena, *weights)
+    )(query, base, steps, scale, mine, other, *weights)
     far = shifted(hyena, "chan", 2)
     near = shifted(near, "chan", 1)
     back = shifted(back, "chan", 3)
@@ -539,23 +542,15 @@
         doc_start.reshape(1, rows),
         read_mask,
     )
-    own = pl.pallas_call(
-        far_kernel,
-        out_shape=jax.ShapeDtypeStruct((rows, width), f32),
-        in_specs=whole(3),
-        out_specs=whole(1)[0],
-        compiler_params=room(4),
-        cost_estimate=pl.CostEstimate(flops=0, bytes_accessed=64 << 20, transcendentals=0),
-        name="far_product",
-    )(own, far, far_weight)
     mixed = pl.pallas_call(
         finish_kernel,
         out_shape=jax.ShapeDtypeStruct(stream.shape, bf16),
-        in_specs=whole(3) + [pl.BlockSpec(memory_space=pl.ANY)],
-        out_specs=whole(1)[0],
+        in_specs=whole(5) + [pl.BlockSpec(memory_space=pl.ANY)],
+        out_specs=in_hbm(1)[0],
+        scratch_shapes=[VMEM(stream.shape, bf16), pltpu.SemaphoreType.DMA((4,))],
         compiler_params=room(4),
         name="finish",
-    )(own, near, back, *fixed(attended))
+    )(own, near, back, far, far_weight, *fixed(attended))
     return (mixed, attended)
 
 

time: 47.4 us -> 47.5 us (level)
    pallas_call x3 -> x1, Pallas kernels: 1.16 us -> 0.75 us  [shards(): pl.pallas_call(gate_kernel, out_shape=(jax.ShapeDtypeStruct((rows, channe...]
  transfers between devices with their start and end apart: 11 -> 11, of which waited for: 5 -> 5; matrix products, arithmetic and copies ran while one was open for 6% -> 6% of each run, Pallas kernels for 18% -> 17%
where the time goes in v5:
time: 47.5 us; the launch traced here: 47.2 us
  starting transfers between devices  23.5 us (49%)
  Pallas kernels  10.7 us (23%)
  waiting for transfers between devices  9.62 us (20%)
  other arithmetic  1.9 us (4%)
  local copies, waits for them, and re-layouts  0.75 us (2%)
  between operations  0.73 us (2%)
    all_to_all x1, starting transfers between devices, shards(): lax.all_to_all(jnp.broadcast_to(both, (ctx_count // 2, half, LANES)), 'ct...  10.3 us
    ppermute x6, starting transfers between devices, shifted(): lax.ppermute(value, axis, [(i, (i + steps) % count) for i in range(count)])  8.05 us
    ppermute x6, waiting for transfers between devices, shifted(): lax.ppermute(value, axis, [(i, (i + steps) % count) for i in range(count)])  6.78 us
    pallas_call x1, Pallas kernels, shards(): pl.pallas_call(attention_kernel, out_shape=(jax.ShapeDtypeStruct(attn_que...  5.43 us
    ppermute x4, starting transfers between devices, core_swap(): return lax.ppermute(value, 'ctx', [(i, i ^ 1) for i in range(count)])  5.18 us
    all_to_all x1, waiting for transfers between devices, shards(): lax.all_to_all(jnp.broadcast_to(both, (ctx_count // 2, half, LANES)), 'ct...  1.99 us
    pallas_call x1, Pallas kernels, shards(): pl.pallas_call(local_kernel, out_shape=(jax.ShapeDtypeStruct((rows, chann...  1.96 us
    select_n x1, other arithmetic, shards(): block_1 = core_swap(jnp.where(core == 0, block, block_2))  1.89 us
  transfers between devices with their start and end apart: 11, of which 5 were waited for; matrix products, arithmetic and copies ran while one was open for 6% of the time, Pallas kernels for 17%

profile of v5, /device:TPU:1, one launch (start us, length us, event | category | flops | bytes accessed | tf_op | source)
XLA Modules:
  0.0 47.2 jit_solution(15760136189427166378)
XLA Ops:
  0.6 1.4 %filter_states.1 = (f32[32,128]{1,0:T(8,128)S(1)}, f32[32,128]{1,0:T(8,128)S(1)}, f32[32,128]{1,0:T(8,128)S(1)}, bf16[256,1024]{1,0:T(8,128)(2,1)S(1)}, bf16[256,1024]{1,0:T(8,128)(2,1)S(1)}) custom-call(bf16[128,512]{1,0:T(8,128)(2,1)} %key_hbm.3, bf16[128,512]{1,0:T(8,128)(2,1)} %value_hbm.3, f32[16,512]{1,0:T(8,128)} %bitcast.5, ...), custom_call_target="tpu_custom_call" | custom-call | tf_op jit(solution)/shard_map/filter_states/pallas_call | solution.py:414
  2.1 2.5 %collective-permute-start = (bf16[256,1024]{1,0:T(8,128)(2,1)S(1)}, bf16[256,1024]{1,0:T(8,128)(2,1)}, u32[]{:S(2)}, u32[]{:S(2)}) collective-permute-start(bf16[256,1024]{1,0:T(8,128)(2,1)S(1)} %get-tuple-element.21.block_hbm), channel_id=1, source_target_pairs={{0,8},{4,12},{8,16},{12,20},{16,24},{20,28},{24,32},{28,36},{32,40... | collective-permute-start | bytes 1572872 | tf_op jit(solution)/shard_map/ppermute | solution.py:30
  4.6 1.0 %collective-permute-start.5 = (f32[32,128]{1,0:T(8,128)S(1)}, f32[32,128]{1,0:T(8,128)S(1)}, u32[]{:S(2)}, u32[]{:S(2)}) collective-permute-start(f32[32,128]{1,0:T(8,128)S(1)} %get-tuple-element.23), channel_id=1, source_target_pairs={{0,4},{4,0},{8,12},{12,8},{16,20},{20,16},{24,28},{28,24},{32,36},... | collective-permute-start | bytes 49160 | tf_op jit(solution)/shard_map/ppermute | solution.py:35
  5.6 2.7 %collective-permute-start.3 = (bf16[256,1024]{1,0:T(8,128)(2,1)S(1)}, bf16[256,1024]{1,0:T(8,128)(2,1)}, u32[]{:S(2)}, u32[]{:S(2)}) collective-permute-start(bf16[256,1024]{1,0:T(8,128)(2,1)S(1)} %get-tuple-element.22), channel_id=1, source_target_pairs={{0,2},{1,3},{2,0},{3,1},{4,6},{5,7},{6,4},{7,5},{8,10},{9,11},{10,... | collective-permute-start | bytes 1572872 | tf_op jit(solution)/shard_map/ppermute | solution.py:30
  8.3 0.0 collective-permute-done.5.after_ref.refs_2_
  8.3 0.7 %broadcast_in_dim.3 = bf16[32,32,128]{2,1,0:T(8,128)(2,1)} broadcast(bf16[32,128]{1,0:T(8,128)(2,1)S(1)} %add_convert_fusion), dimensions={1,2} | broadcast | bytes 270336 | tf_op jit(solution)/shard_map/broadcast_in_dim | solution.py:448
  9.1 10.3 %all-to-all-start = ((bf16[32,32,128]{2,1,0:T(8,128)(2,1)}), bf16[32,32,128]{2,1,0:T(8,128)(2,1)S(1)}, u32[]{:S(2)}, u32[]{:S(2)}) async-start(bf16[32,32,128]{2,1,0:T(8,128)(2,1)} %broadcast_in_dim.3), calls=%async_computation | async-start | bytes 524288 | tf_op jit(solution)/shard_map/all_to_all | solution.py:447
  19.4 3.4 %collective-permute-done.two_hbm = bf16[256,1024]{1,0:T(8,128)(2,1)} collective-permute-done((bf16[256,1024]{1,0:T(8,128)(2,1)S(1)}, bf16[256,1024]{1,0:T(8,128)(2,1)}, u32[]{:S(2)}, u32[]{:S(2)}) %collective-permute-start) | collective-permute-done | bytes 524320 | tf_op jit(solution)/shard_map/ppermute | solution.py:30
  22.8 1.9 %broadcast_select_fusion = bf16[256,1024]{1,0:T(8,128)(2,1)} fusion(bf16[256,1024]{1,0:T(8,128)(2,1)S(1)} %get-tuple-element.21.block_hbm, bf16[256,1024]{1,0:T(8,128)(2,1)} %collective-permute-done.two_hbm, pred[]{:T(512)S(6)} %eq.4), kind=kLoop, calls=%fused_computation | loop fusion | flops 262144 | bytes 1572865 | tf_op jit(solution)/shard_map/jit(_where)/select_n | solution.py:439
  24.7 0.2 collective-permute-start.1
  24.9 0.0 collective-permute-start.2
  24.9 0.5 %collective-permute-start.4 = (bf16[256,1024]{1,0:T(8,128)(2,1)}, bf16[256,1024]{1,0:T(8,128)(2,1)}, u32[]{:S(2)}, u32[]{:S(2)}) collective-permute-start(bf16[256,1024]{1,0:T(8,128)(2,1)} %collective-permute-done.3.half_hbm), channel_id=1, source_target_pairs={{0,4},{4,0},{8,12},{12,8},{16,20},{20,16},{24,28},{28,24},{32,36},... | collective-permute-start | bytes 1572872 | tf_op jit(solution)/shard_map/ppermute | solution.py:35
  25.4 2.0 %local_part.1 = (bf16[128,512]{1,0:T(8,128)(2,1)S(1)}, f32[128,512]{1,0:T(8,128)S(1)}, f32[64,128]{1,0:T(8,128)S(1)}, f32[64,128]{1,0:T(8,128)S(1)}, bf16[512,10...) custom-call(f32[32,128]{1,0:T(8,128)S(1)} %collective-permute-done.5.after_ref.refs_2_, bf16[128,512]{1,0:T(8,128)(2,1)} %key_hbm.3, ...), custom_call_target="tpu_custom_call" | custom-call | bytes 8388608 | tf_op jit(solution)/shard_map/local_part/pallas_call | solution.py:456
  27.3 2.0 %all-to-all-done.refs_0_ = bf16[32,32,128]{2,1,0:T(8,128)(2,1)S(1)} async-done(((bf16[32,32,128]{2,1,0:T(8,128)(2,1)}), bf16[32,32,128]{2,1,0:T(8,128)(2,1)S(1)}, u32[]{:S(2)}, u32[]{:S(2)}) %all-to-all-start) | async-done | bytes 262176 | tf_op jit(solution)/shard_map/all_to_all | solution.py:447
  29.3 0.1 carried_states.1
  29.4 3.5 %collective-permute-start.6 = (f32[32,128]{1,0:T(8,128)S(1)}, f32[32,128]{1,0:T(8,128)S(1)}, u32[]{:S(2)}, u32[]{:S(2)}) collective-permute-start(f32[32,128]{1,0:T(8,128)S(1)} %get-tuple-element.31), channel_id=1, source_target_pairs={{0,4},{4,0},{8,12},{12,8},{16,20},{20,16},{24,28},{28,24},{32,36},... | collective-permute-start | bytes 49160 | tf_op jit(solution)/shard_map/ppermute | solution.py:35
  33.0 0.8 %collective-permute-done.6.other_ref = f32[32,128]{1,0:T(8,128)S(1)} collective-permute-done((f32[32,128]{1,0:T(8,128)S(1)}, f32[32,128]{1,0:T(8,128)S(1)}, u32[]{:S(2)}, u32[]{:S(2)}) %collective-permute-start.6) | collective-permute-done | bytes 16416 | tf_op jit(solution)/shard_map/ppermute | solution.py:35
  33.8 0.7 %gate.1 = (bf16[128,512]{1,0:T(8,128)(2,1)S(1)}, bf16[128,1024]{1,0:T(8,128)(2,1)S(1)}, bf16[128,1024]{1,0:T(8,128)(2,1)S(1)}) custom-call(bf16[128,512]{1,0:T(8,128)(2,1)S(1)} %get-tuple-element.24.query_ref, f32[128,512]{1,0:T(8,128)S(1)} %get-tuple-element.25.base_ref, f32[64,128]{1,0:T(8,128)S(1)} %get-tuple-element.26.refs_4_.steps_ref, ...), custom_call_target="tpu_custom_call" | custom-call | tf_op jit(solution)/shard_map/gate/pallas_call | solution.py:506
  34.6 0.4 collective-permute-start.7
  34.9 2.4 %collective-permute-start.8 = (bf16[128,1024]{1,0:T(8,128)(2,1)S(1)}, bf16[128,1024]{1,0:T(8,128)(2,1)S(1)}, u32[]{:S(2)}, u32[]{:S(2)}) collective-permute-start(bf16[128,1024]{1,0:T(8,128)(2,1)S(1)} %get-tuple-element.37), channel_id=1, source_target_pairs={{0,3},{1,0},{2,1},{3,2},{4,7},{5,4},{6,5},{7,6},{8,11},{9,8},{10,9... | collective-permute-start | bytes 786440 | tf_op jit(solution)/shard_map/ppermute | solution.py:30
  37.4 5.4 %attention.1 = (bf16[128,1024]{1,0:T(8,128)(2,1)}, f32[128,1024]{1,0:T(8,128)S(1)}, bf16[512,1024]{1,0:T(8,128)(2,1)S(1)}) custom-call(bf16[128,1024]{1,0:T(8,128)(2,1)} %query_hbm.3, bf16[256,1024]{1,0:T(8,128)(2,1)} %copy-done, bf16[256,1024]{1,0:T(8,128)(2,1)} %collective-permute-done.1.one_hbm, bf16[256,1024]{1,0:T(8,128)(2,1)} %collective-permute-done.two_hbm, ...), custom_call_target="tpu_custom_call" | custom-call | tf_op jit(solution)/shard_map/attention/pallas_call | solution.py:519
  42.8 2.5 %collective-permute-done.9.far_ref = bf16[128,512]{1,0:T(8,128)(2,1)S(1)} collective-permute-done((bf16[128,512]{1,0:T(8,128)(2,1)S(1)}, bf16[128,512]{1,0:T(8,128)(2,1)S(1)}, u32[]{:S(2)}, u32[]{:S(2)}) %collective-permute-start.9) | collective-permute-done | bytes 131104 | tf_op jit(solution)/shard_map/ppermute | solution.py:30
  45.3 0.9 %collective-permute-done.7.near_ref = bf16[128,1024]{1,0:T(8,128)(2,1)S(1)} collective-permute-done((bf16[128,1024]{1,0:T(8,128)(2,1)S(1)}, bf16[128,1024]{1,0:T(8,128)(2,1)S(1)}, u32[]{:S(2)}, u32[]{:S(2)}) %collective-permute-start.7) | collective-permute-done | bytes 262176 | tf_op jit(solution)/shard_map/ppermute | solution.py:30
  46.2 1.0 %finish.1 = bf16[128,1024]{1,0:T(8,128)(2,1)} custom-call(f32[128,1024]{1,0:T(8,128)S(1)} %get-tuple-element.35.own_ref, bf16[128,1024]{1,0:T(8,128)(2,1)S(1)} %collective-permute-done.7.near_ref, bf16[128,1024]{1,0:T(8,128)(2,1)S(1)} %collective-permute-done.8.back_ref, bf16[128,512]{1,0:T(8,128)(2,1)S(1)} %collective-permute-done.9.far_ref, ...), custom_call_target="tpu_custom_call" | custom-call | tf_op jit(solution)/shard_map/finish/pallas_call | solution.py:545
  (13 shorter events, 0.0 us)
Async XLA Ops:
  2.1 32.5 %copy-start = (bf16[256,1024]{1,0:T(8,128)(2,1)}, bf16[256,1024]{1,0:T(8,128)(2,1)S(1)}, u32[]{:S(2)}) copy-start(bf16[256,1024]{1,0:T(8,128)(2,1)S(1)} %get-tuple-element.21.block_hbm) | copy-start | bytes 1572868
  2.1 20.7 %collective-permute-start = (bf16[256,1024]{1,0:T(8,128)(2,1)S(1)}, bf16[256,1024]{1,0:T(8,128)(2,1)}, u32[]{:S(2)}, u32[]{:S(2)}) collective-permute-start(bf16[256,1024]{1,0:T(8,128)(2,1)S(1)} %get-tuple-element.21.block_hbm), channel_id=1, source_target_pairs={{0,8},{4,12},{8,16},{12,20},{16,24},{20,28},{24,32},{28,36},{32,40... | collective-permute-start | bytes 1572872 | tf_op jit(solution)/shard_map/ppermute | solution.py:30
  4.6 3.7 %collective-permute-start.5 = (f32[32,128]{1,0:T(8,128)S(1)}, f32[32,128]{1,0:T(8,128)S(1)}, u32[]{:S(2)}, u32[]{:S(2)}) collective-permute-start(f32[32,128]{1,0:T(8,128)S(1)} %get-tuple-element.23), channel_id=1, source_target_pairs={{0,4},{4,0},{8,12},{12,8},{16,20},{20,16},{24,28},{28,24},{32,36},... | collective-permute-start | bytes 49160 | tf_op jit(solution)/shard_map/ppermute | solution.py:35
  5.6 19.3 %collective-permute-start.3 = (bf16[256,1024]{1,0:T(8,128)(2,1)S(1)}, bf16[256,1024]{1,0:T(8,128)(2,1)}, u32[]{:S(2)}, u32[]{:S(2)}) collective-permute-start(bf16[256,1024]{1,0:T(8,128)(2,1)S(1)} %get-tuple-element.22), channel_id=1, source_target_pairs={{0,2},{1,3},{2,0},{3,1},{4,6},{5,7},{6,4},{7,5},{8,10},{9,11},{10,... | collective-permute-start | bytes 1572872 | tf_op jit(solution)/shard_map/ppermute | solution.py:30
  9.1 20.3 %all-to-all-start = ((bf16[32,32,128]{2,1,0:T(8,128)(2,1)}), bf16[32,32,128]{2,1,0:T(8,128)(2,1)S(1)}, u32[]{:S(2)}, u32[]{:S(2)}) async-start(bf16[32,32,128]{2,1,0:T(8,128)(2,1)} %broadcast_in_dim.3), calls=%async_computation | async-start | bytes 524288 | tf_op jit(solution)/shard_map/all_to_all | solution.py:447
  24.7 12.7 %copy-start.1 = (s32[128]{0:T(128)S(1)}, s32[128]{0:T(128)}, u32[]{:S(2)}) copy-start(s32[128]{0:T(128)} %param.24) | copy-start | bytes 1540
  24.7 12.7 %copy-start.2 = (s32[1,4]{1,0:T(1,128)S(1)}, s32[1,4]{1,0:T(1,128)}, u32[]{:S(2)}) copy-start(s32[1,4]{1,0:T(1,128)} %read_ref.1) | copy-start | bytes 52
  24.7 12.7 %collective-permute-start.1 = (bf16[256,1024]{1,0:T(8,128)(2,1)}, bf16[256,1024]{1,0:T(8,128)(2,1)}, u32[]{:S(2)}, u32[]{:S(2)}) collective-permute-start(bf16[256,1024]{1,0:T(8,128)(2,1)} %broadcast_select_fusion), channel_id=1, source_target_pairs={{0,4},{4,0},{8,12},{12,8},{16,20},{20,16},{24,28},{28,24},{32,36},... | collective-permute-start | bytes 1572872 | tf_op jit(solution)/shard_map/ppermute | solution.py:35
  24.9 12.5 %collective-permute-start.2 = (bf16[256,1024]{1,0:T(8,128)(2,1)}, bf16[256,1024]{1,0:T(8,128)(2,1)}, u32[]{:S(2)}, u32[]{:S(2)}) collective-permute-start(bf16[256,1024]{1,0:T(8,128)(2,1)} %collective-permute-done.two_hbm), channel_id=1, source_target_pairs={{0,4},{4,8},{8,12},{12,16},{16,20},{20,24},{24,28},{28,32},{32,36}... | collective-permute-start | bytes 1572872 | tf_op jit(solution)/shard_map/ppermute | solution.py:30
  24.9 12.5 %collective-permute-start.4 = (bf16[256,1024]{1,0:T(8,128)(2,1)}, bf16[256,1024]{1,0:T(8,128)(2,1)}, u32[]{:S(2)}, u32[]{:S(2)}) collective-permute-start(bf16[256,1024]{1,0:T(8,128)(2,1)} %collective-permute-done.3.half_hbm), channel_id=1, source_target_pairs={{0,4},{4,0},{8,12},{12,8},{16,20},{20,16},{24,28},{28,24},{32,36},... | collective-permute-start | bytes 1572872 | tf_op jit(solution)/shard_map/ppermute | solution.py:35
  29.4 4.3 %collective-permute-start.6 = (f32[32,128]{1,0:T(8,128)S(1)}, f32[32,128]{1,0:T(8,128)S(1)}, u32[]{:S(2)}, u32[]{:S(2)}) collective-permute-start(f32[32,128]{1,0:T(8,128)S(1)} %get-tuple-element.31), channel_id=1, source_target_pairs={{0,4},{4,0},{8,12},{12,8},{16,20},{20,16},{24,28},{28,24},{32,36},... | collective-permute-start | bytes 49160 | tf_op jit(solution)/shard_map/ppermute | solution.py:35
  34.6 11.6 %collective-permute-start.7 = (bf16[128,1024]{1,0:T(8,128)(2,1)S(1)}, bf16[128,1024]{1,0:T(8,128)(2,1)S(1)}, u32[]{:S(2)}, u32[]{:S(2)}) collective-permute-start(bf16[128,1024]{1,0:T(8,128)(2,1)S(1)} %get-tuple-element.36), channel_id=1, source_target_pairs={{0,1},{1,2},{2,3},{3,0},{4,5},{5,6},{6,7},{7,4},{8,9},{9,10},{10,1... | collective-permute-start | bytes 786440 | tf_op jit(solution)/shard_map/ppermute | solution.py:30
  34.9 11.3 %collective-permute-start.8 = (bf16[128,1024]{1,0:T(8,128)(2,1)S(1)}, bf16[128,1024]{1,0:T(8,128)(2,1)S(1)}, u32[]{:S(2)}, u32[]{:S(2)}) collective-permute-start(bf16[128,1024]{1,0:T(8,128)(2,1)S(1)} %get-tuple-element.37), channel_id=1, source_target_pairs={{0,3},{1,0},{2,1},{3,2},{4,7},{5,4},{6,5},{7,6},{8,11},{9,8},{10,9... | collective-permute-start | bytes 786440 | tf_op jit(solution)/shard_map/ppermute | solution.py:30
  37.3 8.0 %collective-permute-start.9 = (bf16[128,512]{1,0:T(8,128)(2,1)S(1)}, bf16[128,512]{1,0:T(8,128)(2,1)S(1)}, u32[]{:S(2)}, u32[]{:S(2)}) collective-permute-start(bf16[128,512]{1,0:T(8,128)(2,1)S(1)} %get-tuple-element.34.hyena_ref), channel_id=1, source_target_pairs={{0,2},{1,3},{2,0},{3,1},{4,6},{5,7},{6,4},{7,5},{8,10},{9,11},{10,... | collective-permute-start | bytes 393224 | tf_op jit(solution)/shard_map/ppermute | solution.py:30

commit v6 on v5

--- a/solution.py
+++ b/solution.py
@@ -127,7 +127,8 @@
         state_ref[8 * i : 8 * i + 8, :] = total
     half = keep_ref.shape[0]
     keep_ref[...] = half_rows(state_ref, core, half)
-    send_ref[...] = half_rows(state_ref, 1 - core, half)
+    for i in range(send_ref.shape[0]):
+        send_ref[i] = half_rows(state_ref, 1 - core, half)
     rates_ref[...] = half_rows(all_rates_ref, core, half)
     for copy in copies[3:]:
         copy.wait()
@@ -415,7 +416,7 @@
         states_kernel,
         out_shape=(
             state_half,
-            state_half,
+            jax.ShapeDtypeStruct((20, half, LANES), f32),
             state_half,
             jax.ShapeDtypeStruct((2 * rows, attn_key.shape[1]), bf16),
             jax.ShapeDtypeStruct((channels // 2, width), bf16),
@@ -439,7 +440,7 @@
     block_1 = core_swap(jnp.where(core == 0, block, block_2))
     far_half = shifted(far_half, "chan", 2)
     far_other = core_swap(far_half)
-    got = core_swap(send)
+    got = core_swap(send)[0]
     first = jnp.where(core == 0, keep, got)
     second = jnp.where(core == 0, got, keep)
     both = (first * jnp.exp(-rows * rates) + second).astype(bf16)

time: 47.5 us -> 47.4 us (level)
  waiting for transfers between devices: 9.62 us -> 8.97 us
    ppermute x4, starting transfers between devices: 5.18 us -> 7.91 us  [core_swap(): return lax.ppermute(value, 'ctx', [(i, i ^ 1) for i in range(count)])]
    ppermute x6, starting transfers between devices: 8.05 us -> 5.53 us  [shifted(): lax.ppermute(value, axis, [(i, (i + steps) % count) for i in range(count)])]
    all_to_all x1, waiting for transfers between devices: 1.99 us -> 0.34 us  [shards(): lax.all_to_all(jnp.broadcast_to(both, (ctx_count // 2, half, LANES)), 'ct...]
    ppermute x6, waiting for transfers between devices: 6.78 us -> 7.78 us  [shifted(): lax.ppermute(value, axis, [(i, (i + steps) % count) for i in range(count)])]
  transfers between devices with their start and end apart: 11 -> 11, of which waited for: 5 -> 4; matrix products, arithmetic and copies ran while one was open for 6% -> 6% of each run, Pallas kernels for 17% -> 18%
where the time goes in v6:
time: 47.4 us; the launch traced here: 46.8 us
  starting transfers between devices  23.8 us (50%)
  Pallas kernels  10.7 us (23%)
  waiting for transfers between devices  8.97 us (19%)
  other arithmetic  1.9 us (4%)
  local copies, waits for them, and re-layouts  0.75 us (2%)
  between operations  0.74 us (2%)
    all_to_all x1, starting transfers between devices, shards(): lax.all_to_all(jnp.broadcast_to(both, (ctx_count // 2, half, LANES)), 'ct...  10.3 us
    ppermute x4, starting transfers between devices, core_swap(): return lax.ppermute(value, 'ctx', [(i, i ^ 1) for i in range(count)])  7.91 us
    ppermute x6, waiting for transfers between devices, shifted(): lax.ppermute(value, axis, [(i, (i + steps) % count) for i in range(count)])  7.78 us
    ppermute x6, starting transfers between devices, shifted(): lax.ppermute(value, axis, [(i, (i + steps) % count) for i in range(count)])  5.53 us
    pallas_call x1, Pallas kernels, shards(): pl.pallas_call(attention_kernel, out_shape=(jax.ShapeDtypeStruct(attn_que...  5.44 us
    pallas_call x1, Pallas kernels, shards(): pl.pallas_call(local_kernel, out_shape=(jax.ShapeDtypeStruct((rows, chann...  1.96 us
    select_n x1, other arithmetic, shards(): block_1 = core_swap(jnp.where(core == 0, block, block_2))  1.89 us
    pallas_call x1, Pallas kernels, shards(): pl.pallas_call(states_kernel, out_shape=(state_half, jax.ShapeDtypeStruct...  1.46 us
  transfers between devices with their start and end apart: 11, of which 4 were waited for; matrix products, arithmetic and copies ran while one was open for 6% of the time, Pallas kernels for 18%

profile of v6, /device:TPU:1, one launch (start us, length us, event | category | flops | bytes accessed | tf_op | source)
XLA Modules:
  0.0 46.8 jit_solution(12419382334292446699)
XLA Ops:
  0.6 1.5 %filter_states.1 = (f32[32,128]{1,0:T(8,128)S(1)}, f32[20,32,128]{2,1,0:T(8,128)S(1)}, f32[32,128]{1,0:T(8,128)S(1)}, bf16[256,1024]{1,0:T(8,128)(2,1)S(1)}, bf16[256,1024]{1,0:T(8,128)(2,1)S(1)}) custom-call(bf16[128,512]{1,0:T(8,128)(2,1)} %key_hbm.3, bf16[128,512]{1,0:T(8,128)(2,1)} %value_hbm.3, f32[16,512]{1,0:T(8,128)} %bitcast.9, ...), custom_call_target="tpu_custom_call" | custom-call | tf_op jit(solution)/shard_map/filter_states/pallas_call | solution.py:415
  2.1 3.3 %collective-permute-start.5 = (f32[20,32,128]{2,1,0:T(8,128)S(1)}, f32[20,32,128]{2,1,0:T(8,128)S(1)}, u32[]{:S(2)}, u32[]{:S(2)}) collective-permute-start(f32[20,32,128]{2,1,0:T(8,128)S(1)} %get-tuple-element.23), channel_id=1, source_target_pairs={{0,4},{4,0},{8,12},{12,8},{16,20},{20,16},{24,28},{28,24},{32,36},... | collective-permute-start | bytes 983048 | tf_op jit(solution)/shard_map/ppermute | solution.py:35
  5.4 0.0 collective-permute-start
  5.4 2.7 %collective-permute-start.3 = (bf16[256,1024]{1,0:T(8,128)(2,1)S(1)}, bf16[256,1024]{1,0:T(8,128)(2,1)}, u32[]{:S(2)}, u32[]{:S(2)}) collective-permute-start(bf16[256,1024]{1,0:T(8,128)(2,1)S(1)} %get-tuple-element.22), channel_id=1, source_target_pairs={{0,2},{1,3},{2,0},{3,1},{4,6},{5,7},{6,4},{7,5},{8,10},{9,11},{10,... | collective-permute-start | bytes 1572872 | tf_op jit(solution)/shard_map/ppermute | solution.py:30
  8.1 0.0 collective-permute-done.5
  8.1 0.7 %broadcast_in_dim.3 = bf16[32,32,128]{2,1,0:T(8,128)(2,1)} broadcast(bf16[32,128]{1,0:T(8,128)(2,1)S(1)} %add_convert_fusion), dimensions={1,2} | broadcast | bytes 270336 | tf_op jit(solution)/shard_map/broadcast_in_dim | solution.py:449
  8.9 10.3 %all-to-all-start = ((bf16[32,32,128]{2,1,0:T(8,128)(2,1)}), bf16[32,32,128]{2,1,0:T(8,128)(2,1)S(1)}, u32[]{:S(2)}, u32[]{:S(2)}) async-start(bf16[32,32,128]{2,1,0:T(8,128)(2,1)} %broadcast_in_dim.3), calls=%async_computation | async-start | bytes 524288 | tf_op jit(solution)/shard_map/all_to_all | solution.py:448
  19.2 4.9 %collective-permute-done.two_hbm = bf16[256,1024]{1,0:T(8,128)(2,1)} collective-permute-done((bf16[256,1024]{1,0:T(8,128)(2,1)S(1)}, bf16[256,1024]{1,0:T(8,128)(2,1)}, u32[]{:S(2)}, u32[]{:S(2)}) %collective-permute-start) | collective-permute-done | bytes 524320 | tf_op jit(solution)/shard_map/ppermute | solution.py:30
  24.0 1.9 %broadcast_select_fusion = bf16[256,1024]{1,0:T(8,128)(2,1)} fusion(bf16[256,1024]{1,0:T(8,128)(2,1)S(1)} %get-tuple-element.21.block_hbm, bf16[256,1024]{1,0:T(8,128)(2,1)} %collective-permute-done.two_hbm, pred[]{:T(512)S(6)} %eq.4), kind=kLoop, calls=%fused_computation | loop fusion | flops 262144 | bytes 1572865 | tf_op jit(solution)/shard_map/jit(_where)/select_n | solution.py:440
  25.9 0.1 collective-permute-start.2
  26.0 0.0 collective-permute-done.3.half_hbm
  26.0 0.5 %collective-permute-start.4 = (bf16[256,1024]{1,0:T(8,128)(2,1)}, bf16[256,1024]{1,0:T(8,128)(2,1)}, u32[]{:S(2)}, u32[]{:S(2)}) collective-permute-start(bf16[256,1024]{1,0:T(8,128)(2,1)} %collective-permute-done.3.half_hbm), channel_id=1, source_target_pairs={{0,4},{4,0},{8,12},{12,8},{16,20},{20,16},{24,28},{28,24},{32,36},... | collective-permute-start | bytes 1572872 | tf_op jit(solution)/shard_map/ppermute | solution.py:35
  26.5 2.0 %local_part.1 = (bf16[128,512]{1,0:T(8,128)(2,1)S(1)}, f32[128,512]{1,0:T(8,128)S(1)}, f32[64,128]{1,0:T(8,128)S(1)}, f32[64,128]{1,0:T(8,128)S(1)}, bf16[512,10...) custom-call(f32[32,128]{1,0:T(8,128)S(1)} %slice_bitcast_fusion.after_ref.refs_2_, bf16[128,512]{1,0:T(8,128)(2,1)} %key_hbm.3, ...), custom_call_target="tpu_custom_call" | custom-call | bytes 8388608 | tf_op jit(solution)/shard_map/local_part/pallas_call | solution.py:457
  28.5 0.3 all-to-all-done.refs_0_
  28.8 0.1 carried_states.1
  28.9 4.1 %collective-permute-start.6 = (f32[32,128]{1,0:T(8,128)S(1)}, f32[32,128]{1,0:T(8,128)S(1)}, u32[]{:S(2)}, u32[]{:S(2)}) collective-permute-start(f32[32,128]{1,0:T(8,128)S(1)} %get-tuple-element.31), channel_id=1, source_target_pairs={{0,4},{4,0},{8,12},{12,8},{16,20},{20,16},{24,28},{28,24},{32,36},... | collective-permute-start | bytes 49160 | tf_op jit(solution)/shard_map/ppermute | solution.py:35
  33.0 0.8 %collective-permute-done.6.other_ref = f32[32,128]{1,0:T(8,128)S(1)} collective-permute-done((f32[32,128]{1,0:T(8,128)S(1)}, f32[32,128]{1,0:T(8,128)S(1)}, u32[]{:S(2)}, u32[]{:S(2)}) %collective-permute-start.6) | collective-permute-done | bytes 16416 | tf_op jit(solution)/shard_map/ppermute | solution.py:35
  33.9 0.7 %gate.1 = (bf16[128,512]{1,0:T(8,128)(2,1)S(1)}, bf16[128,1024]{1,0:T(8,128)(2,1)S(1)}, bf16[128,1024]{1,0:T(8,128)(2,1)S(1)}) custom-call(bf16[128,512]{1,0:T(8,128)(2,1)S(1)} %get-tuple-element.24.query_ref, f32[128,512]{1,0:T(8,128)S(1)} %get-tuple-element.25.base_ref, f32[64,128]{1,0:T(8,128)S(1)} %get-tuple-element.26.refs_4_.steps_ref, ...), custom_call_target="tpu_custom_call" | custom-call | tf_op jit(solution)/shard_map/gate/pallas_call | solution.py:507
  34.6 0.1 collective-permute-start.7
  34.7 2.7 %collective-permute-start.8 = (bf16[128,1024]{1,0:T(8,128)(2,1)S(1)}, bf16[128,1024]{1,0:T(8,128)(2,1)S(1)}, u32[]{:S(2)}, u32[]{:S(2)}) collective-permute-start(bf16[128,1024]{1,0:T(8,128)(2,1)S(1)} %get-tuple-element.37), channel_id=1, source_target_pairs={{0,3},{1,0},{2,1},{3,2},{4,7},{5,4},{6,5},{7,6},{8,11},{9,8},{10,9... | collective-permute-start | bytes 786440 | tf_op jit(solution)/shard_map/ppermute | solution.py:30
  37.4 0.0 collective-permute-start.9
  37.5 5.4 %attention.1 = (bf16[128,1024]{1,0:T(8,128)(2,1)}, f32[128,1024]{1,0:T(8,128)S(1)}, bf16[512,1024]{1,0:T(8,128)(2,1)S(1)}) custom-call(bf16[128,1024]{1,0:T(8,128)(2,1)} %query_hbm.3, bf16[256,1024]{1,0:T(8,128)(2,1)} %copy-done, bf16[256,1024]{1,0:T(8,128)(2,1)} %collective-permute-done.1.one_hbm, bf16[256,1024]{1,0:T(8,128)(2,1)} %collective-permute-done.two_hbm, ...), custom_call_target="tpu_custom_call" | custom-call | tf_op jit(solution)/shard_map/attention/pallas_call | solution.py:520
  42.9 2.9 %collective-permute-done.9.far_ref = bf16[128,512]{1,0:T(8,128)(2,1)S(1)} collective-permute-done((bf16[128,512]{1,0:T(8,128)(2,1)S(1)}, bf16[128,512]{1,0:T(8,128)(2,1)S(1)}, u32[]{:S(2)}, u32[]{:S(2)}) %collective-permute-start.9) | collective-permute-done | bytes 131104 | tf_op jit(solution)/shard_map/ppermute | solution.py:30
  45.8 1.0 %finish.1 = bf16[128,1024]{1,0:T(8,128)(2,1)} custom-call(f32[128,1024]{1,0:T(8,128)S(1)} %get-tuple-element.35.own_ref, bf16[128,1024]{1,0:T(8,128)(2,1)S(1)} %collective-permute-done.7.near_ref, bf16[128,1024]{1,0:T(8,128)(2,1)S(1)} %collective-permute-done.8.back_ref, bf16[128,512]{1,0:T(8,128)(2,1)S(1)} %collective-permute-done.9.far_ref, ...), custom_call_target="tpu_custom_call" | custom-call | tf_op jit(solution)/shard_map/finish/pallas_call | solution.py:546
  (14 shorter events, 0.0 us)
Async XLA Ops:
  2.1 32.5 %copy-start = (bf16[256,1024]{1,0:T(8,128)(2,1)}, bf16[256,1024]{1,0:T(8,128)(2,1)S(1)}, u32[]{:S(2)}) copy-start(bf16[256,1024]{1,0:T(8,128)(2,1)S(1)} %get-tuple-element.21.block_hbm) | copy-start | bytes 1572868
  2.1 6.0 %collective-permute-start.5 = (f32[20,32,128]{2,1,0:T(8,128)S(1)}, f32[20,32,128]{2,1,0:T(8,128)S(1)}, u32[]{:S(2)}, u32[]{:S(2)}) collective-permute-start(f32[20,32,128]{2,1,0:T(8,128)S(1)} %get-tuple-element.23), channel_id=1, source_target_pairs={{0,4},{4,0},{8,12},{12,8},{16,20},{20,16},{24,28},{28,24},{32,36},... | collective-permute-start | bytes 983048 | tf_op jit(solution)/shard_map/ppermute | solution.py:35
  5.4 18.6 %collective-permute-start = (bf16[256,1024]{1,0:T(8,128)(2,1)S(1)}, bf16[256,1024]{1,0:T(8,128)(2,1)}, u32[]{:S(2)}, u32[]{:S(2)}) collective-permute-start(bf16[256,1024]{1,0:T(8,128)(2,1)S(1)} %get-tuple-element.21.block_hbm), channel_id=1, source_target_pairs={{0,8},{4,12},{8,16},{12,20},{16,24},{20,28},{24,32},{28,36},{32,40... | collective-permute-start | bytes 1572872 | tf_op jit(solution)/shard_map/ppermute | solution.py:30
  5.4 20.6 %collective-permute-start.3 = (bf16[256,1024]{1,0:T(8,128)(2,1)S(1)}, bf16[256,1024]{1,0:T(8,128)(2,1)}, u32[]{:S(2)}, u32[]{:S(2)}) collective-permute-start(bf16[256,1024]{1,0:T(8,128)(2,1)S(1)} %get-tuple-element.22), channel_id=1, source_target_pairs={{0,2},{1,3},{2,0},{3,1},{4,6},{5,7},{6,4},{7,5},{8,10},{9,11},{10,... | collective-permute-start | bytes 1572872 | tf_op jit(solution)/shard_map/ppermute | solution.py:30
  8.9 20.0 %all-to-all-start = ((bf16[32,32,128]{2,1,0:T(8,128)(2,1)}), bf16[32,32,128]{2,1,0:T(8,128)(2,1)S(1)}, u32[]{:S(2)}, u32[]{:S(2)}) async-start(bf16[32,32,128]{2,1,0:T(8,128)(2,1)} %broadcast_in_dim.3), calls=%async_computation | async-start | bytes 524288 | tf_op jit(solution)/shard_map/all_to_all | solution.py:448
  25.9 11.5 %copy-start.1 = (s32[128]{0:T(128)S(1)}, s32[128]{0:T(128)}, u32[]{:S(2)}) copy-start(s32[128]{0:T(128)} %param.24) | copy-start | bytes 1540
  25.9 11.5 %copy-start.2 = (s32[1,4]{1,0:T(1,128)S(1)}, s32[1,4]{1,0:T(1,128)}, u32[]{:S(2)}) copy-start(s32[1,4]{1,0:T(1,128)} %read_ref.1) | copy-start | bytes 52
  25.9 11.5 %collective-permute-start.1 = (bf16[256,1024]{1,0:T(8,128)(2,1)}, bf16[256,1024]{1,0:T(8,128)(2,1)}, u32[]{:S(2)}, u32[]{:S(2)}) collective-permute-start(bf16[256,1024]{1,0:T(8,128)(2,1)} %broadcast_select_fusion), channel_id=1, source_target_pairs={{0,4},{4,0},{8,12},{12,8},{16,20},{20,16},{24,28},{28,24},{32,36},... | collective-permute-start | bytes 1572872 | tf_op jit(solution)/shard_map/ppermute | solution.py:35
  25.9 11.5 %collective-permute-start.2 = (bf16[256,1024]{1,0:T(8,128)(2,1)}, bf16[256,1024]{1,0:T(8,128)(2,1)}, u32[]{:S(2)}, u32[]{:S(2)}) collective-permute-start(bf16[256,1024]{1,0:T(8,128)(2,1)} %collective-permute-done.two_hbm), channel_id=1, source_target_pairs={{0,4},{4,8},{8,12},{12,16},{16,20},{20,24},{24,28},{28,32},{32,36}... | collective-permute-start | bytes 1572872 | tf_op jit(solution)/shard_map/ppermute | solution.py:30
  26.0 11.4 %collective-permute-start.4 = (bf16[256,1024]{1,0:T(8,128)(2,1)}, bf16[256,1024]{1,0:T(8,128)(2,1)}, u32[]{:S(2)}, u32[]{:S(2)}) collective-permute-start(bf16[256,1024]{1,0:T(8,128)(2,1)} %collective-permute-done.3.half_hbm), channel_id=1, source_target_pairs={{0,4},{4,0},{8,12},{12,8},{16,20},{20,16},{24,28},{28,24},{32,36},... | collective-permute-start | bytes 1572872 | tf_op jit(solution)/shard_map/ppermute | solution.py:35
  28.9 4.9 %collective-permute-start.6 = (f32[32,128]{1,0:T(8,128)S(1)}, f32[32,128]{1,0:T(8,128)S(1)}, u32[]{:S(2)}, u32[]{:S(2)}) collective-permute-start(f32[32,128]{1,0:T(8,128)S(1)} %get-tuple-element.31), channel_id=1, source_target_pairs={{0,4},{4,0},{8,12},{12,8},{16,20},{20,16},{24,28},{28,24},{32,36},... | collective-permute-start | bytes 49160 | tf_op jit(solution)/shard_map/ppermute | solution.py:35
  34.6 11.2 %collective-permute-start.7 = (bf16[128,1024]{1,0:T(8,128)(2,1)S(1)}, bf16[128,1024]{1,0:T(8,128)(2,1)S(1)}, u32[]{:S(2)}, u32[]{:S(2)}) collective-permute-start(bf16[128,1024]{1,0:T(8,128)(2,1)S(1)} %get-tuple-element.36), channel_id=1, source_target_pairs={{0,1},{1,2},{2,3},{3,0},{4,5},{5,6},{6,7},{7,4},{8,9},{9,10},{10,1... | collective-permute-start | bytes 786440 | tf_op jit(solution)/shard_map/ppermute | solution.py:30
  34.7 11.1 %collective-permute-start.8 = (bf16[128,1024]{1,0:T(8,128)(2,1)S(1)}, bf16[128,1024]{1,0:T(8,128)(2,1)S(1)}, u32[]{:S(2)}, u32[]{:S(2)}) collective-permute-start(bf16[128,1024]{1,0:T(8,128)(2,1)S(1)} %get-tuple-element.37), channel_id=1, source_target_pairs={{0,3},{1,0},{2,1},{3,2},{4,7},{5,4},{6,5},{7,6},{8,11},{9,8},{10,9... | collective-permute-start | bytes 786440 | tf_op jit(solution)/shard_map/ppermute | solution.py:30
  37.4 8.4 %collective-permute-start.9 = (bf16[128,512]{1,0:T(8,128)(2,1)S(1)}, bf16[128,512]{1,0:T(8,128)(2,1)S(1)}, u32[]{:S(2)}, u32[]{:S(2)}) collective-permute-start(bf16[128,512]{1,0:T(8,128)(2,1)S(1)} %get-tuple-element.34.hyena_ref), channel_id=1, source_target_pairs={{0,2},{1,3},{2,0},{3,1},{4,6},{5,7},{6,4},{7,5},{8,10},{9,11},{10,... | collective-permute-start | bytes 393224 | tf_op jit(solution)/shard_map/ppermute | solution.py:30
